TPU v7x, 32 devices: a whole 2x2x4 slice. The times are simulated.
32 devices in a mesh: groups: 1, gx: 32 (over z, y, x, core).
Axes of the slice: x: 2, y: 2, z: 4, core: 2. Of those that a mesh axis runs over, the one named last changes fastest.
Arguments:
- hidden_field: bfloat16 [128, 32, 64, 512], P(('groups', 'gx')), may hold values from -6 to 6
- cotangent: bfloat16 [128, 32, 64, 512], P(('groups', 'gx')), may hold values from -6 to 6
- spectral_weight: bfloat16 [1024, 2, 32, 512], P('gx'), may hold values from -6 to 6
- local_weight: bfloat16 [32, 32], replicated, may hold values from -1 to 1
- local_bias: float32 [32], replicated, may hold values from -3 to 3
Outputs:
- output: bfloat16 [128, 32, 64, 512], P(('groups', 'gx'))
- grad_field: bfloat16 [128, 32, 64, 512], P(('groups', 'gx'))
- grad_spectral: float32 [1024, 2, 32, 512], P('gx', 'groups')
- grad_local: float32 [32, 32], P('groups')
- grad_bias: float32 [32], P('groups')
All inputs are finite; a program needn't handle non-finite values.
Results may differ from a plain program's by a relative error of at most 0.0058.
Values sent between devices are 32-bit elements; how exact they have to be, the bound alone decides.
No kernel may reach another device: no remote copies, remote signals or barrier semaphores. Data moves between devices by JAX's collectives and lax.ppermute only.
A program may use at most 192 MiB of HBM per device.

v0:
```python
import math

import jax
import jax.numpy as jnp
from jax import lax
from jax.sharding import PartitionSpec as P

NX = 128
NY = 64
NZ = 64
NT = 8
KX = 16
KY = 16
KZ = 16
KT = 4


HIGHEST = lax.Precision.HIGHEST


def kept_frequency(kept):
    serial = jnp.arange(kept, dtype=jnp.int32)
    return jnp.where(serial < kept // 2, serial, serial - kept)


def axis_tables(positions, length, kept):
    wound = positions[:, None] * kept_frequency(kept)[None, :] % length
    angles = 2.0 * math.pi / length * wound.astype(jnp.float32)
    return (jnp.cos(angles), jnp.sin(angles))


def joint_table():
    cells = jnp.arange(NZ * NT, dtype=jnp.int32)
    depth = cells // NT
    moment = cells % NT
    kept_z = jnp.repeat(kept_frequency(KZ), KT)
    kept_t = jnp.tile(jnp.arange(KT, dtype=jnp.int32), KZ)
    wound = depth[:, None] * kept_z[None, :] % NZ * NT + moment[:, None] * kept_t[None, :] % NT * NZ
    angles = 2.0 * math.pi / (NZ * NT) * (wound % (NZ * NT)).astype(jnp.float32)
    return jnp.concatenate([jnp.cos(angles), -jnp.sin(angles)], axis=1).astype(jnp.bfloat16)


def forward_planes(values, joint, y_cosine, y_sine):
    mixed_zt = jnp.einsum("xcyp,pq->xcyq", values, joint, preferred_element_type=jnp.float32)
    half = mixed_zt.shape[-1] // 2
    real_part = mixed_zt[..., :half]
    imag_part = mixed_zt[..., half:]
    out_real = jnp.einsum("xcym,yk->xckm", real_part, y_cosine, precision=HIGHEST) + jnp.einsum(
        "xcym,yk->xckm", imag_part, y_sine, precision=HIGHEST
    )
    out_imag = jnp.einsum("xcym,yk->xckm", imag_part, y_cosine, precision=HIGHEST) - jnp.einsum(
        "xcym,yk->xckm", real_part, y_sine, precision=HIGHEST
    )
    stacked = jnp.stack([out_real, out_imag], axis=1)
    return stacked.reshape(
        stacked.shape[0], 2, stacked.shape[2], stacked.shape[3] * stacked.shape[4]
    )


def inverse_planes(spectra, joint, y_cosine, y_sine):
    kept_y = y_cosine.shape[1]
    parts = spectra.reshape(
        spectra.shape[0], 2, spectra.shape[2], kept_y, spectra.shape[3] // kept_y
    )
    real_part = parts[:, 0]
    imag_part = parts[:, 1]
    out_real = jnp.einsum("xckm,yk->xcym", real_part, y_cosine, precision=HIGHEST) - jnp.einsum(
        "xckm,yk->xcym", imag_part, y_sine, precision=HIGHEST
    )
    out_imag = jnp.einsum("xckm,yk->xcym", real_part, y_sine, precision=HIGHEST) + jnp.einsum(
        "xckm,yk->xcym", imag_part, y_cosine, precision=HIGHEST
    )
    joined = jnp.concatenate([out_real, out_imag], axis=-1).astype(jnp.bfloat16)
    return jnp.einsum("xcyq,pq->xcyp", joined, joint, preferred_element_type=jnp.float32)


def to_modes(spectra, x_cosine, x_sine):
    real_part = spectra[:, 0]
    imag_part = spectra[:, 1]
    out_real = jnp.einsum("xcm,xk->mck", real_part, x_cosine, precision=HIGHEST) + jnp.einsum(
        "xcm,xk->mck", imag_part, x_sine, precision=HIGHEST
    )
    out_imag = jnp.einsum("xcm,xk->mck", imag_part, x_cosine, precision=HIGHEST) - jnp.einsum(
        "xcm,xk->mck", real_part, x_sine, precision=HIGHEST
    )
    return jnp.stack([out_real, out_imag], axis=1)


def to_planes(mixed, x_cosine, x_sine):
    real_part = mixed[:, 0]
    imag_part = mixed[:, 1]
    out_real = jnp.einsum("mck,xk->xcm", real_part, x_cosine, precision=HIGHEST) - jnp.einsum(
        "mck,xk->xcm", imag_part, x_sine, precision=HIGHEST
    )
    out_imag = jnp.einsum("mck,xk->xcm", real_part, x_sine, precision=HIGHEST) + jnp.einsum(
        "mck,xk->xcm", imag_part, x_cosine, precision=HIGHEST
    )
    return jnp.stack([out_real, out_imag], axis=1)


def split_weight(spectral_weight):
    full = spectral_weight.astype(jnp.float32)
    return full.reshape(
        full.shape[0], 2, full.shape[2], full.shape[3] // full.shape[2], full.shape[2]
    )


def mode_product(modes, weight_parts):
    w_real = weight_parts[:, 0]
    w_imag = weight_parts[:, 1]
    m_real = modes[:, 0]
    m_imag = modes[:, 1]
    out_real = jnp.einsum("mik,miko->mok", m_real, w_real, precision=HIGHEST) - jnp.einsum(
        "mik,miko->mok", m_imag, w_imag, precision=HIGHEST
    )
    out_imag = jnp.einsum("mik,miko->mok", m_real, w_imag, precision=HIGHEST) + jnp.einsum(
        "mik,miko->mok", m_imag, w_real, precision=HIGHEST
    )
    return jnp.stack([out_real, out_imag], axis=1)


def mode_adjoint(dmodes, weight_parts):
    w_real = weight_parts[:, 0]
    w_imag = weight_parts[:, 1]
    d_real = dmodes[:, 0]
    d_imag = dmodes[:, 1]
    out_real = jnp.einsum("mok,miko->mik", d_real, w_real, precision=HIGHEST) + jnp.einsum(
        "mok,miko->mik", d_imag, w_imag, precision=HIGHEST
    )
    out_imag = jnp.einsum("mok,miko->mik", d_imag, w_real, precision=HIGHEST) - jnp.einsum(
        "mok,miko->mik", d_real, w_imag, precision=HIGHEST
    )
    return jnp.stack([out_real, out_imag], axis=1)


def mode_gradient(modes, dmodes):
    m_real = modes[:, 0]
    m_imag = modes[:, 1]
    d_real = dmodes[:, 0]
    d_imag = dmodes[:, 1]
    out_real = jnp.einsum("mik,mok->miko", m_real, d_real, precision=HIGHEST) + jnp.einsum(
        "mik,mok->miko", m_imag, d_imag, precision=HIGHEST
    )
    out_imag = jnp.einsum("mik,mok->miko", m_real, d_imag, precision=HIGHEST) - jnp.einsum(
        "mik,mok->miko", m_imag, d_real, precision=HIGHEST
    )
    stacked = jnp.stack([out_real, out_imag], axis=1)
    return stacked.reshape(
        stacked.shape[0], 2, stacked.shape[2], stacked.shape[3] * stacked.shape[4]
    )


def mode_scale(first_mode, mode_count):
    serial = first_mode + jnp.arange(mode_count, dtype=jnp.int32)
    weights = jnp.where(serial % KT == 0, 1.0, 2.0) / (NX * NY * NZ * NT)
    return weights[:, None, None, None]


def gelu_value(values):
    return 0.5 * values * (1.0 + jax.scipy.special.erf(values / math.sqrt(2.0)))


def gelu_slope(values):
    return 0.5 * (1.0 + jax.scipy.special.erf(values / math.sqrt(2.0))) + values * jnp.exp(
        -0.5 * values * values
    ) / math.sqrt(2.0 * math.pi)


def on_device(hidden_field, cotangent, spectral_weight, local_weight, local_bias):
    planes = hidden_field.shape[0]
    mode_count = spectral_weight.shape[0]
    group_size = lax.axis_size("gx")
    own_index = lax.axis_index("gx")
    joint = joint_table()
    y_cosine, y_sine = axis_tables(jnp.arange(NY, dtype=jnp.int32), NY, KY)
    all_cosine, all_sine = axis_tables(jnp.arange(planes * group_size, dtype=jnp.int32), NX, KX)
    factor = mode_scale(own_index * mode_count, mode_count)
    weight_parts = split_weight(spectral_weight)

    def to_owner(spectra):
        moved = lax.all_to_all(spectra, "gx", split_axis=3, concat_axis=0, tiled=True)
        return to_modes(moved, all_cosine, all_sine)

    def to_slabs(mixed):
        return lax.all_to_all(
            to_planes(mixed, all_cosine, all_sine), "gx", split_axis=0, concat_axis=3, tiled=True
        )

    spectra = forward_planes(hidden_field, joint, y_cosine, y_sine)
    modes = to_owner(spectra)
    mixed = mode_product(modes, weight_parts) * factor
    back = to_slabs(mixed)
    local_term = jnp.einsum(
        "xiyp,io->xoyp", hidden_field, local_weight, preferred_element_type=jnp.float32
    )
    pre = (
        inverse_planes(back, joint, y_cosine, y_sine) + local_term + local_bias[None, :, None, None]
    )
    output = gelu_value(pre).astype(jnp.bfloat16)
    slope = cotangent.astype(jnp.float32) * gelu_slope(pre)
    slope_low = slope.astype(jnp.bfloat16)
    local_part = jnp.einsum(
        "xiyp,xoyp->io", hidden_field, slope_low, preferred_element_type=jnp.float32
    )
    bias_part = jnp.sum(slope, axis=(0, 2, 3))
    dspectra = forward_planes(slope_low, joint, y_cosine, y_sine)
    dmodes = to_owner(dspectra) * factor
    grad_spectral = mode_gradient(modes, dmodes)
    dback = to_slabs(mode_adjoint(dmodes, weight_parts))
    local_back = jnp.einsum(
        "xoyp,io->xiyp", slope_low, local_weight, preferred_element_type=jnp.float32
    )
    grad_field = (inverse_planes(dback, joint, y_cosine, y_sine) + local_back).astype(jnp.bfloat16)
    grad_local, grad_bias = lax.psum((local_part, bias_part), "gx")
    return (output, grad_field, grad_spectral, grad_local, grad_bias)


def solution(mesh):
    placed = (
        P(("groups", "gx"), None, None, None),
        P(("groups", "gx"), None, None, None),
        P("gx", None, None, None),
        P(),
        P(),
    )
    return jax.shard_map(
        on_device,
        mesh=mesh,
        in_specs=placed,
        out_specs=(
            P(("groups", "gx"), None, None, None),
            P(("groups", "gx"), None, None, None),
            P("gx", "groups", None, None),
            P("groups", None),
            P("groups"),
        ),
        check_vma=False,
    )
```

profile of v0, /device:TPU:0, one launch (start us, length us, event | category | flops | bytes accessed | tf_op | source)
XLA Modules:
  0.0 529.8 jit_solution(13162627939163591825)
XLA Ops:
  24.2 8.8 %fusion.333 = f32[1024,4,2,32]{3,2,1,0:T(2,128)} fusion(f32[4,1,32,1024]{2,1,0,3:T(1,128)S(1)} %bitcast.325, f32[4,1,32,1024]{2,1,0,3:T(1,128)} %bitcast.327), kind=kLoop, calls=%fused_computation.353 | loop fusion | flops 262144 | bytes 2097152
  39.5 7.5 %all-to-all-start = ((f32[32,1,8192]{2,1,0:T(1,128)}), f32[32,1,8192]{2,1,0:T(1,128)S(1)}, u32[]{:S(2)}, u32[]{:S(2)}) async-start(f32[32,1,8192]{2,1,0:T(1,128)} %reshape.115), calls=%async_computation | async-start | bytes 2097152 | tf_op jit(solution)/shard_map/all_to_all | solution.py:181
  47.0 10.2 %reshape.87 = bf16[32,2,32,16,32]{4,3,2,1,0:T(8,128)(2,1)} reshape(bf16[32,2,32,512]{3,2,1,0:T(8,128)(2,1)} %param.7) | data formatting | bytes 4194304 | tf_op jit(solution)/shard_map/reshape | solution.py:103
  57.2 6.7 %slice_bitcast_fusion.1 = (bf16[32,32,16,32]{3,2,1,0:T(8,128)(2,1)}, bf16[32,32,16,32]{3,2,1,0:T(8,128)(2,1)}) fusion(bf16[32,2,32,16,32]{4,3,2,1,0:T(8,128)(2,1)} %reshape.87), kind=kLoop, calls=%fused_computation.22 | loop fusion | bytes 4194304 | tf_op jit(solution)/shard_map/squeeze | solution.py:109
  63.9 6.7 %copy.254 = bf16[32,32,16,32]{1,3,2,0:T(8,128)(2,1)} copy(bf16[32,32,16,32]{3,2,1,0:T(8,128)(2,1)} %get-tuple-element.46) | data formatting | bytes 2097152 | tf_op jit(solution)/shard_map/squeeze | solution.py:110
  70.6 6.7 %copy.251 = bf16[32,32,16,32]{1,3,2,0:T(8,128)(2,1)} copy(bf16[32,32,16,32]{3,2,1,0:T(8,128)(2,1)} %get-tuple-element.45) | data formatting | bytes 2097152 | tf_op jit(solution)/shard_map/squeeze | solution.py:109
  86.1 7.4 %copy.265 = f32[4,2,32,32,32]{4,2,1,0,3:T(8,128)} copy(f32[4,2,32,32,32]{2,1,0,4,3:T(2,128)} %bitcast.319) | data formatting | bytes 2097152 | tf_op jit(solution)/shard_map/all_to_all | solution.py:181
  112.4 8.7 %fusion.335 = f32[32,16,1,32]{3,2,1,0:T(1,128)S(1)} fusion(f32[32,32,16,1]{1,3,2,0:T(1,128)S(1)} %copy.236, bf16[32,32,16,32]{1,3,2,0:T(8,128)(2,1)} %copy.254), kind=kOutput, calls=%fused_computation.355 | convolution fusion | flops 6291456 | bytes 1179648 | tf_op jit(solution)/shard_map/mik,miko->mok/dot_general | solution.py:113
  121.1 6.6 %fusion.337 = f32[32,16,1,32]{3,2,1,0:T(1,128)S(1)} fusion(f32[32,32,16,1]{1,3,2,0:T(1,128)S(1)} %copy.236, bf16[32,32,16,32]{1,3,2,0:T(8,128)(2,1)S(1)} %copy-done.6), kind=kOutput, calls=%fused_computation.357 | convolution fusion | flops 6291456 | bytes 1179648 | tf_op jit(solution)/shard_map/mik,miko->mok/dot_general | solution.py:116
  127.7 6.6 %fusion.334 = f32[32,16,1,32]{3,2,1,0:T(1,128)S(1)} fusion(f32[32,32,16,1]{1,3,2,0:T(1,128)S(1)} %copy.233, bf16[32,32,16,32]{1,3,2,0:T(8,128)(2,1)S(1)} %copy-done.6), kind=kOutput, calls=%fused_computation.354 | convolution fusion | flops 6291456 | bytes 1179648 | tf_op jit(solution)/shard_map/mik,miko->mok/dot_general | solution.py:113
  134.3 7.0 %fusion.336 = f32[32,16,1,32]{3,2,1,0:T(1,128)S(1)} fusion(f32[32,32,16,1]{1,3,2,0:T(1,128)S(1)} %copy.233, bf16[32,32,16,32]{1,3,2,0:T(8,128)(2,1)S(1)} %copy-done.4), kind=kOutput, calls=%fused_computation.356 | convolution fusion | flops 6291456 | bytes 1179648 | tf_op jit(solution)/shard_map/mik,miko->mok/dot_general | solution.py:116
  161.0 15.5 %fusion.12 = f32[32,4,64,512]{3,0,2,1:T(8,128)} fusion(bf16[4,32,64,512]{3,2,1,0:T(8,128)(2,1)} %param.5, bf16[32,32]{1,0:T(8,128)(2,1)S(1)} %copy-done), kind=kOutput, calls=%fused_computation.19 | convolution fusion | flops 268435456 | bytes 25167872 | tf_op jit(solution)/shard_map/xiyp,io->xoyp/dot_general | solution.py:193
  176.6 10.7 %all-to-all-done.1 = f32[32,1,8192]{2,1,0:T(1,128)S(1)} async-done(((f32[32,1,8192]{2,1,0:T(1,128)}), f32[32,1,8192]{2,1,0:T(1,128)S(1)}, u32[]{:S(2)}, u32[]{:S(2)}) %all-to-all-start.1) | async-done | bytes 1048608 | tf_op jit(solution)/shard_map/all_to_all | solution.py:185
  218.4 22.7 %fusion.329 = (f32[32]{0:T(128)}, bf16[4,32,64,512]{3,2,1,0:T(8,128)(2,1)S(1)}, bf16[4,32,64,512]{3,2,1,0:T(8,128)(2,1)}) fusion(bf16[4,32,64,512]{3,2,1,0:T(8,128)(2,1)S(1)} %bitcast.350, f32[32]{0:T(128)S(1)} %copy-done.13, f32[32,4,64,512]{3,0,2,1:T(8,128)} %fusion.12, bf16[512,64]{0,1:T(8,128)(2,1)S(1)} %get-tuple-element.58, ...), kind=kOutput, calls=%fused_computation.349 | convolution fusion | flops 1149501440 | bytes 44171520 | tf_op jit(solution)/shard_map/xcyq,pq->xcyp/dot_general | solution.py:74
  261.0 8.8 %fusion.332 = f32[1024,4,2,32]{3,2,1,0:T(2,128)} fusion(f32[4,1,32,1024]{2,1,0,3:T(1,128)} %bitcast.328, f32[4,1,32,1024]{2,1,0,3:T(1,128)S(1)} %bitcast.326), kind=kLoop, calls=%fused_computation.352 | loop fusion | flops 262144 | bytes 2097152
  269.8 6.6 %reshape.119 = f32[32,1,8192]{2,1,0:T(1,128)} reshape(f32[1024,4,2,32]{3,2,1,0:T(2,128)} %fusion.332) | data formatting | bytes 2097152
  282.5 23.8 %all-to-all-done.2 = f32[32,1,8192]{2,1,0:T(1,128)S(1)} async-done(((f32[32,1,8192]{2,1,0:T(1,128)}), f32[32,1,8192]{2,1,0:T(1,128)S(1)}, u32[]{:S(2)}, u32[]{:S(2)}) %all-to-all-start.2) | async-done | bytes 1048608 | tf_op jit(solution)/shard_map/all_to_all | solution.py:181
  314.4 7.6 %copy.273 = f32[4,2,32,32,32]{4,2,1,0,3:T(8,128)} copy(f32[4,2,32,32,32]{2,1,0,4,3:T(2,128)} %bitcast.321) | data formatting | bytes 2097152 | tf_op jit(solution)/shard_map/all_to_all | solution.py:181
  372.3 23.3 %fusion.70 = f32[32,32]{0,1:T(8,128)S(1)} fusion(bf16[4,32,64,512]{3,2,1,0:T(8,128)(2,1)} %param.5, bf16[4,32,64,512]{3,2,1,0:T(8,128)(2,1)} %copy-done.3), kind=kOutput, calls=%fused_computation.81 | convolution fusion | flops 268435456 | bytes 16781312 | tf_op jit(solution)/shard_map/xiyp,xoyp->io/dot_general | solution.py:202
  395.6 40.9 %all-reduce = (f32[32,32]{0,1:T(8,128)S(1)}, f32[32]{0:T(128)}) all-reduce(f32[32,32]{0,1:T(8,128)S(1)} %fusion.70, f32[32]{0:T(128)S(1)} %copy-done.12), channel_id=1, replica_groups=mesh['groups'=1,'gx'=32] {'gx'}, use_global_device_ids=true, to_apply=%region_0.1 | all-reduce | flops 1056 | bytes 8448 | tf_op jit(solution)/shard_map/psum | solution.py:214
  437.2 15.8 %fusion.9 = f32[4,64,512,32]{2,3,1,0:T(8,128)} fusion(bf16[4,32,64,512]{3,2,1,0:T(8,128)(2,1)} %copy-done.3, bf16[32,32]{1,0:T(8,128)(2,1)S(1)} %copy-done), kind=kOutput, calls=%fused_computation.16 | convolution fusion | flops 268435456 | bytes 25167872 | tf_op jit(solution)/shard_map/xoyp,io->xiyp/dot_general | solution.py:210
  453.0 8.5 %add_bitcast_fusion = (f32[32,32,16,32]{3,2,1,0:T(8,128)}, f32[32,32,16,32]{3,2,1,0:T(8,128)}) fusion(f32[32,16,32]{1,2,0:T(8,128)S(1)} %copy-done.10, f32[32,16,32]{2,1,0:T(8,128)S(1)} %get-tuple-element.54, f32[32,16,32]{1,2,0:T(8,128)S(1)} %copy-done.11, f32[32,16,32]{2,1,0:T(8,128)S(1)} %get-tuple-element.53), kind=kLoop, calls=%fused_computation.13 | loop fusion | flops 3145728 | bytes 4456448 | tf_op jit(solution)/shard_map/add | solution.py:141
  467.7 7.3 %stack.82 = f32[32,1,32,512]{3,2,1,0:T(8,128)} reshape(f32[32,32,16,32]{3,2,1,0:T(8,128)} %get-tuple-element.52) | data formatting | bytes 4194304 | tf_op jit(solution)/shard_map/stack | solution.py:147
  510.7 18.9 %fusion.5 = bf16[4,32,64,512]{3,2,1,0:T(8,128)(2,1)} fusion(f32[4,64,512,32]{2,3,1,0:T(8,128)} %fusion.9, bf16[4,32,64,64]{3,2,1,0:T(8,128)(2,1)S(1)} %fusion.39, bf16[4,32,64,64]{3,2,1,0:T(8,128)(2,1)S(1)} %fusion.38, bf16[512,64]{0,1:T(8,128)(2,1)S(1)} %get-tuple-element.58, bf16[512,64]{0,1:T(8,128)(2,1)S(1)} %get-tuple-element.57), kind=kOutput, calls=%fused_computation.7 | convolution fusion | flops 1086586880 | bytes 27394048 | tf_op jit(solution)/shard_map/xcyq,pq->xcyp/dot_general | solution.py:74
  (126 shorter events, 235.2 us)
Async XLA Ops:
  0.6 160.4 %copy-start = (bf16[32,32]{1,0:T(8,128)(2,1)S(1)}, bf16[32,32]{1,0:T(8,128)(2,1)}, u32[]{:S(2)}) copy-start(bf16[32,32]{1,0:T(8,128)(2,1)} %param.8) | copy-start | bytes 6148
  7.4 6.7 %copy-start.1 = (f32[4,32,64,128]{3,2,1,0:T(8,128)}, f32[4,32,64,128]{3,2,1,0:T(8,128)S(1)}, u32[]{:S(2)}) copy-start(f32[4,32,64,128]{3,2,1,0:T(8,128)S(1)} %convolution_bitcast_fusion) | copy-start | bytes 12582916
  39.5 37.8 %all-to-all-start = ((f32[32,1,8192]{2,1,0:T(1,128)}), f32[32,1,8192]{2,1,0:T(1,128)S(1)}, u32[]{:S(2)}, u32[]{:S(2)}) async-start(f32[32,1,8192]{2,1,0:T(1,128)} %reshape.115), calls=%async_computation | async-start | bytes 2097152 | tf_op jit(solution)/shard_map/all_to_all | solution.py:181
  112.1 15.5 %copy-start.8 = (f32[16,32,32]{2,0,1:T(8,128)}, f32[16,32,32]{2,0,1:T(8,128)S(1)}, u32[]{:S(2)}) copy-start(f32[16,32,32]{2,0,1:T(8,128)S(1)} %convolution_add_fusion.3) | copy-start | bytes 196612
  112.3 8.7 %copy-start.6 = (bf16[32,32,16,32]{1,3,2,0:T(8,128)(2,1)S(1)}, bf16[32,32,16,32]{1,3,2,0:T(8,128)(2,1)}, u32[]{:S(2)}) copy-start(bf16[32,32,16,32]{1,3,2,0:T(8,128)(2,1)} %copy.251) | copy-start | bytes 3145732
  121.1 13.2 %copy-start.4 = (bf16[32,32,16,32]{1,3,2,0:T(8,128)(2,1)S(1)}, bf16[32,32,16,32]{1,3,2,0:T(8,128)(2,1)}, u32[]{:S(2)}) copy-start(bf16[32,32,16,32]{1,3,2,0:T(8,128)(2,1)} %copy.254) | copy-start | bytes 3145732
  154.9 32.3 %all-to-all-start.1 = ((f32[32,1,8192]{2,1,0:T(1,128)}), f32[32,1,8192]{2,1,0:T(1,128)S(1)}, u32[]{:S(2)}, u32[]{:S(2)}) async-start(f32[32,1,8192]{2,1,0:T(1,128)} %reshape.117), calls=%async_computation.1 | async-start | bytes 2097152 | tf_op jit(solution)/shard_map/all_to_all | solution.py:185
  206.6 11.8 %slice-start = ((s8[8388608]{0:T(1024)(128)(4,1)}), s8[4194304]{0:T(1024)(128)(4,1)S(1)}, s32[]{:S(2)}) async-start(s8[8388608]{0:T(1024)(128)(4,1)} %bitcast.349), calls=%async_computation.4 | async-start | bytes 8388608
  210.2 8.2 %slice-start.1 = ((s8[8388608]{0:T(1024)(128)(4,1)}), s8[4194304]{0:T(1024)(128)(4,1)S(1)}, s32[]{:S(2)}) async-start(s8[8388608]{0:T(1024)(128)(4,1)} %bitcast.349), calls=%async_computation.5 | async-start | bytes 8388608
  214.2 4.1 copy-start.13
  241.0 3.4 copy-start.3
  244.4 6.7 %copy-start.2 = (f32[4,32,64,128]{3,2,1,0:T(8,128)}, f32[4,32,64,128]{3,2,1,0:T(8,128)S(1)}, u32[]{:S(2)}) copy-start(f32[4,32,64,128]{3,2,1,0:T(8,128)S(1)} %fusion.328) | copy-start | bytes 12582916
  269.8 11.4 %copy-start.9 = (f32[16,32,32]{2,0,1:T(8,128)S(1)}, f32[16,32,32]{2,0,1:T(8,128)}, u32[]{:S(2)}) copy-start(f32[16,32,32]{2,0,1:T(8,128)} %copy-done.8) | copy-start | bytes 196612
  276.4 29.9 %all-to-all-start.2 = ((f32[32,1,8192]{2,1,0:T(1,128)}), f32[32,1,8192]{2,1,0:T(1,128)S(1)}, u32[]{:S(2)}, u32[]{:S(2)}) async-start(f32[32,1,8192]{2,1,0:T(1,128)} %reshape.119), calls=%async_computation.2 | async-start | bytes 2097152 | tf_op jit(solution)/shard_map/all_to_all | solution.py:181
  333.3 7.8 %copy-start.7 = (bf16[32,32,16,32]{1,3,2,0:T(8,128)(2,1)S(1)}, bf16[32,32,16,32]{1,3,2,0:T(8,128)(2,1)}, u32[]{:S(2)}) copy-start(bf16[32,32,16,32]{1,3,2,0:T(8,128)(2,1)} %copy.251) | copy-start | bytes 3145732
  338.7 5.8 %copy-start.5 = (bf16[32,32,16,32]{1,3,2,0:T(8,128)(2,1)S(1)}, bf16[32,32,16,32]{1,3,2,0:T(8,128)(2,1)}, u32[]{:S(2)}) copy-start(bf16[32,32,16,32]{1,3,2,0:T(8,128)(2,1)} %copy.254) | copy-start | bytes 3145732
  368.3 111.2 %all-to-all-start.3 = ((f32[32,1,8192]{2,1,0:T(1,128)}), f32[32,1,8192]{2,1,0:T(1,128)S(1)}, u32[]{:S(2)}, u32[]{:S(2)}) async-start(f32[32,1,8192]{2,1,0:T(1,128)} %reshape.121), calls=%async_computation.3 | async-start | bytes 2097152 | tf_op jit(solution)/shard_map/all_to_all | solution.py:185
  372.3 23.3 %copy-start.12 = (f32[32]{0:T(128)S(1)}, f32[32]{0:T(128)}, u32[]{:S(2)}) copy-start(f32[32]{0:T(128)} %get-tuple-element.42) | copy-start | bytes 388
  437.2 15.8 %copy-start.10 = (f32[32,16,32]{1,2,0:T(8,128)S(1)}, f32[32,16,32]{1,2,0:T(8,128)}, u32[]{:S(2)}) copy-start(f32[32,16,32]{1,2,0:T(8,128)} %copy.226) | copy-start | bytes 196612
  437.2 15.8 %copy-start.11 = (f32[32,16,32]{1,2,0:T(8,128)S(1)}, f32[32,16,32]{1,2,0:T(8,128)}, u32[]{:S(2)}) copy-start(f32[32,16,32]{1,2,0:T(8,128)} %copy.225) | copy-start | bytes 196612
where the time goes:
time: 540 us; the launch traced here: 530 us
  matrix products  234 us (43%)
  local copies, waits for them, and re-layouts  153 us (28%)
  other arithmetic  45 us (8%)
  blocking collectives  40.9 us (8%)
  waiting for transfers between devices  34.4 us (6%)
  starting transfers between devices  21.2 us (4%)
    unnamed x43, local copies, waits for them, and re-layouts  43.9 us
    dot_general x2, matrix products, inverse_planes(): jnp.einsum('xcyq,pq->xcyp', joined, joint, preferred_element_type=jnp.flo...  41.6 us
    psum x1, blocking collectives, on_device(): grad_local, grad_bias = lax.psum((local_part, bias_part), 'gx')  40.9 us
    all_to_all x2, waiting for transfers between devices, to_owner(): lax.all_to_all(spectra, 'gx', split_axis=3, concat_axis=0, tiled=True)  23.8 us
    dot_general x1, matrix products, on_device(): jnp.einsum('xiyp,xoyp->io', hidden_field, slope_low, preferred_element_ty...  23.3 us
    reshape x4, local copies, waits for them, and re-layouts, inverse_planes(): spectra.reshape(spectra.shape[0], 2, spectra.shape[2], kept_y, spectra.sh...  19.1 us
    unnamed x3, other arithmetic  17.7 us
    dot_general x1, matrix products, on_device(): jnp.einsum('xoyp,io->xiyp', slope_low, local_weight, preferred_element_ty...  15.8 us
  transfers between devices with their start and end apart: 4, of which 2 were waited for; matrix products, arithmetic and copies ran while one was open for 22% of the time, Pallas kernels for 0%

commit v1 on v0

v1 whole, which is shorter than its diff:
```python
import functools
import math

import jax
import jax.numpy as jnp
import ml_dtypes
import numpy as np
from jax import lax
from jax.experimental import pallas as pl
from jax.experimental.pallas import tpu as pltpu
from jax.sharding import PartitionSpec as P

NX, NY, NZ, NT = 128, 64, 64, 8
KX, KY, KZ, KT = 16, 16, 16, 4
C = 32
Q = KZ * KT
CELLS = NZ * NT
YB = 16
F32, BF16 = jnp.float32, jnp.bfloat16
HIGHEST = lax.Precision.HIGHEST
MIB = 1 << 20


def frequency(kept):
    serial = np.arange(kept)
    return np.where(serial < kept // 2, serial, serial - kept)


def angles(positions, length, kept):
    wound = (np.asarray(positions)[:, None] * frequency(kept)[None, :]) % length
    return 2.0 * math.pi / length * wound


def split2(table):
    high = table.astype(ml_dtypes.bfloat16)
    low = (table - high.astype(np.float64)).astype(ml_dtypes.bfloat16)
    return high, low


def zt_tables(modes_here):
    cells = np.arange(CELLS)
    depth, moment = cells // NT, cells % NT
    kept_z, kept_t = np.repeat(frequency(KZ), KT), np.tile(np.arange(KT), KZ)
    wound = (depth[:, None] * kept_z * NT + moment[:, None] * kept_t * NZ) % CELLS
    theta = 2.0 * math.pi / CELLS * wound
    cosine, sine = np.cos(theta), np.sin(theta)
    groups = Q // modes_here
    shape = (CELLS, groups, modes_here)
    cosine, sine = cosine.reshape(shape), sine.reshape(shape)
    first = np.stack([cosine, -sine], axis=2).reshape(CELLS, 2 * Q)
    second = np.stack([-sine, -cosine], axis=2).reshape(CELLS, 2 * Q)
    return np.concatenate([first, second], axis=1).astype(ml_dtypes.bfloat16)


def y_forward_table():
    theta = angles(np.arange(NY), NY, KY)
    table = np.concatenate([np.cos(theta), np.sin(theta)], axis=0).T
    high, low = split2(table)
    return np.concatenate([high, low], axis=0)


def y_inverse_table():
    theta = angles(np.arange(NY), NY, KY)
    table = np.concatenate([np.cos(theta), np.sin(theta)], axis=0)
    high, low = split2(table)
    return np.concatenate([high, high, low], axis=1)


def x_tables(planes, devices):
    theta = angles(np.arange(devices) * planes, NX, KX).T
    cosine, sine = np.cos(theta), np.sin(theta)
    forward = np.block([[cosine, sine], [-sine, cosine]]).astype(np.float32)
    turn = np.repeat(angles(np.arange(planes), NX, KX).T, C, axis=1)
    return (
        forward,
        np.ascontiguousarray(forward.T),
        np.cos(turn).astype(np.float32),
        np.sin(turn).astype(np.float32),
    )


def diagonal_mask():
    return (np.arange(KX * C)[None, :] // C == np.arange(KX)[:, None]).astype(np.float32)


def halves(value):
    high = value.astype(BF16)
    return high, (value - high.astype(F32)).astype(BF16)


def dot(left, right):
    return jnp.dot(left, right, preferred_element_type=F32)


def lane_total(value, step):
    span = value.shape[1] // 2
    while span >= step:
        value = value + pltpu.roll(value, span, 1)
        span //= 2
    return value


def y_forward(sums, y_table, gathered, first_row, lanes):
    count = sums.shape[0] // NY
    for pair in range(0, count, 2):
        one = sums[pair * NY : (pair + 1) * NY].astype(BF16)
        two = sums[(pair + 1) * NY : (pair + 2) * NY].astype(BF16)
        right = jnp.concatenate(
            [
                jnp.concatenate([one[:, : 2 * Q], two[:, : 2 * Q]], axis=1),
                jnp.concatenate([one[:, 2 * Q :], two[:, 2 * Q :]], axis=1),
            ],
            axis=0,
        )
        both = dot(y_table, right)
        out = both[:KY] + both[KY:]
        gathered[pl.ds(first_row + pair, KY, stride=lanes), :] = out[:, : 2 * Q]
        gathered[pl.ds(first_row + pair + 1, KY, stride=lanes), :] = out[:, 2 * Q :]


def send_layout(gathered, out_ref, lanes):
    for ky in range(KY):
        out_ref[ky * 2 * Q : (ky + 1) * 2 * Q, :] = gathered[ky * lanes : (ky + 1) * lanes, :].T


def forward_kernel(field, zt, y_table, out, gathered, *, lanes, block):
    plane, part = pl.program_id(0), pl.program_id(1)
    sums = dot(field[0].reshape(block * NY, CELLS), zt[...])
    y_forward(sums, y_table[...], gathered, plane * C + part * block, lanes)

    @pl.when((plane == pl.num_programs(0) - 1) & (part == pl.num_programs(1) - 1))
    def _():
        send_layout(gathered, out, lanes)


def forward_planes(field, zt, y_table):
    planes = field.shape[0]
    lanes, block = planes * C, 8
    return pl.pallas_call(
        functools.partial(forward_kernel, lanes=lanes, block=block),
        grid=(planes, C // block),
        in_specs=[
            pl.BlockSpec((1, block, NY, CELLS), lambda x, c: (x, c, 0, 0)),
            pl.BlockSpec(zt.shape, lambda x, c: (0, 0)),
            pl.BlockSpec(y_table.shape, lambda x, c: (0, 0)),
        ],
        out_specs=pl.BlockSpec((KY * 2 * Q, lanes), lambda x, c: (0, 0)),
        out_shape=jax.ShapeDtypeStruct((KY * 2 * Q, lanes), F32),
        scratch_shapes=[pltpu.VMEM((KY * lanes, 2 * Q), F32)],
        compiler_params=pltpu.CompilerParams(vmem_limit_bytes=32 * MIB),
        cost_estimate=pl.CostEstimate(flops=2 * 10**9, bytes_accessed=9 * MIB, transcendentals=0),
    )(field, zt, y_table)


QB = 8


def modes_of(received, q_count, devices, lanes, forward, cosine, sine):
    columns = []
    for q in range(q_count):
        parts = [
            received[pl.ds(ri * q_count + q, devices, stride=2 * q_count), :] for ri in range(2)
        ]
        columns.append(jnp.concatenate(parts, axis=0))
    right = jnp.concatenate(columns, axis=1) if lanes % 128 == 0 else None
    found = []
    if right is not None:
        summed = jnp.dot(forward, right, precision=HIGHEST, preferred_element_type=F32)
    for q in range(q_count):
        if right is not None:
            one = summed[:, q * lanes : (q + 1) * lanes]
        else:
            one = jnp.dot(forward, columns[q], precision=HIGHEST, preferred_element_type=F32)
        a_re, a_im = one[:KX], one[KX:]
        m_re = lane_total(a_re * cosine + a_im * sine, C)
        m_im = lane_total(a_im * cosine - a_re * sine, C)
        found.append((m_re, m_im))
    return found


def to_planes(mixed, out, q_count, devices, lanes, inverse, cosine, sine):
    turned = []
    for re, im in mixed:
        turned.append(
            jnp.concatenate([re * cosine - im * sine, re * sine + im * cosine], axis=0)
        )
    if lanes % 128 == 0:
        joined = jnp.concatenate(turned, axis=1)
        back = jnp.dot(inverse, joined, precision=HIGHEST, preferred_element_type=F32)
        backs = [back[:, q * lanes : (q + 1) * lanes] for q in range(q_count)]
    else:
        backs = [
            jnp.dot(inverse, one, precision=HIGHEST, preferred_element_type=F32) for one in turned
        ]
    for q in range(q_count):
        for ri in range(2):
            out[pl.ds(ri * q_count + q, devices, stride=2 * q_count), :] = backs[q][
                ri * devices : (ri + 1) * devices
            ]


def mode_factor(first, q):
    time_frequency = lax.rem(first + q, KT)
    return jnp.where(time_frequency == 0, 1.0, 2.0).astype(F32) / (NX * NY * NZ * NT)


def mix_kernel(
    received, weight, forward, inverse, cosine, sine, mask, out, modes_out, *, devices, lanes
):
    first = pl.program_id(0) * QB
    flat_in = received.reshape(devices * 2 * QB, lanes)
    flat_out = out.reshape(devices * 2 * QB, lanes)
    modes = modes_of(flat_in, QB, devices, lanes, forward[...], cosine[...], sine[...])
    mixed = []
    for q in range(QB):
        both = jnp.concatenate(modes[q], axis=0)
        modes_out[q] = both
        high, low = halves(both[:, :C])
        left = jnp.concatenate([high, low], axis=0)
        by_re, by_im = dot(left, weight[q, 0]), dot(left, weight[q, 1])
        by_re, by_im = by_re[: 2 * KX] + by_re[2 * KX :], by_im[: 2 * KX] + by_im[2 * KX :]
        factor = mode_factor(first, q)
        pieces = []
        for wide in (by_re[:KX] - by_im[KX:], by_im[:KX] + by_re[KX:]):
            kept = wide * mask[...]
            total = kept[:, :128]
            for column in range(128, KX * C, 128):
                total = total + kept[:, column : column + 128]
            pieces.append(lane_total(total, C)[:, :lanes] * factor)
        mixed.append(pieces)
    to_planes(mixed, flat_out, QB, devices, lanes, inverse[...], cosine[...], sine[...])


def whole(array):
    return pl.BlockSpec(array.shape, lambda *_: (0,) * array.ndim)


def mode_specs(devices, modes_here, lanes):
    slab = pl.BlockSpec((devices, 2, QB, lanes), lambda s: (0, 0, s, 0))
    weight = pl.BlockSpec((QB, 2, C, KX * C), lambda s: (s, 0, 0, 0))
    modes = pl.BlockSpec((QB, 2 * KX, lanes), lambda s: (s, 0, 0))
    return slab, weight, modes


def mix_modes(received, weight, tables):
    devices, _, modes_here, lanes = received.shape
    slab, weight_spec, modes = mode_specs(devices, modes_here, lanes)
    return pl.pallas_call(
        functools.partial(mix_kernel, devices=devices, lanes=lanes),
        grid=(modes_here // QB,),
        in_specs=[slab, weight_spec] + [whole(table) for table in tables],
        out_specs=[slab, modes],
        out_shape=[
            jax.ShapeDtypeStruct(received.shape, F32),
            jax.ShapeDtypeStruct((modes_here, 2 * KX, lanes), F32),
        ],
        compiler_params=pltpu.CompilerParams(vmem_limit_bytes=32 * MIB),
        cost_estimate=pl.CostEstimate(flops=10**9, bytes_accessed=5 * MIB, transcendentals=0),
    )(received, weight, *tables)


def spread(value, mask):
    if value.shape[1] < 128:
        value = jnp.concatenate([value] * (128 // value.shape[1]), axis=1)
    else:
        value = value[:, :128]
    return jnp.concatenate([value] * (KX * C // 128), axis=1) * mask


def adjoint_kernel(
    received, weight, forward, inverse, cosine, sine, mask, out, modes_out, *, devices, lanes
):
    first = pl.program_id(0) * QB
    flat_in = received.reshape(devices * 2 * QB, lanes)
    flat_out = out.reshape(devices * 2 * QB, lanes)
    modes = modes_of(flat_in, QB, devices, lanes, forward[...], cosine[...], sine[...])
    group = lax.broadcasted_iota(jnp.int32, (KX, 128), 1) // C
    odd = group % 2 == 1
    mixed = []
    for q in range(QB):
        factor = mode_factor(first, q)
        d_re, d_im = modes[q][0] * factor, modes[q][1] * factor
        modes_out[q] = jnp.concatenate([d_re, d_im], axis=0)
        wide = jnp.concatenate([spread(d_re, mask[...]), spread(d_im, mask[...])], axis=0)
        high, low = halves(wide)
        left = jnp.concatenate([high, low], axis=0)
        right = jnp.concatenate([weight[q, 0], weight[q, 1]] * 2, axis=0)
        product = lax.dot_general(
            left, right, (((1,), (1,)), ((), ())), preferred_element_type=F32
        )
        product = product[: 2 * KX] + product[2 * KX :]
        re = product[:KX] + pltpu.roll(product[KX:], 128 - C, 1)
        im = product[KX:] - pltpu.roll(product[:KX], 128 - C, 1)
        re = jnp.where(odd, pltpu.roll(re, C, 1), re)
        im = jnp.where(odd, pltpu.roll(im, C, 1), im)
        mixed.append((re[:, :lanes], im[:, :lanes]))
    to_planes(mixed, flat_out, QB, devices, lanes, inverse[...], cosine[...], sine[...])


def adjoint_modes(received, weight, tables):
    devices, _, modes_here, lanes = received.shape
    slab, weight_spec, modes = mode_specs(devices, modes_here, lanes)
    return pl.pallas_call(
        functools.partial(adjoint_kernel, devices=devices, lanes=lanes),
        grid=(modes_here // QB,),
        in_specs=[slab, weight_spec] + [whole(table) for table in tables],
        out_specs=[slab, modes],
        out_shape=[
            jax.ShapeDtypeStruct(received.shape, F32),
            jax.ShapeDtypeStruct((modes_here, 2 * KX, lanes), F32),
        ],
        compiler_params=pltpu.CompilerParams(vmem_limit_bytes=32 * MIB),
        cost_estimate=pl.CostEstimate(flops=10**9, bytes_accessed=5 * MIB, transcendentals=0),
    )(received, weight, *tables)


def gradient_kernel(modes, dmodes, mask, out):
    for q in range(QB):
        left = modes[q][:, :C]
        l_high, l_low = halves(left)
        left = jnp.concatenate([l_high, l_high, l_low], axis=0)
        d_re, d_im = spread(dmodes[q, :KX], mask[...]), spread(dmodes[q, KX:], mask[...])
        for part, rows in ((0, (d_re, d_im)), (1, (d_im, -d_re))):
            high, low = halves(jnp.concatenate(rows, axis=0))
            right = jnp.concatenate([high, low, high], axis=0)
            out[q, part] = lax.dot_general(
                left, right, (((0,), (0,)), ((), ())), preferred_element_type=F32
            )


def mode_gradient(modes, dmodes, mask):
    modes_here, _, lanes = modes.shape
    spec = pl.BlockSpec((QB, 2 * KX, lanes), lambda s: (s, 0, 0))
    return pl.pallas_call(
        gradient_kernel,
        grid=(modes_here // QB,),
        in_specs=[spec, spec, whole(mask)],
        out_specs=pl.BlockSpec((QB, 2, C, KX * C), lambda s: (s, 0, 0, 0)),
        out_shape=jax.ShapeDtypeStruct((modes_here, 2, C, KX * C), F32),
        compiler_params=pltpu.CompilerParams(vmem_limit_bytes=32 * MIB),
        cost_estimate=pl.CostEstimate(flops=10**8, bytes_accessed=5 * MIB, transcendentals=0),
    )(modes, dmodes, mask)


def planes_layout(back, gathered, lanes):
    for ky in range(KY):
        gathered[ky * lanes : (ky + 1) * lanes, :] = back[ky * 2 * Q : (ky + 1) * 2 * Q, :].T


def y_inverse(gathered, y_table, inverse_y, plane, lanes):
    for c in range(0, C, 2):
        row = plane * C + c
        pair = jnp.concatenate(
            [
                gathered[pl.ds(row, KY, stride=lanes), :],
                gathered[pl.ds(row + 1, KY, stride=lanes), :],
            ],
            axis=1,
        )
        high, low = halves(pair)
        both = dot(y_table, jnp.concatenate([high, low, high], axis=0)).astype(BF16)
        for k in range(2):
            columns = slice(k * 2 * Q, (k + 1) * 2 * Q)
            inverse_y[c + k, :, : 2 * Q] = both[:NY, columns]
            inverse_y[c + k, :, 2 * Q :] = both[NY:, columns]


def middle_kernel(
    back,
    field,
    cotangent,
    local,
    bias,
    zt,
    zt_turned,
    y_back,
    y_table,
    out,
    slope_out,
    spectra,
    local_grad,
    bias_grad,
    gathered,
    inverse_y,
    pre,
    sums,
    collected,
    *,
    lanes,
):
    plane, part = pl.program_id(0), pl.program_id(1)
    rows = C * YB
    first_step = (plane == 0) & (part == 0)
    last_step = (plane == pl.num_programs(0) - 1) & (part == pl.num_programs(1) - 1)

    @pl.when(first_step)
    def _():
        planes_layout(back, gathered, lanes)
        local_grad[...] = jnp.zeros_like(local_grad)
        bias_grad[...] = jnp.zeros_like(bias_grad)

    @pl.when(part == 0)
    def _():
        y_inverse(gathered, y_back[...], inverse_y, plane, lanes)

    y_rows = pl.ds(pl.multiple_of(part * YB, YB), YB)
    values = field[0].reshape(rows, CELLS)
    own = inverse_y[:, y_rows, :].reshape(rows, 4 * Q)
    pre[...] = dot(local[...], values) + dot(own, zt_turned[...])

    chunk = 2
    half_root = 1.0 / math.sqrt(2.0)

    def pointwise(step, _):
        c = step * chunk
        r = pl.ds(pl.multiple_of(c * YB, chunk * YB), chunk * YB)
        v = pre[r, :] + bias[r, :]
        grade = cotangent[0, pl.ds(c, chunk)].reshape(chunk * YB, CELLS).astype(F32)
        normal = 0.5 + 0.5 * lax.erf(v * half_root)
        result = v * normal
        slope = grade * (normal + v * (jnp.exp(-0.5 * v * v) * (1.0 / math.sqrt(2.0 * math.pi))))
        out[0, pl.ds(c, chunk)] = result.astype(BF16).reshape(chunk, YB, CELLS)
        slope_out[0, pl.ds(c, chunk)] = slope.astype(BF16).reshape(chunk, YB, CELLS)
        folded = slope[:, :128]
        for column in range(128, CELLS, 128):
            folded = folded + slope[:, column : column + 128]
        bias_grad[r, :] += folded
        return 0

    lax.fori_loop(0, C // chunk, pointwise, 0, unroll=False)

    low = slope_out[0].reshape(rows, CELLS)
    sums[:, y_rows, :] = dot(low, zt[...]).reshape(C, YB, 4 * Q)
    local_grad[...] += lax.dot_general(
        values, low, (((1,), (1,)), ((), ())), preferred_element_type=F32
    )

    @pl.when(part == pl.num_programs(1) - 1)
    def _():
        y_forward(sums.reshape(C * NY, 4 * Q), y_table[...], collected, plane * C, lanes)

    @pl.when(last_step)
    def _():
        send_layout(collected, spectra, lanes)


def middle(back, field, cotangent, local, bias, zt, zt_turned, y_back, y_table):
    planes = field.shape[0]
    lanes, rows = planes * C, C * YB
    block = pl.BlockSpec((1, C, YB, CELLS), lambda x, y: (x, 0, y, 0))
    return pl.pallas_call(
        functools.partial(middle_kernel, lanes=lanes),
        grid=(planes, NY // YB),
        in_specs=[
            whole(back),
            block,
            block,
            whole(local),
            whole(bias),
            whole(zt),
            whole(zt_turned),
            whole(y_back),
            whole(y_table),
        ],
        out_specs=[
            block,
            block,
            pl.BlockSpec((KY * 2 * Q, lanes), lambda x, y: (0, 0)),
            pl.BlockSpec((rows, rows), lambda x, y: (0, 0)),
            pl.BlockSpec((rows, 128), lambda x, y: (0, 0)),
        ],
        out_shape=[
            jax.ShapeDtypeStruct(field.shape, BF16),
            jax.ShapeDtypeStruct(field.shape, BF16),
            jax.ShapeDtypeStruct((KY * 2 * Q, lanes), F32),
            jax.ShapeDtypeStruct((rows, rows), F32),
            jax.ShapeDtypeStruct((rows, 128), F32),
        ],
        scratch_shapes=[
            pltpu.VMEM((KY * lanes, 2 * Q), F32),
            pltpu.VMEM((C, NY, 4 * Q), BF16),
            pltpu.VMEM((rows, CELLS), F32),
            pltpu.VMEM((C, NY, 4 * Q), F32),
            pltpu.VMEM((KY * lanes, 2 * Q), F32),
        ],
        compiler_params=pltpu.CompilerParams(vmem_limit_bytes=48 * MIB),
        cost_estimate=pl.CostEstimate(
            flops=13 * 10**9, bytes_accessed=34 * MIB, transcendentals=8 * 10**6
        ),
    )(back, field, cotangent, local, bias, zt, zt_turned, y_back, y_table)


def last_kernel(back, slope, local, zt_turned, y_back, out, gathered, inverse_y, *, lanes):
    plane, part = pl.program_id(0), pl.program_id(1)
    rows = C * YB

    @pl.when((plane == 0) & (part == 0))
    def _():
        planes_layout(back, gathered, lanes)

    @pl.when(part == 0)
    def _():
        y_inverse(gathered, y_back[...], inverse_y, plane, lanes)

    y_rows = pl.ds(pl.multiple_of(part * YB, YB), YB)
    low = slope[0].reshape(rows, CELLS)
    own = inverse_y[:, y_rows, :].reshape(rows, 4 * Q)
    total = dot(local[...], low) + dot(own, zt_turned[...])
    out[0] = total.astype(BF16).reshape(C, YB, CELLS)


def last(back, slope, local, zt_turned, y_back):
    planes = slope.shape[0]
    lanes = planes * C
    block = pl.BlockSpec((1, C, YB, CELLS), lambda x, y: (x, 0, y, 0))
    return pl.pallas_call(
        functools.partial(last_kernel, lanes=lanes),
        grid=(planes, NY // YB),
        in_specs=[whole(back), block, whole(local), whole(zt_turned), whole(y_back)],
        out_specs=block,
        out_shape=jax.ShapeDtypeStruct(slope.shape, BF16),
        scratch_shapes=[
            pltpu.VMEM((KY * lanes, 2 * Q), F32),
            pltpu.VMEM((C, NY, 4 * Q), BF16),
        ],
        compiler_params=pltpu.CompilerParams(vmem_limit_bytes=32 * MIB),
        cost_estimate=pl.CostEstimate(
            flops=6 * 10**9, bytes_accessed=17 * MIB, transcendentals=0
        ),
    )(back, slope, local, zt_turned, y_back)


def on_device(hidden_field, cotangent, spectral_weight, local_weight, local_bias):
    planes, modes_here = hidden_field.shape[0], spectral_weight.shape[0]
    devices = lax.axis_size("gx")
    lanes = planes * C
    zt_host = zt_tables(modes_here)
    zt, zt_turned = jnp.asarray(zt_host), jnp.asarray(np.ascontiguousarray(zt_host.T))
    y_table, y_back = jnp.asarray(y_forward_table()), jnp.asarray(y_inverse_table())
    mask = jnp.asarray(diagonal_mask())
    tables = [jnp.asarray(table) for table in x_tables(planes, devices)] + [mask]

    eye = jnp.eye(YB, dtype=BF16)
    rows = C * YB
    local_back = (local_weight[:, None, :, None] * eye[None, :, None, :]).reshape(rows, rows)
    local_here = (local_weight.T[:, None, :, None] * eye[None, :, None, :]).reshape(rows, rows)
    bias = jnp.repeat(local_bias, YB)[:, None]

    def exchange(value):
        return lax.all_to_all(value, "gx", split_axis=0, concat_axis=0, tiled=True)

    def to_owner(spectra):
        return exchange(spectra.reshape(devices, 2, modes_here, lanes))

    def to_slabs(back):
        return exchange(back).reshape(KY * 2 * Q, lanes)

    spectra = forward_planes(hidden_field, zt, y_table)
    back, modes = mix_modes(to_owner(spectra), spectral_weight, tables)
    output, slope, dspectra, local_part, bias_part = middle(
        to_slabs(back), hidden_field, cotangent, local_here, bias, zt, zt_turned, y_back, y_table
    )
    dback, dmodes = adjoint_modes(to_owner(dspectra), spectral_weight, tables)
    grad_spectral = mode_gradient(modes, dmodes, mask)
    local_sum = jnp.einsum("iyoy->io", local_part.reshape(C, YB, C, YB))
    bias_sum = jnp.sum(bias_part.reshape(C, YB * 128), axis=1)
    partial = jnp.concatenate([local_sum.reshape(C * C // 128, 128), jnp.tile(bias_sum, 4)[None]])
    total = jnp.sum(lax.all_gather(partial, "gx"), axis=0)
    grad_local = total[: C * C // 128].reshape(C, C)
    grad_bias = total[C * C // 128, :C]
    grad_field = last(to_slabs(dback), slope, local_back, zt_turned, y_back)
    return (output, grad_field, grad_spectral, grad_local, grad_bias)


def solution(mesh):
    placed = (
        P(("groups", "gx"), None, None, None),
        P(("groups", "gx"), None, None, None),
        P("gx", None, None, None),
        P(),
        P(),
    )
    return jax.shard_map(
        on_device,
        mesh=mesh,
        in_specs=placed,
        out_specs=(
            P(("groups", "gx"), None, None, None),
            P(("groups", "gx"), None, None, None),
            P("gx", "groups", None, None),
            P("groups", None),
            P("groups"),
        ),
        check_vma=False,
    )
```

time: 540 us -> 266 us (0.49); the launches traced: 530 us -> 266 us
  matrix products: 234 us -> 0 us
  local copies, waits for them, and re-layouts: 153 us -> 33.9 us
  Pallas kernels: 0 us -> 96.3 us
  blocking collectives: 40.9 us -> 105 us
  other arithmetic: 45 us -> 8.39 us
  waiting for transfers between devices: 34.4 us -> 13.6 us
  starting transfers between devices: 21.2 us -> 7.42 us
    dot_general x47 -> x0, matrix products: 234 us -> none  [the longest x2 41.6 us: inverse_planes(): jnp.einsum('xcyq,pq->xcyp', joined, joint, preferred_element_type=jnp.flo...]
    pallas_call x0 -> x6, Pallas kernels: none -> 96.3 us  [the longest x1 57.9 us: middle(): pl.pallas_call(functools.partial(middle_kernel, lanes=lanes), grid=(plane...]
    all_to_all x0 -> x2, blocking collectives: none -> 63 us  [exchange(): return lax.all_to_all(value, 'gx', split_axis=0, concat_axis=0, tiled=True)]
    all_gather x0 -> x1, blocking collectives: none -> 42.3 us  [on_device(): total = jnp.sum(lax.all_gather(partial, 'gx'), axis=0)]
    psum x1 -> x0, blocking collectives: 40.9 us -> none  [on_device(): grad_local, grad_bias = lax.psum((local_part, bias_part), 'gx')]
    unnamed x43 -> x44, local copies, waits for them, and re-layouts: 43.9 us -> 10.4 us
    squeeze x7 -> x1, local copies, waits for them, and re-layouts: 28.4 us -> 0.51 us  [on_device(): grad_bias = total[C * C // 128, :C]]
    another operation x9 -> x3, local copies, waits for them, and re-layouts: 28.5 us -> 0.96 us  [the longest x1 0.87 us: on_device(): bias = jnp.repeat(local_bias, YB)[:, None]]
  transfers between devices with their start and end apart: 4 -> 2, of which waited for: 2 -> 1; matrix products, arithmetic and copies ran while one was open for 22% -> 12% of each run, Pallas kernels for 0% -> 1%
where the time goes in v1:
time: 266 us
  blocking collectives  105 us (39%)
  Pallas kernels  96.3 us (36%)
  local copies, waits for them, and re-layouts  33.9 us (13%)
  waiting for transfers between devices  13.6 us (5%)
  other arithmetic  8.39 us (3%)
  starting transfers between devices  7.42 us (3%)
    all_to_all x2, blocking collectives, exchange(): return lax.all_to_all(value, 'gx', split_axis=0, concat_axis=0, tiled=True)  63 us
    pallas_call x1, Pallas kernels, middle(): pl.pallas_call(functools.partial(middle_kernel, lanes=lanes), grid=(plane...  57.9 us
    all_gather x1, blocking collectives, on_device(): total = jnp.sum(lax.all_gather(partial, 'gx'), axis=0)  42.3 us
    pallas_call x1, Pallas kernels, last(): pl.pallas_call(functools.partial(last_kernel, lanes=lanes), grid=(planes,...  14 us
    all_to_all x2, waiting for transfers between devices, exchange(): return lax.all_to_all(value, 'gx', split_axis=0, concat_axis=0, tiled=True)  13.6 us
    unnamed x44, local copies, waits for them, and re-layouts  10.4 us
    pallas_call x1, Pallas kernels, forward_planes(): pl.pallas_call(functools.partial(forward_kernel, lanes=lanes, block=block...  8.79 us
    mul x1, local copies, waits for them, and re-layouts, on_device(): local_weight[:, None, :, None] * eye[None, :, None, :]  8.43 us
  transfers between devices with their start and end apart: 2, of which 1 were waited for; matrix products, arithmetic and copies ran while one was open for 12% of the time, Pallas kernels for 1%

profile of v1, /device:TPU:0, one launch (start us, length us, event | category | flops | bytes accessed | tf_op | source)
XLA Modules:
  0.0 265.8 jit_solution(13201480581539641527)
XLA Ops:
  0.6 3.4 %copy-done = bf16[4,32,64,512]{3,2,1,0:T(8,128)(2,1)S(1)} copy-done((bf16[4,32,64,512]{3,2,1,0:T(8,128)(2,1)S(1)}, bf16[4,32,64,512]{3,2,1,0:T(8,128)(2,1)}, u32[]{:S(2)}) %copy-start) | copy-done | bytes 8388632
  4.0 0.9 copy-done.2
  5.0 0.7 copy-done.8
  5.7 8.8 %shard_map.173 = f32[2048,128]{1,0:T(8,128)S(1)} custom-call(bf16[4,32,64,512]{3,2,1,0:T(8,128)(2,1)S(1)} %copy-done, bf16[512,256]{1,0:T(8,128)(2,1)S(1)} %copy-done.2, bf16[32,128]{1,0:T(8,128)(2,1)S(1)} %copy-done.8), custom_call_target="tpu_custom_call" | custom-call | flops 2000000000 | bytes 9437184 | tf_op jit(solution)/shard_map/pallas_call | solution.py:139
  14.5 33.3 %all_to_all.20.received = f32[32,2,32,128]{3,2,1,0:T(8,128)S(1)} all-to-all(f32[32,2,32,128]{3,2,1,0:T(8,128)S(1)} %bitcast.13), channel_id=1, replica_groups=mesh['groups'=1,'gx'=32] {'gx'}, dimensions={0} | all-to-all | bytes 2097152 | tf_op jit(solution)/shard_map/all_to_all | solution.py:550
  47.9 6.7 %shard_map.174 = (f32[32,2,32,128]{3,2,1,0:T(8,128)}, f32[32,32,128]{2,1,0:T(8,128)S(1)}) custom-call(f32[32,2,32,128]{3,2,1,0:T(8,128)S(1)} %all_to_all.20.received, bf16[32,2,32,512]{3,2,1,0:T(8,128)(2,1)S(1)} %copy-done.10, f32[32,64]{1,0:T(8,128)S(1)} %copy-done.16, f32[64,32]{1,0:T(8,128)S(1)} %copy-done.15, f32[16,128]{1,0:T(8,128)S(1)} %copy-done.17, ...), custom_call_target="tpu_custom_call" | custom-call | flops 1000000000 | bytes 5242880 | tf_op jit(solution)/shard_map/pallas_call | solution.py:248
  54.6 3.6 %all-to-all-start.1 = ((f32[32,2,32,128]{3,2,1,0:T(8,128)}), f32[32,2,32,128]{3,2,1,0:T(8,128)S(1)}, u32[]{:S(2)}, u32[]{:S(2)}) async-start(f32[32,2,32,128]{3,2,1,0:T(8,128)} %get-tuple-element.14), calls=%async_computation.1 | async-start | bytes 2097152 | tf_op jit(solution)/shard_map/all_to_all | solution.py:550
  58.4 3.7 %broadcast_multiply_fusion = (bf16[32,16,32,16]{3,2,1,0:T(8,128)(2,1)}, bf16[32,16,32,16]{3,2,1,0:T(8,128)(2,1)}) fusion(bf16[32,32]{1,0:T(8,128)(2,1)S(1)} %copy-done.20, bf16[16,16]{1,0:T(8,128)(2,1)S(1)} %fusion, bf16[32,32]{1,0:T(8,128)(2,1)S(1)} %copy.22), kind=kLoop, calls=%fused_computation.1 | loop fusion | flops 524288 | bytes 1053184 | tf_op jit(solution)/shard_map/mul | solution.py:545
  62.1 7.8 %mul.37.local = bf16[512,512]{1,0:T(8,128)(2,1)S(1)} reshape(bf16[32,16,32,16]{3,2,1,0:T(8,128)(2,1)} %get-tuple-element.24) | data formatting | bytes 1048576 | tf_op jit(solution)/shard_map/mul | solution.py:546
  70.0 0.9 broadcast_in_dim_reshape.4.bias
  70.9 13.6 %all-to-all-done.1 = f32[32,2,32,128]{3,2,1,0:T(8,128)S(1)} async-done(((f32[32,2,32,128]{3,2,1,0:T(8,128)}), f32[32,2,32,128]{3,2,1,0:T(8,128)S(1)}, u32[]{:S(2)}, u32[]{:S(2)}) %all-to-all-start.1) | async-done | bytes 1048608 | tf_op jit(solution)/shard_map/all_to_all | solution.py:550
  84.5 0.9 copy-done.6
  85.5 0.9 copy-done.12
  86.4 57.9 %shard_map.175 = (bf16[4,32,64,512]{3,2,1,0:T(8,128)(2,1)}, bf16[4,32,64,512]{3,2,1,0:T(8,128)(2,1)}, f32[2048,128]{1,0:T(8,128)S(1)}, f32[512,512]{1,0:T(8,128)S(1)}, f32[512,128]{1,0:T(8,128)S(1)}) custom-call(f32[2048,128]{1,0:T(8,128)S(1)} %bitcast.15, bf16[4,32,64,512]{3,2,1,0:T(8,128)(2,1)} %field.3, bf16[4,32,64,512]{3,2,1,0:T(8,128)(2,1)} %cotangent.1, ...), custom_call_target="tpu_custom_call" | custom-call | flops 12999999488 | bytes 35651584 | tf_op jit(solution)/shard_map/pallas_call | solution.py:451
  144.3 29.7 %all_to_all.21.received = f32[32,2,32,128]{3,2,1,0:T(8,128)S(1)} all-to-all(f32[32,2,32,128]{3,2,1,0:T(8,128)S(1)} %bitcast.16), channel_id=1, replica_groups=mesh['groups'=1,'gx'=32] {'gx'}, dimensions={0} | all-to-all | bytes 2097152 | tf_op jit(solution)/shard_map/all_to_all | solution.py:550
  174.0 5.7 %shard_map.176 = (f32[32,2,32,128]{3,2,1,0:T(8,128)}, f32[32,32,128]{2,1,0:T(8,128)S(1)}) custom-call(f32[32,2,32,128]{3,2,1,0:T(8,128)S(1)} %all_to_all.21.received, bf16[32,2,32,512]{3,2,1,0:T(8,128)(2,1)S(1)} %copy-done.11, f32[32,64]{1,0:T(8,128)S(1)} %copy-done.16, f32[64,32]{1,0:T(8,128)S(1)} %copy-done.15, f32[16,128]{1,0:T(8,128)S(1)} %copy-done.17, ...), custom_call_target="tpu_custom_call" | custom-call | flops 1000000000 | bytes 5242880 | tf_op jit(solution)/shard_map/pallas_call | solution.py:303
  179.7 3.8 %all-to-all-start.3 = ((f32[32,2,32,128]{3,2,1,0:T(8,128)}), f32[32,2,32,128]{3,2,1,0:T(8,128)S(1)}, u32[]{:S(2)}, u32[]{:S(2)}) async-start(f32[32,2,32,128]{3,2,1,0:T(8,128)} %get-tuple-element.17), calls=%async_computation.3 | async-start | bytes 2097152 | tf_op jit(solution)/shard_map/all_to_all | solution.py:550
  183.5 8.4 %mul.40.local = bf16[512,512]{1,0:T(8,128)(2,1)} reshape(bf16[32,16,32,16]{3,2,1,0:T(8,128)(2,1)} %get-tuple-element.23) | data formatting | bytes 1048576 | tf_op jit(solution)/shard_map/mul | solution.py:545
  192.0 4.9 %reshape.56 = f32[32,16,32,16]{3,2,1,0:T(8,128)} reshape(f32[512,512]{1,0:T(8,128)S(1)} %get-tuple-element.21) | data formatting | bytes 2097152 | tf_op jit(solution)/shard_map/reshape | solution.py:565
  196.9 4.4 %select_reduce_fusion = f32[32,32]{1,0:T(8,128)S(1)} fusion(f32[32,16,32,16]{3,2,1,0:T(8,128)} %reshape.56, pred[16,16]{1,0:T(8,128)(4,1)S(1)} %iota_compare_fusion), kind=kLoop, calls=%fused_computation | loop fusion | flops 523264 | bytes 1052928 | tf_op jit(solution)/shard_map/iyoy->io/reduce_sum | solution.py:565
  201.8 42.3 %all-gather.1 = f32[32,9,128]{2,1,0:T(8,128)S(1)} all-gather(f32[1,9,128]{2,1,0:T(8,128)S(1)} %maximum_bitcast_fusion), channel_id=2, replica_groups=mesh['groups'=1,'gx'=32] {'gx'}, dimensions={0}, use_global_device_ids=true | all-gather | bytes 152064 | tf_op jit(solution)/shard_map/all_gather | solution.py:568
  245.3 3.1 %shard_map.178 = f32[32,2,32,512]{3,2,1,0:T(8,128)} custom-call(f32[32,32,128]{2,1,0:T(8,128)S(1)} %get-tuple-element.19.modes, f32[32,32,128]{2,1,0:T(8,128)S(1)} %get-tuple-element.20.dmodes, f32[16,512]{1,0:T(8,128)S(1)} %copy-done.7), custom_call_target="tpu_custom_call" | custom-call | flops 100000000 | bytes 5242880 | tf_op jit(solution)/shard_map/pallas_call | solution.py:334
  248.4 3.4 %copy-done.19 = bf16[4,32,64,512]{3,2,1,0:T(8,128)(2,1)S(1)} copy-done((bf16[4,32,64,512]{3,2,1,0:T(8,128)(2,1)S(1)}, bf16[4,32,64,512]{3,2,1,0:T(8,128)(2,1)}, u32[]{:S(2)}) %copy-start.19) | copy-done | bytes 8388632
  251.8 14.0 %shard_map.177 = bf16[4,32,64,512]{3,2,1,0:T(8,128)(2,1)} custom-call(f32[2048,128]{1,0:T(8,128)S(1)} %bitcast.14, bf16[4,32,64,512]{3,2,1,0:T(8,128)(2,1)S(1)} %copy-done.19, bf16[512,512]{1,0:T(8,128)(2,1)S(1)} %copy-done.1, bf16[256,512]{1,0:T(8,128)(2,1)S(1)} %copy-done.13, bf16[128,48]{1,0:T(8,128)(2,1)S(1)} %copy-done.14), custom_call_target="tpu_custom_call" | custom-call | flops 6000000000 | bytes 17825792 | tf_op jit(solution)/shard_map/pallas_call | solution.py:516
  (54 shorter events, 2.0 us)
Async XLA Ops:
  0.6 3.4 %copy-start = (bf16[4,32,64,512]{3,2,1,0:T(8,128)(2,1)S(1)}, bf16[4,32,64,512]{3,2,1,0:T(8,128)(2,1)}, u32[]{:S(2)}) copy-start(bf16[4,32,64,512]{3,2,1,0:T(8,128)(2,1)} %field.3) | copy-start | bytes 25165828
  4.0 0.9 copy-start.2
  5.0 0.7 copy-start.8
  5.7 42.2 %copy-start.7 = (f32[16,512]{1,0:T(8,128)S(1)}, f32[16,512]{1,0:T(8,128)}, u32[]{:S(2)}) copy-start(f32[16,512]{1,0:T(8,128)} %constant.25.clone.mask) | copy-start | bytes 98308
  5.7 42.2 %copy-start.10 = (bf16[32,2,32,512]{3,2,1,0:T(8,128)(2,1)S(1)}, bf16[32,2,32,512]{3,2,1,0:T(8,128)(2,1)}, u32[]{:S(2)}) copy-start(bf16[32,2,32,512]{3,2,1,0:T(8,128)(2,1)} %weight.3) | copy-start | bytes 6291460
  5.7 42.2 %copy-start.15 = (f32[64,32]{1,0:T(8,128)S(1)}, f32[64,32]{1,0:T(8,128)}, u32[]{:S(2)}) copy-start(f32[64,32]{1,0:T(8,128)} %constant.27.clone.inverse) | copy-start | bytes 24580
  5.7 42.2 %copy-start.16 = (f32[32,64]{1,0:T(8,128)S(1)}, f32[32,64]{1,0:T(8,128)}, u32[]{:S(2)}) copy-start(f32[32,64]{1,0:T(8,128)} %constant.26.clone.forward) | copy-start | bytes 24580
  5.7 42.2 %copy-start.17 = (f32[16,128]{1,0:T(8,128)S(1)}, f32[16,128]{1,0:T(8,128)}, u32[]{:S(2)}) copy-start(f32[16,128]{1,0:T(8,128)} %constant.28.clone.cosine) | copy-start | bytes 24580
  5.7 42.2 %copy-start.18 = (f32[16,128]{1,0:T(8,128)S(1)}, f32[16,128]{1,0:T(8,128)}, u32[]{:S(2)}) copy-start(f32[16,128]{1,0:T(8,128)} %constant.29.clone.sine) | copy-start | bytes 24580
  14.5 43.8 %copy-start.20 = (bf16[32,32]{1,0:T(8,128)(2,1)S(1)}, bf16[32,32]{1,0:T(8,128)(2,1)}, u32[]{:S(2)}) copy-start(bf16[32,32]{1,0:T(8,128)(2,1)} %param.17) | copy-start | bytes 6148
  54.6 29.9 %all-to-all-start.1 = ((f32[32,2,32,128]{3,2,1,0:T(8,128)}), f32[32,2,32,128]{3,2,1,0:T(8,128)S(1)}, u32[]{:S(2)}, u32[]{:S(2)}) async-start(f32[32,2,32,128]{3,2,1,0:T(8,128)} %get-tuple-element.14), calls=%async_computation.1 | async-start | bytes 2097152 | tf_op jit(solution)/shard_map/all_to_all | solution.py:550
  62.1 7.8 %copy-start.21 = (f32[32]{0:T(128)S(1)}, f32[32]{0:T(128)}, u32[]{:S(2)}) copy-start(f32[32]{0:T(128)} %param.18) | copy-start | bytes 388
  62.1 22.4 %copy-start.3 = (bf16[512,256]{1,0:T(8,128)(2,1)S(1)}, bf16[512,256]{1,0:T(8,128)(2,1)}, u32[]{:S(2)}) copy-start(bf16[512,256]{1,0:T(8,128)(2,1)} %constant.9.clone.zt) | copy-start | bytes 786436
  62.1 22.4 %copy-start.9 = (bf16[32,128]{1,0:T(8,128)(2,1)S(1)}, bf16[32,128]{1,0:T(8,128)(2,1)}, u32[]{:S(2)}) copy-start(bf16[32,128]{1,0:T(8,128)(2,1)} %constant.23.clone.y_table) | copy-start | bytes 24580
  62.1 22.4 %copy-start.14 = (bf16[128,48]{1,0:T(8,128)(2,1)S(1)}, bf16[128,48]{1,0:T(8,128)(2,1)}, u32[]{:S(2)}) copy-start(bf16[128,48]{1,0:T(8,128)(2,1)} %constant.24.clone.y_back) | copy-start | bytes 36868
  84.5 1.0 copy-start.6
  85.5 0.9 copy-start.12
  86.4 87.6 %copy-start.11 = (bf16[32,2,32,512]{3,2,1,0:T(8,128)(2,1)S(1)}, bf16[32,2,32,512]{3,2,1,0:T(8,128)(2,1)}, u32[]{:S(2)}) copy-start(bf16[32,2,32,512]{3,2,1,0:T(8,128)(2,1)} %weight.3) | copy-start | bytes 6291460
  144.3 35.4 %copy-start.4 = (f32[512,128]{1,0:T(8,128)}, f32[512,128]{1,0:T(8,128)S(1)}, u32[]{:S(2)}) copy-start(f32[512,128]{1,0:T(8,128)S(1)} %get-tuple-element.22) | copy-start | bytes 786436
  179.7 68.7 %all-to-all-start.3 = ((f32[32,2,32,128]{3,2,1,0:T(8,128)}), f32[32,2,32,128]{3,2,1,0:T(8,128)S(1)}, u32[]{:S(2)}, u32[]{:S(2)}) async-start(f32[32,2,32,128]{3,2,1,0:T(8,128)} %get-tuple-element.17), calls=%async_computation.3 | async-start | bytes 2097152 | tf_op jit(solution)/shard_map/all_to_all | solution.py:550
  196.9 4.5 %copy-start.5 = (f32[512,128]{1,0:T(8,128)S(1)}, f32[512,128]{1,0:T(8,128)}, u32[]{:S(2)}) copy-start(f32[512,128]{1,0:T(8,128)} %copy-done.4) | copy-start | bytes 786436
  201.2 47.2 %copy-start.1 = (bf16[512,512]{1,0:T(8,128)(2,1)S(1)}, bf16[512,512]{1,0:T(8,128)(2,1)}, u32[]{:S(2)}) copy-start(bf16[512,512]{1,0:T(8,128)(2,1)} %mul.40.local) | copy-start | bytes 1572868
  201.2 47.2 %copy-start.13 = (bf16[256,512]{1,0:T(8,128)(2,1)S(1)}, bf16[256,512]{1,0:T(8,128)(2,1)}, u32[]{:S(2)}) copy-start(bf16[256,512]{1,0:T(8,128)(2,1)} %constant.22.clone.zt_turned) | copy-start | bytes 786436
  248.4 3.4 %copy-start.19 = (bf16[4,32,64,512]{3,2,1,0:T(8,128)(2,1)S(1)}, bf16[4,32,64,512]{3,2,1,0:T(8,128)(2,1)}, u32[]{:S(2)}) copy-start(bf16[4,32,64,512]{3,2,1,0:T(8,128)(2,1)} %get-tuple-element.18.slope) | copy-start | bytes 25165828

commit v2 on v1

--- a/solution.py
+++ b/solution.py
@@ -123,31 +123,32 @@
         out_ref[ky * 2 * Q : (ky + 1) * 2 * Q, :] = gathered[ky * lanes : (ky + 1) * lanes, :].T
 
 
-def forward_kernel(field, zt, y_table, out, gathered, *, lanes, block):
+def forward_kernel(field, zt, y_table, out, gathered, *, lanes, block, group):
     plane, part = pl.program_id(0), pl.program_id(1)
-    sums = dot(field[0].reshape(block * NY, CELLS), zt[...])
-    y_forward(sums, y_table[...], gathered, plane * C + part * block, lanes)
+    for c in range(0, block, group):
+        sums = dot(field[0, c : c + group].reshape(group * NY, CELLS), zt[...])
+        y_forward(sums, y_table[...], gathered, plane * C + part * block + c, lanes)
 
     @pl.when((plane == pl.num_programs(0) - 1) & (part == pl.num_programs(1) - 1))
     def _():
         send_layout(gathered, out, lanes)
 
 
-def forward_planes(field, zt, y_table):
+def forward_planes(field, zt, y_table, block=C, group=16):
     planes = field.shape[0]
-    lanes, block = planes * C, 8
-    return pl.pallas_call(
-        functools.partial(forward_kernel, lanes=lanes, block=block),
+    lanes = planes * C
+    return pl.pallas_call(
+        functools.partial(forward_kernel, lanes=lanes, block=block, group=group),
         grid=(planes, C // block),
         in_specs=[
             pl.BlockSpec((1, block, NY, CELLS), lambda x, c: (x, c, 0, 0)),
-            pl.BlockSpec(zt.shape, lambda x, c: (0, 0)),
-            pl.BlockSpec(y_table.shape, lambda x, c: (0, 0)),
+            whole(zt),
+            whole(y_table),
         ],
         out_specs=pl.BlockSpec((KY * 2 * Q, lanes), lambda x, c: (0, 0)),
         out_shape=jax.ShapeDtypeStruct((KY * 2 * Q, lanes), F32),
         scratch_shapes=[pltpu.VMEM((KY * lanes, 2 * Q), F32)],
-        compiler_params=pltpu.CompilerParams(vmem_limit_bytes=32 * MIB),
+        compiler_params=pltpu.CompilerParams(vmem_limit_bytes=56 * MIB),
         cost_estimate=pl.CostEstimate(flops=2 * 10**9, bytes_accessed=9 * MIB, transcendentals=0),
     )(field, zt, y_table)
 
@@ -347,9 +348,10 @@
         gathered[ky * lanes : (ky + 1) * lanes, :] = back[ky * 2 * Q : (ky + 1) * 2 * Q, :].T
 
 
-def y_inverse(gathered, y_table, inverse_y, plane, lanes):
-    for c in range(0, C, 2):
-        row = plane * C + c
+def y_inverse(gathered, y_table, first_row, count, lanes):
+    found = []
+    for c in range(0, count, 2):
+        row = first_row + c
         pair = jnp.concatenate(
             [
                 gathered[pl.ds(row, KY, stride=lanes), :],
@@ -361,16 +363,33 @@
         both = dot(y_table, jnp.concatenate([high, low, high], axis=0)).astype(BF16)
         for k in range(2):
             columns = slice(k * 2 * Q, (k + 1) * 2 * Q)
-            inverse_y[c + k, :, : 2 * Q] = both[:NY, columns]
-            inverse_y[c + k, :, 2 * Q :] = both[NY:, columns]
+            found.append(jnp.concatenate([both[:NY, columns], both[NY:, columns]], axis=1))
+    return jnp.concatenate(found, axis=0)
+
+
+def local_kernel(field, local, bias, out):
+    rows = C * YB
+    total = dot(local[...], field[0].reshape(rows, CELLS)) + bias[...]
+    out[0] = total.astype(BF16).reshape(C, YB, CELLS)
+
+
+def local_term(field, local, bias):
+    block = pl.BlockSpec((1, C, YB, CELLS), lambda x, y: (x, 0, y, 0))
+    return pl.pallas_call(
+        local_kernel,
+        grid=(field.shape[0], NY // YB),
+        in_specs=[block, whole(local), whole(bias)],
+        out_specs=block,
+        out_shape=jax.ShapeDtypeStruct(field.shape, BF16),
+        compiler_params=pltpu.CompilerParams(vmem_limit_bytes=32 * MIB),
+        cost_estimate=pl.CostEstimate(flops=8 * 10**9, bytes_accessed=25 * MIB, transcendentals=0),
+    )(field, local, bias)
 
 
 def middle_kernel(
     back,
-    field,
+    early,
     cotangent,
-    local,
-    bias,
     zt,
     zt_turned,
     y_back,
@@ -378,156 +397,153 @@
     out,
     slope_out,
     spectra,
-    local_grad,
     bias_grad,
     gathered,
-    inverse_y,
-    pre,
-    sums,
     collected,
     *,
     lanes,
+    block,
+    group,
 ):
     plane, part = pl.program_id(0), pl.program_id(1)
-    rows = C * YB
     first_step = (plane == 0) & (part == 0)
     last_step = (plane == pl.num_programs(0) - 1) & (part == pl.num_programs(1) - 1)
 
     @pl.when(first_step)
     def _():
         planes_layout(back, gathered, lanes)
-        local_grad[...] = jnp.zeros_like(local_grad)
         bias_grad[...] = jnp.zeros_like(bias_grad)
 
-    @pl.when(part == 0)
-    def _():
-        y_inverse(gathered, y_back[...], inverse_y, plane, lanes)
-
-    y_rows = pl.ds(pl.multiple_of(part * YB, YB), YB)
-    values = field[0].reshape(rows, CELLS)
-    own = inverse_y[:, y_rows, :].reshape(rows, 4 * Q)
-    pre[...] = dot(local[...], values) + dot(own, zt_turned[...])
-
-    chunk = 2
     half_root = 1.0 / math.sqrt(2.0)
-
-    def pointwise(step, _):
-        c = step * chunk
-        r = pl.ds(pl.multiple_of(c * YB, chunk * YB), chunk * YB)
-        v = pre[r, :] + bias[r, :]
-        grade = cotangent[0, pl.ds(c, chunk)].reshape(chunk * YB, CELLS).astype(F32)
-        normal = 0.5 + 0.5 * lax.erf(v * half_root)
-        result = v * normal
-        slope = grade * (normal + v * (jnp.exp(-0.5 * v * v) * (1.0 / math.sqrt(2.0 * math.pi))))
-        out[0, pl.ds(c, chunk)] = result.astype(BF16).reshape(chunk, YB, CELLS)
-        slope_out[0, pl.ds(c, chunk)] = slope.astype(BF16).reshape(chunk, YB, CELLS)
-        folded = slope[:, :128]
-        for column in range(128, CELLS, 128):
-            folded = folded + slope[:, column : column + 128]
-        bias_grad[r, :] += folded
-        return 0
-
-    lax.fori_loop(0, C // chunk, pointwise, 0, unroll=False)
-
-    low = slope_out[0].reshape(rows, CELLS)
-    sums[:, y_rows, :] = dot(low, zt[...]).reshape(C, YB, 4 * Q)
-    local_grad[...] += lax.dot_general(
-        values, low, (((1,), (1,)), ((), ())), preferred_element_type=F32
-    )
-
-    @pl.when(part == pl.num_programs(1) - 1)
-    def _():
-        y_forward(sums.reshape(C * NY, 4 * Q), y_table[...], collected, plane * C, lanes)
+    for g in range(0, block, group):
+        first_row = plane * C + part * block + g
+        own = y_inverse(gathered, y_back[...], first_row, group, lanes)
+        pre = dot(own, zt_turned[...])
+        low = []
+        for c in range(group):
+            v = pre[c * NY : (c + 1) * NY] + early[0, g + c].astype(F32)
+            grade = cotangent[0, g + c].astype(F32)
+            normal = 0.5 + 0.5 * lax.erf(v * half_root)
+            out[0, g + c] = (v * normal).astype(BF16)
+            bell = jnp.exp(-0.5 * v * v) * (1.0 / math.sqrt(2.0 * math.pi))
+            slope = grade * (normal + v * bell)
+            low.append(slope.astype(BF16))
+            slope_out[0, g + c] = low[-1]
+            folded = slope[:, :128]
+            for column in range(128, CELLS, 128):
+                folded = folded + slope[:, column : column + 128]
+            total = folded[:8]
+            for row in range(8, NY, 8):
+                total = total + folded[row : row + 8]
+            r = pl.ds(pl.multiple_of((part * block + g + c) * 8, 8), 8)
+            bias_grad[r, :] += total
+        sums = dot(jnp.concatenate(low, axis=0), zt[...])
+        y_forward(sums, y_table[...], collected, first_row, lanes)
 
     @pl.when(last_step)
     def _():
         send_layout(collected, spectra, lanes)
 
 
-def middle(back, field, cotangent, local, bias, zt, zt_turned, y_back, y_table):
-    planes = field.shape[0]
-    lanes, rows = planes * C, C * YB
-    block = pl.BlockSpec((1, C, YB, CELLS), lambda x, y: (x, 0, y, 0))
-    return pl.pallas_call(
-        functools.partial(middle_kernel, lanes=lanes),
-        grid=(planes, NY // YB),
+def middle(back, early, cotangent, zt, zt_turned, y_back, y_table, block=C, group=16):
+    planes = cotangent.shape[0]
+    lanes = planes * C
+    spec = pl.BlockSpec((1, block, NY, CELLS), lambda x, c: (x, c, 0, 0))
+    return pl.pallas_call(
+        functools.partial(middle_kernel, lanes=lanes, block=block, group=group),
+        grid=(planes, C // block),
         in_specs=[
             whole(back),
-            block,
-            block,
-            whole(local),
-            whole(bias),
+            spec,
+            spec,
             whole(zt),
             whole(zt_turned),
             whole(y_back),
             whole(y_table),
         ],
         out_specs=[
-            block,
-            block,
-            pl.BlockSpec((KY * 2 * Q, lanes), lambda x, y: (0, 0)),
-            pl.BlockSpec((rows, rows), lambda x, y: (0, 0)),
-            pl.BlockSpec((rows, 128), lambda x, y: (0, 0)),
-        ],
+            spec,
+            spec,
+            pl.BlockSpec((KY * 2 * Q, lanes), lambda x, c: (0, 0)),
+            pl.BlockSpec((C * 8, 128), lambda x, c: (0, 0)),
+        ],
+        out_shape=[
+            jax.ShapeDtypeStruct(cotangent.shape, BF16),
+            jax.ShapeDtypeStruct(cotangent.shape, BF16),
+            jax.ShapeDtypeStruct((KY * 2 * Q, lanes), F32),
+            jax.ShapeDtypeStruct((C * 8, 128), F32),
+        ],
+        scratch_shapes=[
+            pltpu.VMEM((KY * lanes, 2 * Q), F32),
+            pltpu.VMEM((KY * lanes, 2 * Q), F32),
+        ],
+        compiler_params=pltpu.CompilerParams(vmem_limit_bytes=56 * MIB),
+        cost_estimate=pl.CostEstimate(
+            flops=5 * 10**9, bytes_accessed=42 * MIB, transcendentals=8 * 10**6
+        ),
+    )(back, early, cotangent, zt, zt_turned, y_back, y_table)
+
+
+def late_kernel(field, slope, local, out, local_grad):
+    rows = C * YB
+
+    @pl.when((pl.program_id(0) == 0) & (pl.program_id(1) == 0))
+    def _():
+        local_grad[...] = jnp.zeros_like(local_grad)
+
+    values, low = field[0].reshape(rows, CELLS), slope[0].reshape(rows, CELLS)
+    out[0] = dot(local[...], low).astype(BF16).reshape(C, YB, CELLS)
+    local_grad[...] += lax.dot_general(
+        values, low, (((1,), (1,)), ((), ())), preferred_element_type=F32
+    )
+
+
+def late_terms(field, slope, local):
+    block = pl.BlockSpec((1, C, YB, CELLS), lambda x, y: (x, 0, y, 0))
+    rows = C * YB
+    return pl.pallas_call(
+        late_kernel,
+        grid=(field.shape[0], NY // YB),
+        in_specs=[block, block, whole(local)],
+        out_specs=[block, pl.BlockSpec((rows, rows), lambda x, y: (0, 0))],
         out_shape=[
             jax.ShapeDtypeStruct(field.shape, BF16),
-            jax.ShapeDtypeStruct(field.shape, BF16),
-            jax.ShapeDtypeStruct((KY * 2 * Q, lanes), F32),
             jax.ShapeDtypeStruct((rows, rows), F32),
-            jax.ShapeDtypeStruct((rows, 128), F32),
-        ],
-        scratch_shapes=[
-            pltpu.VMEM((KY * lanes, 2 * Q), F32),
-            pltpu.VMEM((C, NY, 4 * Q), BF16),
-            pltpu.VMEM((rows, CELLS), F32),
-            pltpu.VMEM((C, NY, 4 * Q), F32),
-            pltpu.VMEM((KY * lanes, 2 * Q), F32),
-        ],
-        compiler_params=pltpu.CompilerParams(vmem_limit_bytes=48 * MIB),
-        cost_estimate=pl.CostEstimate(
-            flops=13 * 10**9, bytes_accessed=34 * MIB, transcendentals=8 * 10**6
-        ),
-    )(back, field, cotangent, local, bias, zt, zt_turned, y_back, y_table)
-
-
-def last_kernel(back, slope, local, zt_turned, y_back, out, gathered, inverse_y, *, lanes):
+        ],
+        compiler_params=pltpu.CompilerParams(vmem_limit_bytes=32 * MIB),
+        cost_estimate=pl.CostEstimate(flops=12 * 10**9, bytes_accessed=25 * MIB, transcendentals=0),
+    )(field, slope, local)
+
+
+def last_kernel(back, early, zt_turned, y_back, out, gathered, *, lanes, block, group):
     plane, part = pl.program_id(0), pl.program_id(1)
-    rows = C * YB
 
     @pl.when((plane == 0) & (part == 0))
     def _():
         planes_layout(back, gathered, lanes)
 
-    @pl.when(part == 0)
-    def _():
-        y_inverse(gathered, y_back[...], inverse_y, plane, lanes)
-
-    y_rows = pl.ds(pl.multiple_of(part * YB, YB), YB)
-    low = slope[0].reshape(rows, CELLS)
-    own = inverse_y[:, y_rows, :].reshape(rows, 4 * Q)
-    total = dot(local[...], low) + dot(own, zt_turned[...])
-    out[0] = total.astype(BF16).reshape(C, YB, CELLS)
-
-
-def last(back, slope, local, zt_turned, y_back):
-    planes = slope.shape[0]
+    for g in range(0, block, group):
+        own = y_inverse(gathered, y_back[...], plane * C + part * block + g, group, lanes)
+        total = dot(own, zt_turned[...]).reshape(group, NY, CELLS)
+        out[0, g : g + group] = (total + early[0, g : g + group].astype(F32)).astype(BF16)
+
+
+def last(back, early, zt_turned, y_back, block=C, group=16):
+    planes = early.shape[0]
     lanes = planes * C
-    block = pl.BlockSpec((1, C, YB, CELLS), lambda x, y: (x, 0, y, 0))
-    return pl.pallas_call(
-        functools.partial(last_kernel, lanes=lanes),
-        grid=(planes, NY // YB),
-        in_specs=[whole(back), block, whole(local), whole(zt_turned), whole(y_back)],
-        out_specs=block,
-        out_shape=jax.ShapeDtypeStruct(slope.shape, BF16),
-        scratch_shapes=[
-            pltpu.VMEM((KY * lanes, 2 * Q), F32),
-            pltpu.VMEM((C, NY, 4 * Q), BF16),
-        ],
-        compiler_params=pltpu.CompilerParams(vmem_limit_bytes=32 * MIB),
+    spec = pl.BlockSpec((1, block, NY, CELLS), lambda x, c: (x, c, 0, 0))
+    return pl.pallas_call(
+        functools.partial(last_kernel, lanes=lanes, block=block, group=group),
+        grid=(planes, C // block),
+        in_specs=[whole(back), spec, whole(zt_turned), whole(y_back)],
+        out_specs=spec,
+        out_shape=jax.ShapeDtypeStruct(early.shape, BF16),
+        scratch_shapes=[pltpu.VMEM((KY * lanes, 2 * Q), F32)],
+        compiler_params=pltpu.CompilerParams(vmem_limit_bytes=56 * MIB),
         cost_estimate=pl.CostEstimate(
-            flops=6 * 10**9, bytes_accessed=17 * MIB, transcendentals=0
+            flops=2 * 10**9, bytes_accessed=17 * MIB, transcendentals=0
         ),
-    )(back, slope, local, zt_turned, y_back)
+    )(back, early, zt_turned, y_back)
 
 
 def on_device(hidden_field, cotangent, spectral_weight, local_weight, local_bias):
@@ -556,19 +572,22 @@
         return exchange(back).reshape(KY * 2 * Q, lanes)
 
     spectra = forward_planes(hidden_field, zt, y_table)
+    early = local_term(hidden_field, local_here, bias)
     back, modes = mix_modes(to_owner(spectra), spectral_weight, tables)
-    output, slope, dspectra, local_part, bias_part = middle(
-        to_slabs(back), hidden_field, cotangent, local_here, bias, zt, zt_turned, y_back, y_table
+    output, slope, dspectra, bias_part = middle(
+        to_slabs(back), early, cotangent, zt, zt_turned, y_back, y_table
     )
+    late, local_part = late_terms(hidden_field, slope, local_back)
     dback, dmodes = adjoint_modes(to_owner(dspectra), spectral_weight, tables)
     grad_spectral = mode_gradient(modes, dmodes, mask)
     local_sum = jnp.einsum("iyoy->io", local_part.reshape(C, YB, C, YB))
-    bias_sum = jnp.sum(bias_part.reshape(C, YB * 128), axis=1)
+    bias_sum = jnp.sum(bias_part.reshape(C, 8 * 128), axis=1)
     partial = jnp.concatenate([local_sum.reshape(C * C // 128, 128), jnp.tile(bias_sum, 4)[None]])
-    total = jnp.sum(lax.all_gather(partial, "gx"), axis=0)
+    copies = jnp.broadcast_to(partial, (devices,) + partial.shape)
+    total = jnp.sum(exchange(copies), axis=0)
     grad_local = total[: C * C // 128].reshape(C, C)
     grad_bias = total[C * C // 128, :C]
-    grad_field = last(to_slabs(dback), slope, local_back, zt_turned, y_back)
+    grad_field = last(to_slabs(dback), late, zt_turned, y_back)
     return (output, grad_field, grad_spectral, grad_local, grad_bias)
 
 

time: 266 us -> 207 us (0.78)
  blocking collectives: 105 us -> 33.5 us
  Pallas kernels: 96.3 us -> 79.1 us
  waiting for transfers between devices: 13.6 us -> 25.2 us
  starting transfers between devices: 7.42 us -> 18 us
  local copies, waits for them, and re-layouts: 33.9 us -> 39.9 us
    all_gather x1 -> x0, blocking collectives: 42.3 us -> none  [on_device(): total = jnp.sum(lax.all_gather(partial, 'gx'), axis=0)]
    all_to_all x2 -> x1, blocking collectives: 63 us -> 33.5 us  [exchange(): return lax.all_to_all(value, 'gx', split_axis=0, concat_axis=0, tiled=True)]
    pallas_call x2 -> x4, Pallas kernels: 71.9 us -> 54.2 us  [the longest x1 20.2 us: middle(): pl.pallas_call(functools.partial(middle_kernel, lanes=lanes, block=block,...]
    all_to_all x2 -> x4, waiting for transfers between devices: 13.6 us -> 25.2 us  [exchange(): return lax.all_to_all(value, 'gx', split_axis=0, concat_axis=0, tiled=True)]
    all_to_all x2 -> x4, starting transfers between devices: 7.42 us -> 18 us  [exchange(): return lax.all_to_all(value, 'gx', split_axis=0, concat_axis=0, tiled=True)]
    unnamed x44 -> x30, local copies, waits for them, and re-layouts: 10.4 us -> 17.1 us
  transfers between devices with their start and end apart: 2 -> 4, of which waited for: 1 -> 2; matrix products, arithmetic and copies ran while one was open for 12% -> 15% of each run, Pallas kernels for 1% -> 16%
where the time goes in v2:
time: 207 us; the launch traced here: 206 us
  Pallas kernels  79.1 us (38%)
  local copies, waits for them, and re-layouts  39.9 us (19%)
  blocking collectives  33.5 us (16%)
  waiting for transfers between devices  25.2 us (12%)
  starting transfers between devices  18 us (9%)
  other arithmetic  9.23 us (4%)
    all_to_all x1, blocking collectives, exchange(): return lax.all_to_all(value, 'gx', split_axis=0, concat_axis=0, tiled=True)  33.5 us
    all_to_all x4, waiting for transfers between devices, exchange(): return lax.all_to_all(value, 'gx', split_axis=0, concat_axis=0, tiled=True)  25.2 us
    pallas_call x1, Pallas kernels, middle(): pl.pallas_call(functools.partial(middle_kernel, lanes=lanes, block=block,...  20.2 us
    all_to_all x4, starting transfers between devices, exchange(): return lax.all_to_all(value, 'gx', split_axis=0, concat_axis=0, tiled=True)  18 us
    unnamed x30, local copies, waits for them, and re-layouts  17.1 us
    pallas_call x1, Pallas kernels, late_terms(): pl.pallas_call(late_kernel, grid=(field.shape[0], NY // YB), in_specs=[bl...  15.9 us
    pallas_call x1, Pallas kernels, last(): pl.pallas_call(functools.partial(last_kernel, lanes=lanes, block=block, g...  9.72 us
    pallas_call x1, Pallas kernels, forward_planes(): pl.pallas_call(functools.partial(forward_kernel, lanes=lanes, block=block...  9.36 us
  transfers between devices with their start and end apart: 4, of which 2 were waited for; matrix products, arithmetic and copies ran while one was open for 15% of the time, Pallas kernels for 16%

profile of v2, /device:TPU:0, one launch (start us, length us, event | category | flops | bytes accessed | tf_op | source)
XLA Modules:
  0.0 205.8 jit_solution(6392551737390996053)
XLA Ops:
  0.7 9.4 %shard_map.173 = f32[2048,128]{1,0:T(8,128)} custom-call(bf16[4,32,64,512]{3,2,1,0:T(8,128)(2,1)} %field.5, bf16[512,256]{1,0:T(8,128)(2,1)} %constant.9.clone.zt, bf16[32,128]{1,0:T(8,128)(2,1)} %constant.23.clone.y_table), custom_call_target="tpu_custom_call" | custom-call | flops 2000000000 | bytes 9437184 | tf_op jit(solution)/shard_map/pallas_call | solution.py:140
  10.1 33.5 %all_to_all.25.received = f32[32,2,32,128]{3,2,1,0:T(8,128)S(1)} all-to-all(f32[32,2,32,128]{3,2,1,0:T(8,128)} %bitcast.12), channel_id=1, replica_groups=mesh['groups'=1,'gx'=32] {'gx'}, dimensions={0} | all-to-all | bytes 2097152 | tf_op jit(solution)/shard_map/all_to_all | solution.py:566
  43.7 6.8 %shard_map.174 = (f32[32,2,32,128]{3,2,1,0:T(8,128)}, f32[32,32,128]{2,1,0:T(8,128)S(1)}) custom-call(f32[32,2,32,128]{3,2,1,0:T(8,128)S(1)} %all_to_all.25.received, bf16[32,2,32,512]{3,2,1,0:T(8,128)(2,1)S(1)} %copy-done.4, f32[32,64]{1,0:T(8,128)S(1)} %copy-done.7, f32[64,32]{1,0:T(8,128)S(1)} %copy-done.6, f32[16,128]{1,0:T(8,128)S(1)} %copy-done.9, ...), custom_call_target="tpu_custom_call" | custom-call | flops 1000000000 | bytes 5242880 | tf_op jit(solution)/shard_map/pallas_call | solution.py:249
  50.4 3.6 %all-to-all-start.1 = ((f32[32,2,32,128]{3,2,1,0:T(8,128)}), f32[32,2,32,128]{3,2,1,0:T(8,128)S(1)}, u32[]{:S(2)}, u32[]{:S(2)}) async-start(f32[32,2,32,128]{3,2,1,0:T(8,128)} %get-tuple-element.15), calls=%async_computation.1 | async-start | bytes 2097152 | tf_op jit(solution)/shard_map/all_to_all | solution.py:566
  54.4 3.7 %broadcast_multiply_fusion = (bf16[32,16,32,16]{3,2,1,0:T(8,128)(2,1)}, bf16[32,16,32,16]{3,2,1,0:T(8,128)(2,1)}) fusion(bf16[32,32]{1,0:T(8,128)(2,1)S(1)} %copy-done.13, bf16[16,16]{1,0:T(8,128)(2,1)S(1)} %fusion, bf16[32,32]{1,0:T(8,128)(2,1)S(1)} %copy.24), kind=kLoop, calls=%fused_computation.1 | loop fusion | flops 524288 | bytes 1053184 | tf_op jit(solution)/shard_map/mul | solution.py:561
  58.1 7.8 %mul.37.local = bf16[512,512]{1,0:T(8,128)(2,1)S(1)} reshape(bf16[32,16,32,16]{3,2,1,0:T(8,128)(2,1)} %get-tuple-element.26) | data formatting | bytes 1048576 | tf_op jit(solution)/shard_map/mul | solution.py:562
  65.9 3.4 %copy-done = bf16[4,32,64,512]{3,2,1,0:T(8,128)(2,1)S(1)} copy-done((bf16[4,32,64,512]{3,2,1,0:T(8,128)(2,1)S(1)}, bf16[4,32,64,512]{3,2,1,0:T(8,128)(2,1)}, u32[]{:S(2)}) %copy-start) | copy-done | bytes 8388632
  69.3 8.3 %shard_map.175.early = bf16[4,32,64,512]{3,2,1,0:T(8,128)(2,1)S(1)} custom-call(bf16[4,32,64,512]{3,2,1,0:T(8,128)(2,1)S(1)} %copy-done, bf16[512,512]{1,0:T(8,128)(2,1)S(1)} %mul.37.local, f32[512,1]{1,0:T(8,128)S(1)} %broadcast_in_dim_reshape.4.bias), custom_call_target="tpu_custom_call" | custom-call | flops 8000000000 | bytes 26214400 | tf_op jit(solution)/shard_map/pallas_call | solution.py:378
  77.6 3.4 %copy-done.10 = bf16[4,32,64,512]{3,2,1,0:T(8,128)(2,1)} copy-done((bf16[4,32,64,512]{3,2,1,0:T(8,128)(2,1)}, bf16[4,32,64,512]{3,2,1,0:T(8,128)(2,1)S(1)}, u32[]{:S(2)}) %copy-start.10) | copy-done | bytes 8388632
  82.0 20.2 %shard_map.176 = (bf16[4,32,64,512]{3,2,1,0:T(8,128)(2,1)}, bf16[4,32,64,512]{3,2,1,0:T(8,128)(2,1)}, f32[2048,128]{1,0:T(8,128)}, f32[256,128]{1,0:T(8,128)}) custom-call(f32[2048,128]{1,0:T(8,128)} %bitcast.14, bf16[4,32,64,512]{3,2,1,0:T(8,128)(2,1)} %copy-done.10, bf16[4,32,64,512]{3,2,1,0:T(8,128)(2,1)} %cotangent.1, ...), custom_call_target="tpu_custom_call" | custom-call | flops 5000000000 | bytes 44040192 | tf_op jit(solution)/shard_map/pallas_call | solution.py:452
  102.2 6.0 %all-to-all-start.2 = ((f32[32,2,32,128]{3,2,1,0:T(8,128)}), f32[32,2,32,128]{3,2,1,0:T(8,128)S(1)}, u32[]{:S(2)}, u32[]{:S(2)}) async-start(f32[32,2,32,128]{3,2,1,0:T(8,128)} %bitcast.13), calls=%async_computation.2 | async-start | bytes 2097152 | tf_op jit(solution)/shard_map/all_to_all | solution.py:566
  108.3 7.8 %mul.40.local = bf16[512,512]{1,0:T(8,128)(2,1)S(1)} reshape(bf16[32,16,32,16]{3,2,1,0:T(8,128)(2,1)} %get-tuple-element.25) | data formatting | bytes 1048576 | tf_op jit(solution)/shard_map/mul | solution.py:561
  117.4 3.4 %copy-done.1 = bf16[4,32,64,512]{3,2,1,0:T(8,128)(2,1)S(1)} copy-done((bf16[4,32,64,512]{3,2,1,0:T(8,128)(2,1)S(1)}, bf16[4,32,64,512]{3,2,1,0:T(8,128)(2,1)}, u32[]{:S(2)}) %copy-start.1) | copy-done | bytes 8388632
  120.8 15.9 %shard_map.178 = (bf16[4,32,64,512]{3,2,1,0:T(8,128)(2,1)S(1)}, f32[512,512]{1,0:T(8,128)S(1)}) custom-call(bf16[4,32,64,512]{3,2,1,0:T(8,128)(2,1)S(1)} %copy-done.1, bf16[4,32,64,512]{3,2,1,0:T(8,128)(2,1)} %get-tuple-element.19.slope, bf16[512,512]{1,0:T(8,128)(2,1)S(1)} %mul.40.local), custom_call_target="tpu_custom_call" | custom-call | flops 12000000000 | bytes 26214400 | tf_op jit(solution)/shard_map/pallas_call | solution.py:504
  136.7 3.2 %copy-done.2 = bf16[4,32,64,512]{3,2,1,0:T(8,128)(2,1)} copy-done((bf16[4,32,64,512]{3,2,1,0:T(8,128)(2,1)}, bf16[4,32,64,512]{3,2,1,0:T(8,128)(2,1)S(1)}, u32[]{:S(2)}) %copy-start.2) | copy-done | bytes 8388632
  139.9 4.8 %reshape.56 = f32[32,16,32,16]{3,2,1,0:T(8,128)} reshape(f32[512,512]{1,0:T(8,128)S(1)} %get-tuple-element.23) | data formatting | bytes 2097152 | tf_op jit(solution)/shard_map/reshape | solution.py:583
  144.7 4.3 %select_reduce_fusion = f32[32,32]{1,0:T(8,128)S(1)} fusion(f32[32,16,32,16]{3,2,1,0:T(8,128)} %reshape.56, pred[16,16]{1,0:T(8,128)(4,1)S(1)} %iota_compare_fusion), kind=kLoop, calls=%fused_computation | loop fusion | flops 523264 | bytes 1052928 | tf_op jit(solution)/shard_map/iyoy->io/reduce_sum | solution.py:583
  149.8 5.7 %all-to-all-start.4 = ((f32[32,9,128]{2,1,0:T(8,128)}), f32[32,9,128]{2,1,0:T(8,128)S(1)}, u32[]{:S(2)}, u32[]{:S(2)}) async-start(f32[32,9,128]{2,1,0:T(8,128)} %broadcast_in_dim.19), calls=%async_computation.4 | async-start | bytes 524288 | tf_op jit(solution)/shard_map/all_to_all | solution.py:566
  157.1 5.7 %shard_map.177 = (f32[32,2,32,128]{3,2,1,0:T(8,128)}, f32[32,32,128]{2,1,0:T(8,128)S(1)}) custom-call(f32[32,2,32,128]{3,2,1,0:T(8,128)S(1)} %all-to-all-done.2.received, bf16[32,2,32,512]{3,2,1,0:T(8,128)(2,1)S(1)} %copy-done.5, f32[32,64]{1,0:T(8,128)S(1)} %copy-done.7, f32[64,32]{1,0:T(8,128)S(1)} %copy-done.6, f32[16,128]{1,0:T(8,128)S(1)} %copy-done.9, ...), custom_call_target="tpu_custom_call" | custom-call | flops 1000000000 | bytes 5242880 | tf_op jit(solution)/shard_map/pallas_call | solution.py:304
  162.8 3.3 %all-to-all-done.4 = f32[32,9,128]{2,1,0:T(8,128)S(1)} async-done(((f32[32,9,128]{2,1,0:T(8,128)}), f32[32,9,128]{2,1,0:T(8,128)S(1)}, u32[]{:S(2)}, u32[]{:S(2)}) %all-to-all-start.4) | async-done | bytes 147488 | tf_op jit(solution)/shard_map/all_to_all | solution.py:566
  166.1 2.6 %all-to-all-start.3 = ((f32[32,2,32,128]{3,2,1,0:T(8,128)}), f32[32,2,32,128]{3,2,1,0:T(8,128)S(1)}, u32[]{:S(2)}, u32[]{:S(2)}) async-start(f32[32,2,32,128]{3,2,1,0:T(8,128)} %get-tuple-element.18), calls=%async_computation.3 | async-start | bytes 2097152 | tf_op jit(solution)/shard_map/all_to_all | solution.py:566
  170.0 3.1 %shard_map.180 = f32[32,2,32,512]{3,2,1,0:T(8,128)} custom-call(f32[32,32,128]{2,1,0:T(8,128)S(1)} %get-tuple-element.21.modes, f32[32,32,128]{2,1,0:T(8,128)S(1)} %get-tuple-element.22.dmodes, f32[16,512]{1,0:T(8,128)S(1)} %copy-done.3), custom_call_target="tpu_custom_call" | custom-call | flops 100000000 | bytes 5242880 | tf_op jit(solution)/shard_map/pallas_call | solution.py:335
  173.1 21.8 %all-to-all-done.3 = f32[32,2,32,128]{3,2,1,0:T(8,128)S(1)} async-done(((f32[32,2,32,128]{3,2,1,0:T(8,128)}), f32[32,2,32,128]{3,2,1,0:T(8,128)S(1)}, u32[]{:S(2)}, u32[]{:S(2)}) %all-to-all-start.3) | async-done | bytes 1048608 | tf_op jit(solution)/shard_map/all_to_all | solution.py:566
  196.0 9.7 %shard_map.179 = bf16[4,32,64,512]{3,2,1,0:T(8,128)(2,1)} custom-call(f32[2048,128]{1,0:T(8,128)} %bitcast.11, bf16[4,32,64,512]{3,2,1,0:T(8,128)(2,1)} %copy-done.2, bf16[256,512]{1,0:T(8,128)(2,1)} %constant.22.clone.zt_turned, bf16[128,48]{1,0:T(8,128)(2,1)} %constant.24.clone.y_back), custom_call_target="tpu_custom_call" | custom-call | flops 2000000000 | bytes 17825792 | tf_op jit(solution)/shard_map/pallas_call | solution.py:535
  (45 shorter events, 7.4 us)
Async XLA Ops:
  0.6 43.0 %copy-start.3 = (f32[16,512]{1,0:T(8,128)S(1)}, f32[16,512]{1,0:T(8,128)}, u32[]{:S(2)}) copy-start(f32[16,512]{1,0:T(8,128)} %constant.25.clone.mask) | copy-start | bytes 98308
  0.6 43.0 %copy-start.8 = (f32[16,128]{1,0:T(8,128)S(1)}, f32[16,128]{1,0:T(8,128)}, u32[]{:S(2)}) copy-start(f32[16,128]{1,0:T(8,128)} %constant.29.clone.sine) | copy-start | bytes 24580
  0.7 43.0 %copy-start.9 = (f32[16,128]{1,0:T(8,128)S(1)}, f32[16,128]{1,0:T(8,128)}, u32[]{:S(2)}) copy-start(f32[16,128]{1,0:T(8,128)} %constant.28.clone.cosine) | copy-start | bytes 24580
  0.7 43.0 %copy-start.6 = (f32[64,32]{1,0:T(8,128)S(1)}, f32[64,32]{1,0:T(8,128)}, u32[]{:S(2)}) copy-start(f32[64,32]{1,0:T(8,128)} %constant.27.clone.inverse) | copy-start | bytes 24580
  0.7 43.0 %copy-start.7 = (f32[32,64]{1,0:T(8,128)S(1)}, f32[32,64]{1,0:T(8,128)}, u32[]{:S(2)}) copy-start(f32[32,64]{1,0:T(8,128)} %constant.26.clone.forward) | copy-start | bytes 24580
  0.7 43.0 %copy-start.4 = (bf16[32,2,32,512]{3,2,1,0:T(8,128)(2,1)S(1)}, bf16[32,2,32,512]{3,2,1,0:T(8,128)(2,1)}, u32[]{:S(2)}) copy-start(bf16[32,2,32,512]{3,2,1,0:T(8,128)(2,1)} %weight.3) | copy-start | bytes 6291460
  0.7 53.4 %copy-start.13 = (bf16[32,32]{1,0:T(8,128)(2,1)S(1)}, bf16[32,32]{1,0:T(8,128)(2,1)}, u32[]{:S(2)}) copy-start(bf16[32,32]{1,0:T(8,128)(2,1)} %param.17) | copy-start | bytes 6148
  0.7 53.4 %copy-start.14 = (f32[32]{0:T(128)S(1)}, f32[32]{0:T(128)}, u32[]{:S(2)}) copy-start(f32[32]{0:T(128)} %param.18) | copy-start | bytes 388
  50.4 30.6 %all-to-all-start.1 = ((f32[32,2,32,128]{3,2,1,0:T(8,128)}), f32[32,2,32,128]{3,2,1,0:T(8,128)S(1)}, u32[]{:S(2)}, u32[]{:S(2)}) async-start(f32[32,2,32,128]{3,2,1,0:T(8,128)} %get-tuple-element.15), calls=%async_computation.1 | async-start | bytes 2097152 | tf_op jit(solution)/shard_map/all_to_all | solution.py:566
  65.9 3.4 %copy-start = (bf16[4,32,64,512]{3,2,1,0:T(8,128)(2,1)S(1)}, bf16[4,32,64,512]{3,2,1,0:T(8,128)(2,1)}, u32[]{:S(2)}) copy-start(bf16[4,32,64,512]{3,2,1,0:T(8,128)(2,1)} %field.5) | copy-start | bytes 25165828
  77.6 3.4 %copy-start.10 = (bf16[4,32,64,512]{3,2,1,0:T(8,128)(2,1)}, bf16[4,32,64,512]{3,2,1,0:T(8,128)(2,1)S(1)}, u32[]{:S(2)}) copy-start(bf16[4,32,64,512]{3,2,1,0:T(8,128)(2,1)S(1)} %shard_map.175.early) | copy-start | bytes 25165828
  81.0 1.0 copy-start.12
  102.2 46.9 %all-to-all-start.2 = ((f32[32,2,32,128]{3,2,1,0:T(8,128)}), f32[32,2,32,128]{3,2,1,0:T(8,128)S(1)}, u32[]{:S(2)}, u32[]{:S(2)}) async-start(f32[32,2,32,128]{3,2,1,0:T(8,128)} %bitcast.13), calls=%async_computation.2 | async-start | bytes 2097152 | tf_op jit(solution)/shard_map/all_to_all | solution.py:566
  117.4 3.4 %copy-start.1 = (bf16[4,32,64,512]{3,2,1,0:T(8,128)(2,1)S(1)}, bf16[4,32,64,512]{3,2,1,0:T(8,128)(2,1)}, u32[]{:S(2)}) copy-start(bf16[4,32,64,512]{3,2,1,0:T(8,128)(2,1)} %field.5) | copy-start | bytes 25165828
  136.7 3.2 %copy-start.2 = (bf16[4,32,64,512]{3,2,1,0:T(8,128)(2,1)}, bf16[4,32,64,512]{3,2,1,0:T(8,128)(2,1)S(1)}, u32[]{:S(2)}) copy-start(bf16[4,32,64,512]{3,2,1,0:T(8,128)(2,1)S(1)} %get-tuple-element.20.early) | copy-start | bytes 25165828
  149.8 16.3 %all-to-all-start.4 = ((f32[32,9,128]{2,1,0:T(8,128)}), f32[32,9,128]{2,1,0:T(8,128)S(1)}, u32[]{:S(2)}, u32[]{:S(2)}) async-start(f32[32,9,128]{2,1,0:T(8,128)} %broadcast_in_dim.19), calls=%async_computation.4 | async-start | bytes 524288 | tf_op jit(solution)/shard_map/all_to_all | solution.py:566
  155.5 1.6 copy-start.5
  166.1 28.9 %all-to-all-start.3 = ((f32[32,2,32,128]{3,2,1,0:T(8,128)}), f32[32,2,32,128]{3,2,1,0:T(8,128)S(1)}, u32[]{:S(2)}, u32[]{:S(2)}) async-start(f32[32,2,32,128]{3,2,1,0:T(8,128)} %get-tuple-element.18), calls=%async_computation.3 | async-start | bytes 2097152 | tf_op jit(solution)/shard_map/all_to_all | solution.py:566
  195.0 1.1 copy-start.11

commit v3 on v2

--- a/solution.py
+++ b/solution.py
@@ -35,6 +35,11 @@
     high = table.astype(ml_dtypes.bfloat16)
     low = (table - high.astype(np.float64)).astype(ml_dtypes.bfloat16)
     return high, low
+
+
+def stacked(table):
+    high, low = split2(table)
+    return np.concatenate([high, high, low], axis=1)
 
 
 def zt_tables(modes_here):
@@ -62,18 +67,17 @@
 def y_inverse_table():
     theta = angles(np.arange(NY), NY, KY)
     table = np.concatenate([np.cos(theta), np.sin(theta)], axis=0)
-    high, low = split2(table)
-    return np.concatenate([high, high, low], axis=1)
+    return stacked(table)
 
 
 def x_tables(planes, devices):
     theta = angles(np.arange(devices) * planes, NX, KX).T
     cosine, sine = np.cos(theta), np.sin(theta)
-    forward = np.block([[cosine, sine], [-sine, cosine]]).astype(np.float32)
+    forward = np.block([[cosine, sine], [-sine, cosine]])
     turn = np.repeat(angles(np.arange(planes), NX, KX).T, C, axis=1)
     return (
-        forward,
-        np.ascontiguousarray(forward.T),
+        stacked(forward),
+        stacked(forward.T),
         np.cos(turn).astype(np.float32),
         np.sin(turn).astype(np.float32),
     )
@@ -86,6 +90,11 @@
 def halves(value):
     high = value.astype(BF16)
     return high, (value - high.astype(F32)).astype(BF16)
+
+
+def three(value):
+    high, low = halves(value)
+    return jnp.concatenate([high, low, high], axis=0)
 
 
 def dot(left, right):
@@ -153,7 +162,7 @@
     )(field, zt, y_table)
 
 
-QB = 8
+Q_BLOCK = 16
 
 
 def modes_of(received, q_count, devices, lanes, forward, cosine, sine):
@@ -166,12 +175,12 @@
     right = jnp.concatenate(columns, axis=1) if lanes % 128 == 0 else None
     found = []
     if right is not None:
-        summed = jnp.dot(forward, right, precision=HIGHEST, preferred_element_type=F32)
+        summed = dot(forward, three(right))
     for q in range(q_count):
         if right is not None:
             one = summed[:, q * lanes : (q + 1) * lanes]
         else:
-            one = jnp.dot(forward, columns[q], precision=HIGHEST, preferred_element_type=F32)
+            one = dot(forward, three(columns[q]))
         a_re, a_im = one[:KX], one[KX:]
         m_re = lane_total(a_re * cosine + a_im * sine, C)
         m_im = lane_total(a_im * cosine - a_re * sine, C)
@@ -187,12 +196,10 @@
         )
     if lanes % 128 == 0:
         joined = jnp.concatenate(turned, axis=1)
-        back = jnp.dot(inverse, joined, precision=HIGHEST, preferred_element_type=F32)
+        back = dot(inverse, three(joined))
         backs = [back[:, q * lanes : (q + 1) * lanes] for q in range(q_count)]
     else:
-        backs = [
-            jnp.dot(inverse, one, precision=HIGHEST, preferred_element_type=F32) for one in turned
-        ]
+        backs = [dot(inverse, three(one)) for one in turned]
     for q in range(q_count):
         for ri in range(2):
             out[pl.ds(ri * q_count + q, devices, stride=2 * q_count), :] = backs[q][
@@ -205,31 +212,36 @@
     return jnp.where(time_frequency == 0, 1.0, 2.0).astype(F32) / (NX * NY * NZ * NT)
 
 
+def beside(one, two):
+    if one.shape[1] < 128:
+        return jnp.concatenate([one, two], axis=1)
+    lane = lax.broadcasted_iota(jnp.int32, one.shape, 1)
+    return jnp.where(lane < C, one, two)[:, : 2 * C]
+
+
 def mix_kernel(
     received, weight, forward, inverse, cosine, sine, mask, out, modes_out, *, devices, lanes
 ):
-    first = pl.program_id(0) * QB
-    flat_in = received.reshape(devices * 2 * QB, lanes)
-    flat_out = out.reshape(devices * 2 * QB, lanes)
-    modes = modes_of(flat_in, QB, devices, lanes, forward[...], cosine[...], sine[...])
+    q_block = weight.shape[0]
+    first = pl.program_id(0) * q_block
+    flat_in = received.reshape(devices * 2 * q_block, lanes)
+    flat_out = out.reshape(devices * 2 * q_block, lanes)
+    modes = modes_of(flat_in, q_block, devices, lanes, forward[...], cosine[...], sine[...])
+    own_block = jnp.concatenate([mask[...]] * 2, axis=0)
     mixed = []
-    for q in range(QB):
-        both = jnp.concatenate(modes[q], axis=0)
-        modes_out[q] = both
-        high, low = halves(both[:, :C])
-        left = jnp.concatenate([high, low], axis=0)
-        by_re, by_im = dot(left, weight[q, 0]), dot(left, weight[q, 1])
-        by_re, by_im = by_re[: 2 * KX] + by_re[2 * KX :], by_im[: 2 * KX] + by_im[2 * KX :]
-        factor = mode_factor(first, q)
-        pieces = []
-        for wide in (by_re[:KX] - by_im[KX:], by_im[:KX] + by_re[KX:]):
-            kept = wide * mask[...]
-            total = kept[:, :128]
-            for column in range(128, KX * C, 128):
-                total = total + kept[:, column : column + 128]
-            pieces.append(lane_total(total, C)[:, :lanes] * factor)
+    for q in range(q_block):
+        re, im = modes[q]
+        modes_out[q] = jnp.concatenate([re, im], axis=0)
+        high, low = halves(jnp.concatenate([beside(re, -im), beside(im, re)], axis=0))
+        product = dot(jnp.concatenate([high, low], axis=0), weight[q].reshape(2 * C, KX * C))
+        kept = (product[: 2 * KX] + product[2 * KX :]) * own_block
+        total = kept[:, :128]
+        for column in range(128, KX * C, 128):
+            total = total + kept[:, column : column + 128]
+        total = lane_total(total, C)[:, :lanes] * mode_factor(first, q)
+        pieces = (total[:KX], total[KX:])
         mixed.append(pieces)
-    to_planes(mixed, flat_out, QB, devices, lanes, inverse[...], cosine[...], sine[...])
+    to_planes(mixed, flat_out, q_block, devices, lanes, inverse[...], cosine[...], sine[...])
 
 
 def whole(array):
@@ -237,9 +249,10 @@
 
 
 def mode_specs(devices, modes_here, lanes):
-    slab = pl.BlockSpec((devices, 2, QB, lanes), lambda s: (0, 0, s, 0))
-    weight = pl.BlockSpec((QB, 2, C, KX * C), lambda s: (s, 0, 0, 0))
-    modes = pl.BlockSpec((QB, 2 * KX, lanes), lambda s: (s, 0, 0))
+    q_block = min(Q_BLOCK, modes_here)
+    slab = pl.BlockSpec((devices, 2, q_block, lanes), lambda s: (0, 0, s, 0))
+    weight = pl.BlockSpec((q_block, 2, C, KX * C), lambda s: (s, 0, 0, 0))
+    modes = pl.BlockSpec((q_block, 2 * KX, lanes), lambda s: (s, 0, 0))
     return slab, weight, modes
 
 
@@ -248,7 +261,7 @@
     slab, weight_spec, modes = mode_specs(devices, modes_here, lanes)
     return pl.pallas_call(
         functools.partial(mix_kernel, devices=devices, lanes=lanes),
-        grid=(modes_here // QB,),
+        grid=(modes_here // min(Q_BLOCK, modes_here),),
         in_specs=[slab, weight_spec] + [whole(table) for table in tables],
         out_specs=[slab, modes],
         out_shape=[
@@ -271,14 +284,15 @@
 def adjoint_kernel(
     received, weight, forward, inverse, cosine, sine, mask, out, modes_out, *, devices, lanes
 ):
-    first = pl.program_id(0) * QB
-    flat_in = received.reshape(devices * 2 * QB, lanes)
-    flat_out = out.reshape(devices * 2 * QB, lanes)
-    modes = modes_of(flat_in, QB, devices, lanes, forward[...], cosine[...], sine[...])
+    q_block = weight.shape[0]
+    first = pl.program_id(0) * q_block
+    flat_in = received.reshape(devices * 2 * q_block, lanes)
+    flat_out = out.reshape(devices * 2 * q_block, lanes)
+    modes = modes_of(flat_in, q_block, devices, lanes, forward[...], cosine[...], sine[...])
     group = lax.broadcasted_iota(jnp.int32, (KX, 128), 1) // C
     odd = group % 2 == 1
     mixed = []
-    for q in range(QB):
+    for q in range(q_block):
         factor = mode_factor(first, q)
         d_re, d_im = modes[q][0] * factor, modes[q][1] * factor
         modes_out[q] = jnp.concatenate([d_re, d_im], axis=0)
@@ -295,7 +309,7 @@
         re = jnp.where(odd, pltpu.roll(re, C, 1), re)
         im = jnp.where(odd, pltpu.roll(im, C, 1), im)
         mixed.append((re[:, :lanes], im[:, :lanes]))
-    to_planes(mixed, flat_out, QB, devices, lanes, inverse[...], cosine[...], sine[...])
+    to_planes(mixed, flat_out, q_block, devices, lanes, inverse[...], cosine[...], sine[...])
 
 
 def adjoint_modes(received, weight, tables):
@@ -303,7 +317,7 @@
     slab, weight_spec, modes = mode_specs(devices, modes_here, lanes)
     return pl.pallas_call(
         functools.partial(adjoint_kernel, devices=devices, lanes=lanes),
-        grid=(modes_here // QB,),
+        grid=(modes_here // min(Q_BLOCK, modes_here),),
         in_specs=[slab, weight_spec] + [whole(table) for table in tables],
         out_specs=[slab, modes],
         out_shape=[
@@ -316,7 +330,7 @@
 
 
 def gradient_kernel(modes, dmodes, mask, out):
-    for q in range(QB):
+    for q in range(modes.shape[0]):
         left = modes[q][:, :C]
         l_high, l_low = halves(left)
         left = jnp.concatenate([l_high, l_high, l_low], axis=0)
@@ -331,12 +345,13 @@
 
 def mode_gradient(modes, dmodes, mask):
     modes_here, _, lanes = modes.shape
-    spec = pl.BlockSpec((QB, 2 * KX, lanes), lambda s: (s, 0, 0))
+    q_block = min(Q_BLOCK, modes_here)
+    spec = pl.BlockSpec((q_block, 2 * KX, lanes), lambda s: (s, 0, 0))
     return pl.pallas_call(
         gradient_kernel,
-        grid=(modes_here // QB,),
+        grid=(modes_here // q_block,),
         in_specs=[spec, spec, whole(mask)],
-        out_specs=pl.BlockSpec((QB, 2, C, KX * C), lambda s: (s, 0, 0, 0)),
+        out_specs=pl.BlockSpec((q_block, 2, C, KX * C), lambda s: (s, 0, 0, 0)),
         out_shape=jax.ShapeDtypeStruct((modes_here, 2, C, KX * C), F32),
         compiler_params=pltpu.CompilerParams(vmem_limit_bytes=32 * MIB),
         cost_estimate=pl.CostEstimate(flops=10**8, bytes_accessed=5 * MIB, transcendentals=0),
@@ -359,31 +374,140 @@
             ],
             axis=1,
         )
-        high, low = halves(pair)
-        both = dot(y_table, jnp.concatenate([high, low, high], axis=0)).astype(BF16)
+        both = dot(y_table, three(pair)).astype(BF16)
         for k in range(2):
             columns = slice(k * 2 * Q, (k + 1) * 2 * Q)
             found.append(jnp.concatenate([both[:NY, columns], both[NY:, columns]], axis=1))
     return jnp.concatenate(found, axis=0)
 
 
-def local_kernel(field, local, bias, out):
+def row_pick():
+    return (np.arange(C * YB)[:, None] // YB == np.arange(C)[None, :]).astype(ml_dtypes.bfloat16)
+
+
+def same_y():
+    rows = np.arange(C * YB)
+    return (rows[:, None] % YB == rows[None, :] % YB).astype(ml_dtypes.bfloat16)
+
+
+def channel_map(weight, pick, same, out):
+    rows = dot(pick, weight).astype(BF16)
+    wide = lax.dot_general(rows, pick, (((1,), (1,)), ((), ())), preferred_element_type=F32)
+    out[...] = wide.astype(BF16) * same
+
+
+def local_kernel(field, weight, bias, pick, same, out, local):
     rows = C * YB
-    total = dot(local[...], field[0].reshape(rows, CELLS)) + bias[...]
-    out[0] = total.astype(BF16).reshape(C, YB, CELLS)
-
-
-def local_term(field, local, bias):
-    block = pl.BlockSpec((1, C, YB, CELLS), lambda x, y: (x, 0, y, 0))
+
+    @pl.when((pl.program_id(0) == 0) & (pl.program_id(1) == 0))
+    def _():
+        channel_map(weight[...], pick[...], same[...], local)
+
+    for part in range(field.shape[2] // YB):
+        y = slice(part * YB, (part + 1) * YB)
+        total = dot(local[...], field[0, :, y].reshape(rows, CELLS)) + bias[...]
+        out[0, :, y] = total.astype(BF16).reshape(C, YB, CELLS)
+
+
+def local_term(field, weight, bias, pick, same, parts=1):
+    block = pl.BlockSpec((1, C, NY // parts, CELLS), lambda x, y: (x, 0, y, 0))
+    rows = C * YB
     return pl.pallas_call(
         local_kernel,
-        grid=(field.shape[0], NY // YB),
-        in_specs=[block, whole(local), whole(bias)],
+        grid=(field.shape[0], parts),
+        in_specs=[block, whole(weight), whole(bias), whole(pick), whole(same)],
         out_specs=block,
         out_shape=jax.ShapeDtypeStruct(field.shape, BF16),
-        compiler_params=pltpu.CompilerParams(vmem_limit_bytes=32 * MIB),
-        cost_estimate=pl.CostEstimate(flops=8 * 10**9, bytes_accessed=25 * MIB, transcendentals=0),
-    )(field, local, bias)
+        scratch_shapes=[pltpu.VMEM((rows, rows), BF16)],
+        compiler_params=pltpu.CompilerParams(vmem_limit_bytes=56 * MIB),
+        cost_estimate=pl.CostEstimate(flops=4 * 10**9, bytes_accessed=17 * MIB, transcendentals=0),
+    )(field, weight, bias, pick, same)
+
+
+def late_kernel(slope, weight, pick, same, out, local):
+    rows = C * YB
+
+    @pl.when((pl.program_id(0) == 0) & (pl.program_id(1) == 0))
+    def _():
+        channel_map(weight[...], pick[...], same[...], local)
+
+    for part in range(slope.shape[2] // YB):
+        y = slice(part * YB, (part + 1) * YB)
+        total = dot(local[...], slope[0, :, y].reshape(rows, CELLS))
+        out[0, :, y] = total.astype(BF16).reshape(C, YB, CELLS)
+
+
+def late_term(slope, weight, pick, same, parts=1):
+    block = pl.BlockSpec((1, C, NY // parts, CELLS), lambda x, y: (x, 0, y, 0))
+    rows = C * YB
+    return pl.pallas_call(
+        late_kernel,
+        grid=(slope.shape[0], parts),
+        in_specs=[block, whole(weight), whole(pick), whole(same)],
+        out_specs=block,
+        out_shape=jax.ShapeDtypeStruct(slope.shape, BF16),
+        scratch_shapes=[pltpu.VMEM((rows, rows), BF16)],
+        compiler_params=pltpu.CompilerParams(vmem_limit_bytes=56 * MIB),
+        cost_estimate=pl.CostEstimate(flops=4 * 10**9, bytes_accessed=17 * MIB, transcendentals=0),
+    )(slope, weight, pick, same)
+
+
+def pointwise_kernel(field, slope, bias_part, pick, same, out, total):
+    rows = C * YB
+    first_step = (pl.program_id(0) == 0) & (pl.program_id(1) == 0)
+    last_step = (pl.program_id(0) == pl.num_programs(0) - 1) & (
+        pl.program_id(1) == pl.num_programs(1) - 1
+    )
+
+    @pl.when(first_step)
+    def _():
+        total[...] = jnp.zeros_like(total)
+
+    for part in range(field.shape[2] // YB):
+        y = slice(part * YB, (part + 1) * YB)
+        total[...] += lax.dot_general(
+            field[0, :, y].reshape(rows, CELLS),
+            slope[0, :, y].reshape(rows, CELLS),
+            (((1,), (1,)), ((), ())),
+            preferred_element_type=F32,
+        )
+
+    @pl.when(last_step)
+    def _():
+        to_f32 = functools.partial(
+            lax.dot_general, precision=HIGHEST, preferred_element_type=F32
+        )
+        chosen = pick[...].astype(F32)
+        tiled = jnp.concatenate([chosen] * 4, axis=1)
+        kept = total[...] * same[...].astype(F32)
+        across = to_f32(kept, tiled, (((1,), (0,)), ((), ())))
+        grads = to_f32(chosen, across, (((0,), (0,)), ((), ())))
+        group = lax.broadcasted_iota(jnp.int32, (8, 128), 1) // C
+        folded = jnp.zeros((8, 128), F32)
+        for g in range(4):
+            folded = jnp.where(group == g, grads[g * 8 : (g + 1) * 8], folded)
+        out[:8, :] = folded
+        lane_sums = to_f32(jnp.ones((8, 128), F32), bias_part[...], (((1,), (1,)), ((), ())))
+        by_channel = (
+            lax.broadcasted_iota(jnp.int32, (8 * C, 128), 0) // 8
+            == lax.broadcasted_iota(jnp.int32, (8 * C, 128), 1)
+        ).astype(F32)
+        out[8:, :] = to_f32(lane_sums, by_channel, (((1,), (0,)), ((), ())))
+
+
+def pointwise_gradient(field, slope, bias_part, pick, same, parts=1):
+    block = pl.BlockSpec((1, C, NY // parts, CELLS), lambda x, y: (x, 0, y, 0))
+    rows = C * YB
+    return pl.pallas_call(
+        pointwise_kernel,
+        grid=(field.shape[0], parts),
+        in_specs=[block, block, whole(bias_part), whole(pick), whole(same)],
+        out_specs=pl.BlockSpec((16, 128), lambda x, y: (0, 0)),
+        out_shape=jax.ShapeDtypeStruct((16, 128), F32),
+        scratch_shapes=[pltpu.VMEM((rows, rows), F32)],
+        compiler_params=pltpu.CompilerParams(vmem_limit_bytes=56 * MIB),
+        cost_estimate=pl.CostEstimate(flops=4 * 10**9, bytes_accessed=17 * MIB, transcendentals=0),
+    )(field, slope, bias_part, pick, same)
 
 
 def middle_kernel(
@@ -484,37 +608,6 @@
     )(back, early, cotangent, zt, zt_turned, y_back, y_table)
 
 
-def late_kernel(field, slope, local, out, local_grad):
-    rows = C * YB
-
-    @pl.when((pl.program_id(0) == 0) & (pl.program_id(1) == 0))
-    def _():
-        local_grad[...] = jnp.zeros_like(local_grad)
-
-    values, low = field[0].reshape(rows, CELLS), slope[0].reshape(rows, CELLS)
-    out[0] = dot(local[...], low).astype(BF16).reshape(C, YB, CELLS)
-    local_grad[...] += lax.dot_general(
-        values, low, (((1,), (1,)), ((), ())), preferred_element_type=F32
-    )
-
-
-def late_terms(field, slope, local):
-    block = pl.BlockSpec((1, C, YB, CELLS), lambda x, y: (x, 0, y, 0))
-    rows = C * YB
-    return pl.pallas_call(
-        late_kernel,
-        grid=(field.shape[0], NY // YB),
-        in_specs=[block, block, whole(local)],
-        out_specs=[block, pl.BlockSpec((rows, rows), lambda x, y: (0, 0))],
-        out_shape=[
-            jax.ShapeDtypeStruct(field.shape, BF16),
-            jax.ShapeDtypeStruct((rows, rows), F32),
-        ],
-        compiler_params=pltpu.CompilerParams(vmem_limit_bytes=32 * MIB),
-        cost_estimate=pl.CostEstimate(flops=12 * 10**9, bytes_accessed=25 * MIB, transcendentals=0),
-    )(field, slope, local)
-
-
 def last_kernel(back, early, zt_turned, y_back, out, gathered, *, lanes, block, group):
     plane, part = pl.program_id(0), pl.program_id(1)
 
@@ -556,10 +649,7 @@
     mask = jnp.asarray(diagonal_mask())
     tables = [jnp.asarray(table) for table in x_tables(planes, devices)] + [mask]
 
-    eye = jnp.eye(YB, dtype=BF16)
-    rows = C * YB
-    local_back = (local_weight[:, None, :, None] * eye[None, :, None, :]).reshape(rows, rows)
-    local_here = (local_weight.T[:, None, :, None] * eye[None, :, None, :]).reshape(rows, rows)
+    pick, same = jnp.asarray(row_pick()), jnp.asarray(same_y())
     bias = jnp.repeat(local_bias, YB)[:, None]
 
     def exchange(value):
@@ -572,21 +662,22 @@
         return exchange(back).reshape(KY * 2 * Q, lanes)
 
     spectra = forward_planes(hidden_field, zt, y_table)
-    early = local_term(hidden_field, local_here, bias)
+    early = local_term(hidden_field, local_weight.T, bias, pick, same)
     back, modes = mix_modes(to_owner(spectra), spectral_weight, tables)
     output, slope, dspectra, bias_part = middle(
         to_slabs(back), early, cotangent, zt, zt_turned, y_back, y_table
     )
-    late, local_part = late_terms(hidden_field, slope, local_back)
+    total = pointwise_gradient(hidden_field, slope, bias_part, pick, same)
     dback, dmodes = adjoint_modes(to_owner(dspectra), spectral_weight, tables)
+    dback, slope, total = lax.optimization_barrier((dback, slope, total))
+    late = late_term(slope, local_weight, pick, same)
     grad_spectral = mode_gradient(modes, dmodes, mask)
-    local_sum = jnp.einsum("iyoy->io", local_part.reshape(C, YB, C, YB))
-    bias_sum = jnp.sum(bias_part.reshape(C, 8 * 128), axis=1)
-    partial = jnp.concatenate([local_sum.reshape(C * C // 128, 128), jnp.tile(bias_sum, 4)[None]])
-    copies = jnp.broadcast_to(partial, (devices,) + partial.shape)
-    total = jnp.sum(exchange(copies), axis=0)
-    grad_local = total[: C * C // 128].reshape(C, C)
-    grad_bias = total[C * C // 128, :C]
+    span = 1
+    while span < devices:
+        total = total + lax.ppermute(total, "gx", [(d, d ^ span) for d in range(devices)])
+        span *= 2
+    grad_local = total[:8].reshape(8, 4, C).swapaxes(0, 1).reshape(C, C)
+    grad_bias = total[8, :C]
     grad_field = last(to_slabs(dback), late, zt_turned, y_back)
     return (output, grad_field, grad_spectral, grad_local, grad_bias)
 

time: 207 us -> 181 us (0.87)
  local copies, waits for them, and re-layouts: 39.9 us -> 6.43 us
  waiting for transfers between devices: 25.2 us -> 35 us
  other arithmetic: 9.23 us -> 0.71 us
  starting transfers between devices: 18 us -> 22.3 us
    mul x2 -> x0, local copies, waits for them, and re-layouts: 15.6 us -> none  [the longest x1 7.78 us: on_device(): local_weight[:, None, :, None] * eye[None, :, None, :]]
    unnamed x30 -> x23, local copies, waits for them, and re-layouts: 17.1 us -> 4.28 us
    ppermute x0 -> x5, starting transfers between devices: none -> 11.3 us  [on_device(): lax.ppermute(total, 'gx', [(d, d ^ span) for d in range(devices)])]
    all_to_all x4 -> x3, starting transfers between devices: 18 us -> 11.1 us  [exchange(): return lax.all_to_all(value, 'gx', split_axis=0, concat_axis=0, tiled=True)]
    pallas_call x3 -> x4, Pallas kernels: 27.3 us -> 33.7 us  [the longest x1 11.3 us: pointwise_gradient(): pl.pallas_call(pointwise_kernel, grid=(field.shape[0], parts), in_specs=[...]
    ppermute x0 -> x5, waiting for transfers between devices: none -> 5.62 us  [on_device(): lax.ppermute(total, 'gx', [(d, d ^ span) for d in range(devices)])]
    reduce_sum x4 -> x0, other arithmetic: 5.51 us -> none  [the longest x1 4.33 us: on_device(): local_sum = jnp.einsum('iyoy->io', local_part.reshape(C, YB, C, YB))]
    reshape x3 -> x1, local copies, waits for them, and re-layouts: 5.55 us -> 0.08 us  [on_device(): grad_local = total[:8].reshape(8, 4, C).swapaxes(0, 1).reshape(C, C)]
  transfers between devices with their start and end apart: 4 -> 8, of which waited for: 2 -> 5; matrix products, arithmetic and copies ran while one was open for 15% -> 2% of each run, Pallas kernels for 16% -> 19%
where the time goes in v3:
time: 181 us; the launch traced here: 180 us
  Pallas kernels  81 us (45%)
  waiting for transfers between devices  35 us (19%)
  blocking collectives  33.5 us (19%)
  starting transfers between devices  22.3 us (12%)
  local copies, waits for them, and re-layouts  6.43 us (4%)
    all_to_all x1, blocking collectives, exchange(): return lax.all_to_all(value, 'gx', split_axis=0, concat_axis=0, tiled=True)  33.5 us
    all_to_all x3, waiting for transfers between devices, exchange(): return lax.all_to_all(value, 'gx', split_axis=0, concat_axis=0, tiled=True)  29.4 us
    pallas_call x1, Pallas kernels, middle(): pl.pallas_call(functools.partial(middle_kernel, lanes=lanes, block=block,...  20.2 us
    pallas_call x1, Pallas kernels, pointwise_gradient(): pl.pallas_call(pointwise_kernel, grid=(field.shape[0], parts), in_specs=[...  11.3 us
    ppermute x5, starting transfers between devices, on_device(): lax.ppermute(total, 'gx', [(d, d ^ span) for d in range(devices)])  11.3 us
    all_to_all x3, starting transfers between devices, exchange(): return lax.all_to_all(value, 'gx', split_axis=0, concat_axis=0, tiled=True)  11.1 us
    pallas_call x1, Pallas kernels, local_term(): pl.pallas_call(local_kernel, grid=(field.shape[0], parts), in_specs=[bloc...  9.95 us
    pallas_call x1, Pallas kernels, late_term(): pl.pallas_call(late_kernel, grid=(slope.shape[0], parts), in_specs=[block...  9.85 us
  transfers between devices with their start and end apart: 8, of which 5 were waited for; matrix products, arithmetic and copies ran while one was open for 2% of the time, Pallas kernels for 19%

profile of v3, /device:TPU:0, one launch (start us, length us, event | category | flops | bytes accessed | tf_op | source)
XLA Modules:
  0.0 179.8 jit_solution(11513399859637492889)
XLA Ops:
  0.7 9.4 %shard_map.191 = f32[2048,128]{1,0:T(8,128)} custom-call(bf16[4,32,64,512]{3,2,1,0:T(8,128)(2,1)} %field.5, bf16[512,256]{1,0:T(8,128)(2,1)} %constant.22.clone.zt, bf16[32,128]{1,0:T(8,128)(2,1)} %constant.24.clone.y_table), custom_call_target="tpu_custom_call" | custom-call | flops 2000000000 | bytes 9437184 | tf_op jit(solution)/shard_map/pallas_call | solution.py:149
  10.1 33.5 %all_to_all.20.received = f32[32,2,32,128]{3,2,1,0:T(8,128)S(1)} all-to-all(f32[32,2,32,128]{3,2,1,0:T(8,128)} %bitcast.12), channel_id=1, replica_groups=mesh['groups'=1,'gx'=32] {'gx'}, dimensions={0} | all-to-all | bytes 2097152 | tf_op jit(solution)/shard_map/all_to_all | solution.py:656
  43.7 3.7 %shard_map.192 = (f32[32,2,32,128]{3,2,1,0:T(8,128)}, f32[32,32,128]{2,1,0:T(8,128)S(1)}) custom-call(f32[32,2,32,128]{3,2,1,0:T(8,128)S(1)} %all_to_all.20.received, bf16[32,2,32,512]{3,2,1,0:T(8,128)(2,1)S(1)} %copy-done.1, bf16[32,192]{1,0:T(8,128)(2,1)S(1)} %copy-done.3, bf16[64,96]{1,0:T(8,128)(2,1)S(1)} %copy-done.4, f32[16,128]{1,0:T(8,128)S(1)} %copy-done.5, ...), custom_call_target="tpu_custom_call" | custom-call | flops 1000000000 | bytes 5242880 | tf_op jit(solution)/shard_map/pallas_call | solution.py:262
  47.3 3.6 %all-to-all-start.1 = ((f32[32,2,32,128]{3,2,1,0:T(8,128)}), f32[32,2,32,128]{3,2,1,0:T(8,128)S(1)}, u32[]{:S(2)}, u32[]{:S(2)}) async-start(f32[32,2,32,128]{3,2,1,0:T(8,128)} %get-tuple-element.16), calls=%async_computation.1 | async-start | bytes 2097152 | tf_op jit(solution)/shard_map/all_to_all | solution.py:656
  52.6 9.9 %shard_map.193.early = bf16[4,32,64,512]{3,2,1,0:T(8,128)(2,1)} custom-call(bf16[4,32,64,512]{3,2,1,0:T(8,128)(2,1)} %field.5, bf16[32,32]{1,0:T(8,128)(2,1)} %bitcast.16, f32[512,1]{1,0:T(8,128)} %broadcast_in_dim_reshape.4.bias, bf16[512,32]{1,0:T(8,128)(2,1)} %constant.31.clone.pick, bf16[512,512]{1,0:T(8,128)(2,1)} %constant.32.clone.same), custom_call_target="tpu_custom_call" | custom-call | flops 4000000000 | bytes 17825792 | tf_op jit(solution)/shard_map/pallas_call | solution.py:415
  62.5 14.7 %all-to-all-done.1 = f32[32,2,32,128]{3,2,1,0:T(8,128)S(1)} async-done(((f32[32,2,32,128]{3,2,1,0:T(8,128)}), f32[32,2,32,128]{3,2,1,0:T(8,128)S(1)}, u32[]{:S(2)}, u32[]{:S(2)}) %all-to-all-start.1) | async-done | bytes 1048608 | tf_op jit(solution)/shard_map/all_to_all | solution.py:656
  77.2 1.0 copy-done.8
  78.2 20.2 %shard_map.194 = (bf16[4,32,64,512]{3,2,1,0:T(8,128)(2,1)}, bf16[4,32,64,512]{3,2,1,0:T(8,128)(2,1)}, f32[2048,128]{1,0:T(8,128)}, f32[256,128]{1,0:T(8,128)}) custom-call(f32[2048,128]{1,0:T(8,128)} %bitcast.13, bf16[4,32,64,512]{3,2,1,0:T(8,128)(2,1)} %shard_map.193.early, bf16[4,32,64,512]{3,2,1,0:T(8,128)(2,1)} %cotangent.1, ...), custom_call_target="tpu_custom_call" | custom-call | flops 5000000000 | bytes 44040192 | tf_op jit(solution)/shard_map/pallas_call | solution.py:576
  98.4 3.8 %all-to-all-start.2 = ((f32[32,2,32,128]{3,2,1,0:T(8,128)}), f32[32,2,32,128]{3,2,1,0:T(8,128)S(1)}, u32[]{:S(2)}, u32[]{:S(2)}) async-start(f32[32,2,32,128]{3,2,1,0:T(8,128)} %bitcast.14), calls=%async_computation.2 | async-start | bytes 2097152 | tf_op jit(solution)/shard_map/all_to_all | solution.py:656
  102.2 11.3 %shard_map.196 = f32[16,128]{1,0:T(8,128)} custom-call(bf16[4,32,64,512]{3,2,1,0:T(8,128)(2,1)} %field.5, bf16[4,32,64,512]{3,2,1,0:T(8,128)(2,1)} %get-tuple-element.23.slope, f32[256,128]{1,0:T(8,128)} %get-tuple-element.21.bias_part, bf16[512,32]{1,0:T(8,128)(2,1)} %constant.31.clone.pick, bf16[512,512]{1,0:T(8,128)(2,1)} %constant.32.clone.same), custom_call_target="tpu_custom_call" | custom-call | flops 4000000000 | bytes 17825792 | tf_op jit(solution)/shard_map/pallas_call | solution.py:501
  113.5 14.7 %all-to-all-done.2.received = f32[32,2,32,128]{3,2,1,0:T(8,128)S(1)} async-done(((f32[32,2,32,128]{3,2,1,0:T(8,128)}), f32[32,2,32,128]{3,2,1,0:T(8,128)S(1)}, u32[]{:S(2)}, u32[]{:S(2)}) %all-to-all-start.2) | async-done | bytes 1048608 | tf_op jit(solution)/shard_map/all_to_all | solution.py:656
  128.3 1.6 copy-done.2
  129.9 4.3 %shard_map.195 = (f32[32,2,32,128]{3,2,1,0:T(8,128)}, f32[32,32,128]{2,1,0:T(8,128)S(1)}) custom-call(f32[32,2,32,128]{3,2,1,0:T(8,128)S(1)} %all-to-all-done.2.received, bf16[32,2,32,512]{3,2,1,0:T(8,128)(2,1)S(1)} %copy-done.2, bf16[32,192]{1,0:T(8,128)(2,1)S(1)} %copy-done.3, bf16[64,96]{1,0:T(8,128)(2,1)S(1)} %copy-done.4, f32[16,128]{1,0:T(8,128)S(1)} %copy-done.5, ...), custom_call_target="tpu_custom_call" | custom-call | flops 1000000000 | bytes 5242880 | tf_op jit(solution)/shard_map/pallas_call | solution.py:318
  134.2 3.6 %all-to-all-start.3 = ((f32[32,2,32,128]{3,2,1,0:T(8,128)}), f32[32,2,32,128]{3,2,1,0:T(8,128)S(1)}, u32[]{:S(2)}, u32[]{:S(2)}) async-start(f32[32,2,32,128]{3,2,1,0:T(8,128)} %get-tuple-element.22), calls=%async_computation.3 | async-start | bytes 2097152 | tf_op jit(solution)/shard_map/all_to_all | solution.py:656
  138.1 1.1 collective-permute-done
  139.9 1.8 collective-permute-start.1
  141.7 2.8 %collective-permute-done.1 = f32[16,128]{1,0:T(8,128)S(1)} collective-permute-done((f32[16,128]{1,0:T(8,128)S(1)}, f32[16,128]{1,0:T(8,128)S(1)}, u32[]{:S(2)}, u32[]{:S(2)}) %collective-permute-start.1) | collective-permute-done | bytes 8224 | tf_op jit(solution)/shard_map/ppermute | solution.py:677
  144.5 3.8 %collective-permute-start.2 = (f32[16,128]{1,0:T(8,128)S(1)}, f32[16,128]{1,0:T(8,128)S(1)}, u32[]{:S(2)}, u32[]{:S(2)}) collective-permute-start(f32[16,128]{1,0:T(8,128)S(1)} %add.16), channel_id=1, source_target_pairs={{0,4},{1,5},{2,6},{3,7},{4,0},{5,1},{6,2},{7,3},{8,12},{9,13},{10,... | collective-permute-start | bytes 24584 | tf_op jit(solution)/shard_map/ppermute | solution.py:677
  148.3 1.7 collective-permute-done.2
  150.1 9.9 %shard_map.197.early = bf16[4,32,64,512]{3,2,1,0:T(8,128)(2,1)} custom-call(bf16[4,32,64,512]{3,2,1,0:T(8,128)(2,1)} %get-tuple-element.23.slope, bf16[32,32]{1,0:T(8,128)(2,1)} %weight.5, bf16[512,32]{1,0:T(8,128)(2,1)} %constant.31.clone.pick, bf16[512,512]{1,0:T(8,128)(2,1)} %constant.32.clone.same), custom_call_target="tpu_custom_call" | custom-call | flops 4000000000 | bytes 17825792 | tf_op jit(solution)/shard_map/pallas_call | solution.py:443
  160.0 5.3 %collective-permute-start.4 = (f32[16,128]{1,0:T(8,128)S(1)}, f32[16,128]{1,0:T(8,128)S(1)}, u32[]{:S(2)}, u32[]{:S(2)}) collective-permute-start(f32[16,128]{1,0:T(8,128)S(1)} %add.18), channel_id=1, source_target_pairs={{0,16},{1,17},{2,18},{3,19},{4,20},{5,21},{6,22},{7,23},{8,24},{9,... | collective-permute-start | bytes 24584 | tf_op jit(solution)/shard_map/ppermute | solution.py:677
  165.3 2.6 %shard_map.199 = f32[32,2,32,512]{3,2,1,0:T(8,128)} custom-call(f32[32,32,128]{2,1,0:T(8,128)S(1)} %get-tuple-element.24.modes, f32[32,32,128]{2,1,0:T(8,128)S(1)} %get-tuple-element.25.dmodes, f32[16,512]{1,0:T(8,128)S(1)} %copy-done), custom_call_target="tpu_custom_call" | custom-call | flops 100000000 | bytes 5242880 | tf_op jit(solution)/shard_map/pallas_call | solution.py:350
  169.1 1.0 copy-done.7
  170.1 9.7 %shard_map.198 = bf16[4,32,64,512]{3,2,1,0:T(8,128)(2,1)} custom-call(f32[2048,128]{1,0:T(8,128)} %bitcast.11, bf16[4,32,64,512]{3,2,1,0:T(8,128)(2,1)} %shard_map.197.early, bf16[256,512]{1,0:T(8,128)(2,1)} %constant.23.clone.zt_turned, bf16[128,48]{1,0:T(8,128)(2,1)} %constant.25.clone.y_back), custom_call_target="tpu_custom_call" | custom-call | flops 2000000000 | bytes 17825792 | tf_op jit(solution)/shard_map/pallas_call | solution.py:628
  (36 shorter events, 4.0 us)
Async XLA Ops:
  0.6 43.0 %copy-start = (f32[16,512]{1,0:T(8,128)S(1)}, f32[16,512]{1,0:T(8,128)}, u32[]{:S(2)}) copy-start(f32[16,512]{1,0:T(8,128)} %constant.26.clone.mask) | copy-start | bytes 98308
  0.6 43.0 %copy-start.3 = (bf16[32,192]{1,0:T(8,128)(2,1)S(1)}, bf16[32,192]{1,0:T(8,128)(2,1)}, u32[]{:S(2)}) copy-start(bf16[32,192]{1,0:T(8,128)(2,1)} %constant.27.clone.forward) | copy-start | bytes 36868
  0.7 43.0 %copy-start.4 = (bf16[64,96]{1,0:T(8,128)(2,1)S(1)}, bf16[64,96]{1,0:T(8,128)(2,1)}, u32[]{:S(2)}) copy-start(bf16[64,96]{1,0:T(8,128)(2,1)} %constant.28.clone.inverse) | copy-start | bytes 36868
  0.7 43.0 %copy-start.5 = (f32[16,128]{1,0:T(8,128)S(1)}, f32[16,128]{1,0:T(8,128)}, u32[]{:S(2)}) copy-start(f32[16,128]{1,0:T(8,128)} %constant.29.clone.cosine) | copy-start | bytes 24580
  0.7 43.0 %copy-start.6 = (f32[16,128]{1,0:T(8,128)S(1)}, f32[16,128]{1,0:T(8,128)}, u32[]{:S(2)}) copy-start(f32[16,128]{1,0:T(8,128)} %constant.30.clone.sine) | copy-start | bytes 24580
  0.7 43.0 %copy-start.1 = (bf16[32,2,32,512]{3,2,1,0:T(8,128)(2,1)S(1)}, bf16[32,2,32,512]{3,2,1,0:T(8,128)(2,1)}, u32[]{:S(2)}) copy-start(bf16[32,2,32,512]{3,2,1,0:T(8,128)(2,1)} %weight.4) | copy-start | bytes 6291460
  0.7 50.3 %copy-start.10 = (f32[32]{0:T(128)S(1)}, f32[32]{0:T(128)}, u32[]{:S(2)}) copy-start(f32[32]{0:T(128)} %param.20) | copy-start | bytes 388
  0.7 51.2 %copy-start.9 = (bf16[32,32]{1,0:T(8,128)(2,1)S(1)}, bf16[32,32]{1,0:T(8,128)(2,1)}, u32[]{:S(2)}) copy-start(bf16[32,32]{1,0:T(8,128)(2,1)} %weight.5) | copy-start | bytes 6148
  47.3 29.9 %all-to-all-start.1 = ((f32[32,2,32,128]{3,2,1,0:T(8,128)}), f32[32,2,32,128]{3,2,1,0:T(8,128)S(1)}, u32[]{:S(2)}, u32[]{:S(2)}) async-start(f32[32,2,32,128]{3,2,1,0:T(8,128)} %get-tuple-element.16), calls=%async_computation.1 | async-start | bytes 2097152 | tf_op jit(solution)/shard_map/all_to_all | solution.py:656
  77.2 1.0 copy-start.8
  98.4 29.9 %all-to-all-start.2 = ((f32[32,2,32,128]{3,2,1,0:T(8,128)}), f32[32,2,32,128]{3,2,1,0:T(8,128)S(1)}, u32[]{:S(2)}, u32[]{:S(2)}) async-start(f32[32,2,32,128]{3,2,1,0:T(8,128)} %bitcast.14), calls=%async_computation.2 | async-start | bytes 2097152 | tf_op jit(solution)/shard_map/all_to_all | solution.py:656
  128.3 1.6 copy-start.2
  134.2 34.9 %all-to-all-start.3 = ((f32[32,2,32,128]{3,2,1,0:T(8,128)}), f32[32,2,32,128]{3,2,1,0:T(8,128)S(1)}, u32[]{:S(2)}, u32[]{:S(2)}) async-start(f32[32,2,32,128]{3,2,1,0:T(8,128)} %get-tuple-element.22), calls=%async_computation.3 | async-start | bytes 2097152 | tf_op jit(solution)/shard_map/all_to_all | solution.py:656
  137.8 1.4 collective-permute-start
  139.9 4.5 %collective-permute-start.1 = (f32[16,128]{1,0:T(8,128)S(1)}, f32[16,128]{1,0:T(8,128)S(1)}, u32[]{:S(2)}, u32[]{:S(2)}) collective-permute-start(f32[16,128]{1,0:T(8,128)S(1)} %add.15), channel_id=1, source_target_pairs={{0,2},{1,3},{2,0},{3,1},{4,6},{5,7},{6,4},{7,5},{8,10},{9,11},{10,... | collective-permute-start | bytes 24584 | tf_op jit(solution)/shard_map/ppermute | solution.py:677
  144.5 5.5 %collective-permute-start.2 = (f32[16,128]{1,0:T(8,128)S(1)}, f32[16,128]{1,0:T(8,128)S(1)}, u32[]{:S(2)}, u32[]{:S(2)}) collective-permute-start(f32[16,128]{1,0:T(8,128)S(1)} %add.16), channel_id=1, source_target_pairs={{0,4},{1,5},{2,6},{3,7},{4,0},{5,1},{6,2},{7,3},{8,12},{9,13},{10,... | collective-permute-start | bytes 24584 | tf_op jit(solution)/shard_map/ppermute | solution.py:677
  150.0 10.0 %collective-permute-start.3 = (f32[16,128]{1,0:T(8,128)S(1)}, f32[16,128]{1,0:T(8,128)S(1)}, u32[]{:S(2)}, u32[]{:S(2)}) collective-permute-start(f32[16,128]{1,0:T(8,128)S(1)} %add.17), channel_id=1, source_target_pairs={{0,8},{1,9},{2,10},{3,11},{4,12},{5,13},{6,14},{7,15},{8,0},{9,1},... | collective-permute-start | bytes 24584 | tf_op jit(solution)/shard_map/ppermute | solution.py:677
  160.0 7.9 %collective-permute-start.4 = (f32[16,128]{1,0:T(8,128)S(1)}, f32[16,128]{1,0:T(8,128)S(1)}, u32[]{:S(2)}, u32[]{:S(2)}) collective-permute-start(f32[16,128]{1,0:T(8,128)S(1)} %add.18), channel_id=1, source_target_pairs={{0,16},{1,17},{2,18},{3,19},{4,20},{5,21},{6,22},{7,23},{8,24},{9,... | collective-permute-start | bytes 24584 | tf_op jit(solution)/shard_map/ppermute | solution.py:677
  169.1 1.0 copy-start.7

commit v4 on v3

--- a/solution.py
+++ b/solution.py
@@ -16,6 +16,7 @@
 Q = KZ * KT
 CELLS = NZ * NT
 YB = 16
+PIECE = 8
 F32, BF16 = jnp.float32, jnp.bfloat16
 HIGHEST = lax.Precision.HIGHEST
 MIB = 1 << 20
@@ -132,31 +133,55 @@
         out_ref[ky * 2 * Q : (ky + 1) * 2 * Q, :] = gathered[ky * lanes : (ky + 1) * lanes, :].T
 
 
-def forward_kernel(field, zt, y_table, out, gathered, *, lanes, block, group):
-    plane, part = pl.program_id(0), pl.program_id(1)
-    for c in range(0, block, group):
-        sums = dot(field[0, c : c + group].reshape(group * NY, CELLS), zt[...])
-        y_forward(sums, y_table[...], gathered, plane * C + part * block + c, lanes)
-
-    @pl.when((plane == pl.num_programs(0) - 1) & (part == pl.num_programs(1) - 1))
-    def _():
-        send_layout(gathered, out, lanes)
-
-
-def forward_planes(field, zt, y_table, block=C, group=16):
+def pieces(source, target, signals, plane, part):
+    here = (plane, pl.ds(part * PIECE, PIECE))
+    return pltpu.make_async_copy(
+        source.at[here], target.at[here], signals.at[plane * (C // PIECE) + part]
+    )
+
+
+def each_piece(planes):
+    return [(plane, part) for plane in range(planes) for part in range(C // PIECE)]
+
+
+def in_hbm():
+    return pl.BlockSpec(memory_space=pl.ANY)
+
+
+def in_vmem():
+    return pl.BlockSpec(memory_space=pltpu.VMEM)
+
+
+def forward_kernel(field, zt, y_table, out, buffer, gathered, arrived, *, lanes, group):
+    planes = field.shape[0]
+    for plane, part in each_piece(planes):
+        pieces(field, buffer, arrived, plane, part).start()
+
+    def one_plane(plane, _):
+        for c in range(0, C, group):
+            for part in range(c // PIECE, (c + group) // PIECE):
+                pieces(field, buffer, arrived, plane, part).wait()
+            values = buffer[plane, c : c + group].reshape(group * NY, CELLS)
+            y_forward(dot(values, zt[...]), y_table[...], gathered, plane * C + c, lanes)
+        return 0
+
+    lax.fori_loop(0, planes, one_plane, 0)
+    send_layout(gathered, out, lanes)
+
+
+def forward_planes(field, zt, y_table, group=C):
     planes = field.shape[0]
     lanes = planes * C
     return pl.pallas_call(
-        functools.partial(forward_kernel, lanes=lanes, block=block, group=group),
-        grid=(planes, C // block),
-        in_specs=[
-            pl.BlockSpec((1, block, NY, CELLS), lambda x, c: (x, c, 0, 0)),
-            whole(zt),
-            whole(y_table),
-        ],
-        out_specs=pl.BlockSpec((KY * 2 * Q, lanes), lambda x, c: (0, 0)),
+        functools.partial(forward_kernel, lanes=lanes, group=group),
+        in_specs=[in_hbm(), in_vmem(), in_vmem()],
+        out_specs=in_vmem(),
         out_shape=jax.ShapeDtypeStruct((KY * 2 * Q, lanes), F32),
-        scratch_shapes=[pltpu.VMEM((KY * lanes, 2 * Q), F32)],
+        scratch_shapes=[
+            pltpu.VMEM(field.shape, BF16),
+            pltpu.VMEM((KY * lanes, 2 * Q), F32),
+            pltpu.SemaphoreType.DMA((planes * (C // PIECE),)),
+        ],
         compiler_params=pltpu.CompilerParams(vmem_limit_bytes=56 * MIB),
         cost_estimate=pl.CostEstimate(flops=2 * 10**9, bytes_accessed=9 * MIB, transcendentals=0),
     )(field, zt, y_table)
@@ -242,6 +267,30 @@
         pieces = (total[:KX], total[KX:])
         mixed.append(pieces)
     to_planes(mixed, flat_out, q_block, devices, lanes, inverse[...], cosine[...], sine[...])
+
+
+def stage_kernel(*refs):
+    count = len(refs) // 2
+    sources, places, done = refs[:count], refs[count : 2 * count], refs[-1]
+    copies = [
+        pltpu.make_async_copy(source, place, done.at[i])
+        for i, (source, place) in enumerate(zip(sources, places))
+    ]
+    for copy in copies:
+        copy.start()
+    for copy in copies:
+        copy.wait()
+
+
+def stage(*arrays):
+    return pl.pallas_call(
+        stage_kernel,
+        in_specs=[pl.BlockSpec(memory_space=pl.ANY)] * len(arrays),
+        out_specs=[in_vmem() for _ in arrays],
+        out_shape=[pltpu.VMEM(array.shape, array.dtype) for array in arrays],
+        scratch_shapes=[pltpu.SemaphoreType.DMA((len(arrays),))],
+        cost_estimate=pl.CostEstimate(flops=0, bytes_accessed=6 * MIB, transcendentals=0),
+    )(*arrays)
 
 
 def whole(array):
@@ -482,17 +531,13 @@
         kept = total[...] * same[...].astype(F32)
         across = to_f32(kept, tiled, (((1,), (0,)), ((), ())))
         grads = to_f32(chosen, across, (((0,), (0,)), ((), ())))
-        group = lax.broadcasted_iota(jnp.int32, (8, 128), 1) // C
-        folded = jnp.zeros((8, 128), F32)
-        for g in range(4):
-            folded = jnp.where(group == g, grads[g * 8 : (g + 1) * 8], folded)
-        out[:8, :] = folded
+        out[:C, :] = grads
         lane_sums = to_f32(jnp.ones((8, 128), F32), bias_part[...], (((1,), (1,)), ((), ())))
         by_channel = (
             lax.broadcasted_iota(jnp.int32, (8 * C, 128), 0) // 8
             == lax.broadcasted_iota(jnp.int32, (8 * C, 128), 1)
         ).astype(F32)
-        out[8:, :] = to_f32(lane_sums, by_channel, (((1,), (0,)), ((), ())))
+        out[C:, :] = to_f32(lane_sums, by_channel, (((1,), (0,)), ((), ())))
 
 
 def pointwise_gradient(field, slope, bias_part, pick, same, parts=1):
@@ -502,8 +547,8 @@
         pointwise_kernel,
         grid=(field.shape[0], parts),
         in_specs=[block, block, whole(bias_part), whole(pick), whole(same)],
-        out_specs=pl.BlockSpec((16, 128), lambda x, y: (0, 0)),
-        out_shape=jax.ShapeDtypeStruct((16, 128), F32),
+        out_specs=pl.BlockSpec((C + 8, 128), lambda x, y: (0, 0)),
+        out_shape=jax.ShapeDtypeStruct((C + 8, 128), F32),
         scratch_shapes=[pltpu.VMEM((rows, rows), F32)],
         compiler_params=pltpu.CompilerParams(vmem_limit_bytes=56 * MIB),
         cost_estimate=pl.CostEstimate(flops=4 * 10**9, bytes_accessed=17 * MIB, transcendentals=0),
@@ -569,7 +614,7 @@
         send_layout(collected, spectra, lanes)
 
 
-def middle(back, early, cotangent, zt, zt_turned, y_back, y_table, block=C, group=16):
+def middle(back, early, cotangent, zt, zt_turned, y_back, y_table, block=C, group=C):
     planes = cotangent.shape[0]
     lanes = planes * C
     spec = pl.BlockSpec((1, block, NY, CELLS), lambda x, c: (x, c, 0, 0))
@@ -580,10 +625,10 @@
             whole(back),
             spec,
             spec,
-            whole(zt),
-            whole(zt_turned),
-            whole(y_back),
-            whole(y_table),
+            in_vmem(),
+            in_vmem(),
+            in_vmem(),
+            in_vmem(),
         ],
         out_specs=[
             spec,
@@ -601,42 +646,79 @@
             pltpu.VMEM((KY * lanes, 2 * Q), F32),
             pltpu.VMEM((KY * lanes, 2 * Q), F32),
         ],
-        compiler_params=pltpu.CompilerParams(vmem_limit_bytes=56 * MIB),
+        compiler_params=pltpu.CompilerParams(vmem_limit_bytes=50 * MIB),
         cost_estimate=pl.CostEstimate(
             flops=5 * 10**9, bytes_accessed=42 * MIB, transcendentals=8 * 10**6
         ),
     )(back, early, cotangent, zt, zt_turned, y_back, y_table)
 
 
-def last_kernel(back, early, zt_turned, y_back, out, gathered, *, lanes, block, group):
-    plane, part = pl.program_id(0), pl.program_id(1)
-
-    @pl.when((plane == 0) & (part == 0))
-    def _():
-        planes_layout(back, gathered, lanes)
-
-    for g in range(0, block, group):
-        own = y_inverse(gathered, y_back[...], plane * C + part * block + g, group, lanes)
-        total = dot(own, zt_turned[...]).reshape(group, NY, CELLS)
-        out[0, g : g + group] = (total + early[0, g : g + group].astype(F32)).astype(BF16)
-
-
-def last(back, early, zt_turned, y_back, block=C, group=16):
+def last_kernel(
+    back,
+    early,
+    zt_turned,
+    y_back,
+    sums,
+    out,
+    local_grad,
+    bias_grad,
+    buffer,
+    gathered,
+    arrived,
+    left,
+    *,
+    lanes,
+    group,
+):
+    planes = early.shape[0]
+    for plane, part in each_piece(planes):
+        pieces(early, buffer, arrived, plane, part).start()
+    planes_layout(back, gathered, lanes)
+    local_grad[...] = sums[:C, :C]
+    bias_grad[...] = sums[C : C + 1, :C]
+
+    def one_plane(plane, _):
+        for g in range(0, C, group):
+            own = y_inverse(gathered, y_back[...], plane * C + g, group, lanes)
+            total = dot(own, zt_turned[...]).reshape(group, NY, CELLS)
+            parts = range(g // PIECE, (g + group) // PIECE)
+            for part in parts:
+                pieces(early, buffer, arrived, plane, part).wait()
+            here = slice(g, g + group)
+            buffer[plane, here] = (total + buffer[plane, here].astype(F32)).astype(BF16)
+            for part in parts:
+                pieces(buffer, out, left, plane, part).start()
+        return 0
+
+    lax.fori_loop(0, planes, one_plane, 0)
+    for plane, part in each_piece(planes):
+        pieces(buffer, out, left, plane, part).wait()
+
+
+def last(back, early, zt_turned, y_back, sums, group=C):
     planes = early.shape[0]
     lanes = planes * C
-    spec = pl.BlockSpec((1, block, NY, CELLS), lambda x, c: (x, c, 0, 0))
-    return pl.pallas_call(
-        functools.partial(last_kernel, lanes=lanes, block=block, group=group),
-        grid=(planes, C // block),
-        in_specs=[whole(back), spec, whole(zt_turned), whole(y_back)],
-        out_specs=spec,
-        out_shape=jax.ShapeDtypeStruct(early.shape, BF16),
-        scratch_shapes=[pltpu.VMEM((KY * lanes, 2 * Q), F32)],
-        compiler_params=pltpu.CompilerParams(vmem_limit_bytes=56 * MIB),
+    signals = pltpu.SemaphoreType.DMA((planes * (C // PIECE),))
+    return pl.pallas_call(
+        functools.partial(last_kernel, lanes=lanes, group=group),
+        in_specs=[in_vmem(), in_hbm(), in_vmem(), in_vmem(), in_vmem()],
+        out_specs=[in_hbm(), in_vmem(), in_vmem()],
+        out_shape=[
+            jax.ShapeDtypeStruct(early.shape, BF16),
+            jax.ShapeDtypeStruct((C, C), F32),
+            jax.ShapeDtypeStruct((1, C), F32),
+        ],
+        scratch_shapes=[
+            pltpu.VMEM(early.shape, BF16),
+            pltpu.VMEM((KY * lanes, 2 * Q), F32),
+            signals,
+            signals,
+        ],
+        compiler_params=pltpu.CompilerParams(vmem_limit_bytes=52 * MIB),
         cost_estimate=pl.CostEstimate(
             flops=2 * 10**9, bytes_accessed=17 * MIB, transcendentals=0
         ),
-    )(back, early, zt_turned, y_back)
+    )(back, early, zt_turned, y_back, sums)
 
 
 def on_device(hidden_field, cotangent, spectral_weight, local_weight, local_bias):
@@ -655,6 +737,17 @@
     def exchange(value):
         return lax.all_to_all(value, "gx", split_axis=0, concat_axis=0, tiled=True)
 
+    def summed(value, span, end):
+        while span < end:
+            radix = 4 if 4 * span <= end else 2
+            others = [
+                lax.ppermute(value, "gx", [(d, d ^ (k * span)) for d in range(devices)])
+                for k in range(1, radix)
+            ]
+            value = sum(others, value)
+            span *= radix
+        return value
+
     def to_owner(spectra):
         return exchange(spectra.reshape(devices, 2, modes_here, lanes))
 
@@ -662,6 +755,7 @@
         return exchange(back).reshape(KY * 2 * Q, lanes)
 
     spectra = forward_planes(hidden_field, zt, y_table)
+    zt, zt_turned, y_table, y_back = stage(zt, zt_turned, y_table, y_back)
     early = local_term(hidden_field, local_weight.T, bias, pick, same)
     back, modes = mix_modes(to_owner(spectra), spectral_weight, tables)
     output, slope, dspectra, bias_part = middle(
@@ -669,16 +763,14 @@
     )
     total = pointwise_gradient(hidden_field, slope, bias_part, pick, same)
     dback, dmodes = adjoint_modes(to_owner(dspectra), spectral_weight, tables)
+    near = min(devices, 8)
+    total = summed(total, 1, near)
     dback, slope, total = lax.optimization_barrier((dback, slope, total))
     late = late_term(slope, local_weight, pick, same)
     grad_spectral = mode_gradient(modes, dmodes, mask)
-    span = 1
-    while span < devices:
-        total = total + lax.ppermute(total, "gx", [(d, d ^ span) for d in range(devices)])
-        span *= 2
-    grad_local = total[:8].reshape(8, 4, C).swapaxes(0, 1).reshape(C, C)
-    grad_bias = total[8, :C]
-    grad_field = last(to_slabs(dback), late, zt_turned, y_back)
+    total = summed(total, near, devices)
+    grad_field, grad_local, grad_bias = last(to_slabs(dback), late, zt_turned, y_back, total)
+    grad_bias = grad_bias.reshape(C)
     return (output, grad_field, grad_spectral, grad_local, grad_bias)
 
 

time: 181 us -> 172 us (0.950)
  starting transfers between devices: 22.3 us -> 18.9 us
  local copies, waits for them, and re-layouts: 6.43 us -> 3.91 us
  Pallas kernels: 81 us -> 78.5 us
    ppermute x5 -> x7, waiting for transfers between devices: 5.62 us -> 16.7 us  [summed(): lax.ppermute(value, 'gx', [(d, d ^ k * span) for d in range(devices)])]
    all_to_all x3, waiting for transfers between devices: 29.4 us -> 18.4 us  [exchange(): return lax.all_to_all(value, 'gx', split_axis=0, concat_axis=0, tiled=True)]
    ppermute x5 -> x7, starting transfers between devices: 11.3 us -> 7.81 us  [summed(): lax.ppermute(value, 'gx', [(d, d ^ k * span) for d in range(devices)])]
    pallas_call x2 -> x3, Pallas kernels: 19.1 us -> 17.3 us  [the longest x1 8.12 us: forward_planes(): pl.pallas_call(functools.partial(forward_kernel, lanes=lanes, group=group...]
    unnamed x23 -> x21, local copies, waits for them, and re-layouts: 4.28 us -> 2.97 us
  transfers between devices with their start and end apart: 8 -> 10, of which waited for: 5 -> 7; matrix products, arithmetic and copies ran while one was open for 2% -> 1% of each run, Pallas kernels for 19% -> 20%
where the time goes in v4:
time: 172 us
  Pallas kernels  78.5 us (46%)
  waiting for transfers between devices  35 us (20%)
  blocking collectives  33.6 us (20%)
  starting transfers between devices  18.9 us (11%)
  local copies, waits for them, and re-layouts  3.91 us (2%)
    all_to_all x1, blocking collectives, exchange(): return lax.all_to_all(value, 'gx', split_axis=0, concat_axis=0, tiled=True)  33.6 us
    pallas_call x1, Pallas kernels, middle(): pl.pallas_call(functools.partial(middle_kernel, lanes=lanes, block=block,...  19.5 us
    all_to_all x3, waiting for transfers between devices, exchange(): return lax.all_to_all(value, 'gx', split_axis=0, concat_axis=0, tiled=True)  18.4 us
    ppermute x7, waiting for transfers between devices, summed(): lax.ppermute(value, 'gx', [(d, d ^ k * span) for d in range(devices)])  16.7 us
    pallas_call x1, Pallas kernels, pointwise_gradient(): pl.pallas_call(pointwise_kernel, grid=(field.shape[0], parts), in_specs=[...  11.3 us
    all_to_all x3, starting transfers between devices, exchange(): return lax.all_to_all(value, 'gx', split_axis=0, concat_axis=0, tiled=True)  11.1 us
    pallas_call x1, Pallas kernels, local_term(): pl.pallas_call(local_kernel, grid=(field.shape[0], parts), in_specs=[bloc...  9.97 us
    pallas_call x1, Pallas kernels, late_term(): pl.pallas_call(late_kernel, grid=(slope.shape[0], parts), in_specs=[block...  9.86 us
  transfers between devices with their start and end apart: 10, of which 7 were waited for; matrix products, arithmetic and copies ran while one was open for 1% of the time, Pallas kernels for 20%

profile of v4, /device:TPU:0, one launch (start us, length us, event | category | flops | bytes accessed | tf_op | source)
XLA Modules:
  0.0 171.6 jit_solution(10465728423575098158)
XLA Ops:
  0.7 8.1 %shard_map.191 = f32[2048,128]{1,0:T(8,128)} custom-call(bf16[4,32,64,512]{3,2,1,0:T(8,128)(2,1)} %field.5, bf16[512,256]{1,0:T(8,128)(2,1)} %constant.22.clone.zt.refs_0_, bf16[32,128]{1,0:T(8,128)(2,1)} %constant.24.clone.y_table.refs_2_), custom_call_target="tpu_custom_call" | custom-call | flops 2000000000 | bytes 9437184 | tf_op jit(solution)/shard_map/pallas_call | solution.py:175
  8.9 33.6 %all_to_all.20.received = f32[32,2,32,128]{3,2,1,0:T(8,128)S(1)} all-to-all(f32[32,2,32,128]{3,2,1,0:T(8,128)} %bitcast.8), channel_id=1, replica_groups=mesh['groups'=1,'gx'=32] {'gx'}, dimensions={0} | all-to-all | bytes 2097152 | tf_op jit(solution)/shard_map/all_to_all | solution.py:738
  42.5 3.7 %shard_map.192 = (f32[32,2,32,128]{3,2,1,0:T(8,128)}, f32[32,32,128]{2,1,0:T(8,128)S(1)}) custom-call(f32[32,2,32,128]{3,2,1,0:T(8,128)S(1)} %all_to_all.20.received, bf16[32,2,32,512]{3,2,1,0:T(8,128)(2,1)S(1)} %copy-done.2, bf16[32,192]{1,0:T(8,128)(2,1)S(1)} %copy-done.4, bf16[64,96]{1,0:T(8,128)(2,1)S(1)} %copy-done.5, f32[16,128]{1,0:T(8,128)S(1)} %copy-done.6, ...), custom_call_target="tpu_custom_call" | custom-call | flops 1000000000 | bytes 5242880 | tf_op jit(solution)/shard_map/pallas_call | solution.py:311
  46.1 3.6 %all-to-all-start.1 = ((f32[32,2,32,128]{3,2,1,0:T(8,128)}), f32[32,2,32,128]{3,2,1,0:T(8,128)S(1)}, u32[]{:S(2)}, u32[]{:S(2)}) async-start(f32[32,2,32,128]{3,2,1,0:T(8,128)} %get-tuple-element.23), calls=%async_computation.1 | async-start | bytes 2097152 | tf_op jit(solution)/shard_map/all_to_all | solution.py:738
  52.5 10.0 %shard_map.193.early = bf16[4,32,64,512]{3,2,1,0:T(8,128)(2,1)} custom-call(bf16[4,32,64,512]{3,2,1,0:T(8,128)(2,1)} %field.5, bf16[32,32]{1,0:T(8,128)(2,1)} %bitcast.9, f32[512,1]{1,0:T(8,128)} %broadcast_in_dim_reshape.4.bias, bf16[512,32]{1,0:T(8,128)(2,1)} %constant.31.clone.pick, bf16[512,512]{1,0:T(8,128)(2,1)} %constant.32.clone.same), custom_call_target="tpu_custom_call" | custom-call | flops 4000000000 | bytes 17825792 | tf_op jit(solution)/shard_map/pallas_call | solution.py:464
  62.4 13.6 %all-to-all-done.1 = f32[32,2,32,128]{3,2,1,0:T(8,128)S(1)} async-done(((f32[32,2,32,128]{3,2,1,0:T(8,128)}), f32[32,2,32,128]{3,2,1,0:T(8,128)S(1)}, u32[]{:S(2)}, u32[]{:S(2)}) %all-to-all-start.1) | async-done | bytes 1048608 | tf_op jit(solution)/shard_map/all_to_all | solution.py:738
  76.0 19.5 %shard_map.195 = (bf16[4,32,64,512]{3,2,1,0:T(8,128)(2,1)}, bf16[4,32,64,512]{3,2,1,0:T(8,128)(2,1)}, f32[2048,128]{1,0:T(8,128)}, f32[256,128]{1,0:T(8,128)S(1)}) custom-call(f32[2048,128]{1,0:T(8,128)S(1)} %bitcast.7, bf16[4,32,64,512]{3,2,1,0:T(8,128)(2,1)} %shard_map.193.early, bf16[4,32,64,512]{3,2,1,0:T(8,128)(2,1)} %cotangent.1, ...), custom_call_target="tpu_custom_call" | custom-call | flops 5000000000 | bytes 44040192 | tf_op jit(solution)/shard_map/pallas_call | solution.py:621
  96.2 3.8 %all-to-all-start.2 = ((f32[32,2,32,128]{3,2,1,0:T(8,128)}), f32[32,2,32,128]{3,2,1,0:T(8,128)S(1)}, u32[]{:S(2)}, u32[]{:S(2)}) async-start(f32[32,2,32,128]{3,2,1,0:T(8,128)} %bitcast.3), calls=%async_computation.2 | async-start | bytes 2097152 | tf_op jit(solution)/shard_map/all_to_all | solution.py:738
  100.0 11.3 %shard_map.197 = f32[40,128]{1,0:T(8,128)} custom-call(bf16[4,32,64,512]{3,2,1,0:T(8,128)(2,1)} %field.5, bf16[4,32,64,512]{3,2,1,0:T(8,128)(2,1)} %get-tuple-element.34.slope, f32[256,128]{1,0:T(8,128)} %copy-done, bf16[512,32]{1,0:T(8,128)(2,1)} %constant.31.clone.pick, bf16[512,512]{1,0:T(8,128)(2,1)} %constant.32.clone.same), custom_call_target="tpu_custom_call" | custom-call | flops 4000000000 | bytes 17825792 | tf_op jit(solution)/shard_map/pallas_call | solution.py:546
  111.4 1.7 collective-permute-start.1
  113.2 2.2 %collective-permute-done.1 = f32[40,128]{1,0:T(8,128)S(1)} collective-permute-done((f32[40,128]{1,0:T(8,128)}, f32[40,128]{1,0:T(8,128)S(1)}, u32[]{:S(2)}, u32[]{:S(2)}) %collective-permute-start.1) | collective-permute-done | bytes 20512 | tf_op jit(solution)/shard_map/ppermute | solution.py:744
  117.2 1.5 collective-permute-start.3
  118.7 2.5 %collective-permute-done.3 = f32[40,128]{1,0:T(8,128)S(1)} collective-permute-done((f32[40,128]{1,0:T(8,128)S(1)}, f32[40,128]{1,0:T(8,128)S(1)}, u32[]{:S(2)}, u32[]{:S(2)}) %collective-permute-start.3) | collective-permute-done | bytes 20512 | tf_op jit(solution)/shard_map/ppermute | solution.py:744
  121.2 4.8 %all-to-all-done.2.received = f32[32,2,32,128]{3,2,1,0:T(8,128)S(1)} async-done(((f32[32,2,32,128]{3,2,1,0:T(8,128)}), f32[32,2,32,128]{3,2,1,0:T(8,128)S(1)}, u32[]{:S(2)}, u32[]{:S(2)}) %all-to-all-start.2) | async-done | bytes 1048608 | tf_op jit(solution)/shard_map/all_to_all | solution.py:738
  126.0 1.6 copy-done.3
  127.6 4.3 %shard_map.196 = (f32[32,2,32,128]{3,2,1,0:T(8,128)}, f32[32,32,128]{2,1,0:T(8,128)S(1)}) custom-call(f32[32,2,32,128]{3,2,1,0:T(8,128)S(1)} %all-to-all-done.2.received, bf16[32,2,32,512]{3,2,1,0:T(8,128)(2,1)S(1)} %copy-done.3, bf16[32,192]{1,0:T(8,128)(2,1)S(1)} %copy-done.4, bf16[64,96]{1,0:T(8,128)(2,1)S(1)} %copy-done.5, f32[16,128]{1,0:T(8,128)S(1)} %copy-done.6, ...), custom_call_target="tpu_custom_call" | custom-call | flops 1000000000 | bytes 5242880 | tf_op jit(solution)/shard_map/pallas_call | solution.py:367
  131.9 3.6 %all-to-all-start.3 = ((f32[32,2,32,128]{3,2,1,0:T(8,128)}), f32[32,2,32,128]{3,2,1,0:T(8,128)S(1)}, u32[]{:S(2)}, u32[]{:S(2)}) async-start(f32[32,2,32,128]{3,2,1,0:T(8,128)} %get-tuple-element.33), calls=%async_computation.3 | async-start | bytes 2097152 | tf_op jit(solution)/shard_map/all_to_all | solution.py:738
  135.5 1.8 %collective-permute-start.4 = (f32[40,128]{1,0:T(8,128)S(1)}, f32[40,128]{1,0:T(8,128)S(1)}, u32[]{:S(2)}, u32[]{:S(2)}) collective-permute-start(f32[40,128]{1,0:T(8,128)S(1)} %add.24), channel_id=1, source_target_pairs={{0,8},{1,9},{2,10},{3,11},{4,12},{5,13},{6,14},{7,15},{8,0},{9,1},... | collective-permute-start | bytes 61448 | tf_op jit(solution)/shard_map/ppermute | solution.py:744
  137.4 2.4 %collective-permute-start.5 = (f32[40,128]{1,0:T(8,128)S(1)}, f32[40,128]{1,0:T(8,128)S(1)}, u32[]{:S(2)}, u32[]{:S(2)}) collective-permute-start(f32[40,128]{1,0:T(8,128)S(1)} %add.24), channel_id=1, source_target_pairs={{0,16},{1,17},{2,18},{3,19},{4,20},{5,21},{6,22},{7,23},{8,24},{9,... | collective-permute-start | bytes 61448 | tf_op jit(solution)/shard_map/ppermute | solution.py:744
  140.0 9.9 %shard_map.198.early = bf16[4,32,64,512]{3,2,1,0:T(8,128)(2,1)} custom-call(bf16[4,32,64,512]{3,2,1,0:T(8,128)(2,1)} %get-tuple-element.34.slope, bf16[32,32]{1,0:T(8,128)(2,1)} %weight.5, bf16[512,32]{1,0:T(8,128)(2,1)} %constant.31.clone.pick, bf16[512,512]{1,0:T(8,128)(2,1)} %constant.32.clone.same), custom_call_target="tpu_custom_call" | custom-call | flops 4000000000 | bytes 17825792 | tf_op jit(solution)/shard_map/pallas_call | solution.py:492
  149.8 2.6 %shard_map.200 = f32[32,2,32,512]{3,2,1,0:T(8,128)} custom-call(f32[32,32,128]{2,1,0:T(8,128)S(1)} %get-tuple-element.37.modes, f32[32,32,128]{2,1,0:T(8,128)S(1)} %get-tuple-element.38.dmodes, f32[16,512]{1,0:T(8,128)S(1)} %copy-done.1), custom_call_target="tpu_custom_call" | custom-call | flops 100000000 | bytes 5242880 | tf_op jit(solution)/shard_map/pallas_call | solution.py:399
  152.5 1.5 collective-permute-done.4
  153.9 9.4 %collective-permute-done.5 = f32[40,128]{1,0:T(8,128)S(1)} collective-permute-done((f32[40,128]{1,0:T(8,128)S(1)}, f32[40,128]{1,0:T(8,128)S(1)}, u32[]{:S(2)}, u32[]{:S(2)}) %collective-permute-start.5) | collective-permute-done | bytes 20512 | tf_op jit(solution)/shard_map/ppermute | solution.py:744
  163.3 8.1 %shard_map.199 = (bf16[4,32,64,512]{3,2,1,0:T(8,128)(2,1)}, f32[32,32]{1,0:T(8,128)}, f32[1,32]{1,0:T(1,128)}) custom-call(f32[2048,128]{1,0:T(8,128)S(1)} %bitcast.6, bf16[4,32,64,512]{3,2,1,0:T(8,128)(2,1)} %shard_map.198.early, bf16[256,512]{1,0:T(8,128)(2,1)S(1)} %get-tuple-element.25.zt_turned, bf16[128,48]{1,0:T(8,128)(2,1)S(1)} %get-tuple-element.26.y_back, ...), custom_call_target="tpu_custom_call" | custom-call | flops 2000000000 | bytes 17825792 | tf_op jit(solution)/shard_map/pallas_call | solution.py:702
  (33 shorter events, 5.6 us)
Async XLA Ops:
  0.6 41.8 %copy-start.1 = (f32[16,512]{1,0:T(8,128)S(1)}, f32[16,512]{1,0:T(8,128)}, u32[]{:S(2)}) copy-start(f32[16,512]{1,0:T(8,128)} %constant.26.clone.mask) | copy-start | bytes 98308
  0.6 41.8 %copy-start.4 = (bf16[32,192]{1,0:T(8,128)(2,1)S(1)}, bf16[32,192]{1,0:T(8,128)(2,1)}, u32[]{:S(2)}) copy-start(bf16[32,192]{1,0:T(8,128)(2,1)} %constant.27.clone.forward) | copy-start | bytes 36868
  0.7 41.8 %copy-start.5 = (bf16[64,96]{1,0:T(8,128)(2,1)S(1)}, bf16[64,96]{1,0:T(8,128)(2,1)}, u32[]{:S(2)}) copy-start(bf16[64,96]{1,0:T(8,128)(2,1)} %constant.28.clone.inverse) | copy-start | bytes 36868
  0.7 41.8 %copy-start.6 = (f32[16,128]{1,0:T(8,128)S(1)}, f32[16,128]{1,0:T(8,128)}, u32[]{:S(2)}) copy-start(f32[16,128]{1,0:T(8,128)} %constant.29.clone.cosine) | copy-start | bytes 24580
  0.7 41.8 %copy-start.7 = (f32[16,128]{1,0:T(8,128)S(1)}, f32[16,128]{1,0:T(8,128)}, u32[]{:S(2)}) copy-start(f32[16,128]{1,0:T(8,128)} %constant.30.clone.sine) | copy-start | bytes 24580
  0.7 41.7 %copy-start.2 = (bf16[32,2,32,512]{3,2,1,0:T(8,128)(2,1)S(1)}, bf16[32,2,32,512]{3,2,1,0:T(8,128)(2,1)}, u32[]{:S(2)}) copy-start(bf16[32,2,32,512]{3,2,1,0:T(8,128)(2,1)} %weight.4) | copy-start | bytes 6291460
  0.7 49.0 %copy-start.9 = (f32[32]{0:T(128)S(1)}, f32[32]{0:T(128)}, u32[]{:S(2)}) copy-start(f32[32]{0:T(128)} %param.20) | copy-start | bytes 388
  0.7 50.0 %copy-start.8 = (bf16[32,32]{1,0:T(8,128)(2,1)S(1)}, bf16[32,32]{1,0:T(8,128)(2,1)}, u32[]{:S(2)}) copy-start(bf16[32,32]{1,0:T(8,128)(2,1)} %weight.5) | copy-start | bytes 6148
  46.1 29.9 %all-to-all-start.1 = ((f32[32,2,32,128]{3,2,1,0:T(8,128)}), f32[32,2,32,128]{3,2,1,0:T(8,128)S(1)}, u32[]{:S(2)}, u32[]{:S(2)}) async-start(f32[32,2,32,128]{3,2,1,0:T(8,128)} %get-tuple-element.23), calls=%async_computation.1 | async-start | bytes 2097152 | tf_op jit(solution)/shard_map/all_to_all | solution.py:738
  95.5 0.7 copy-start
  96.2 29.9 %all-to-all-start.2 = ((f32[32,2,32,128]{3,2,1,0:T(8,128)}), f32[32,2,32,128]{3,2,1,0:T(8,128)S(1)}, u32[]{:S(2)}, u32[]{:S(2)}) async-start(f32[32,2,32,128]{3,2,1,0:T(8,128)} %bitcast.3), calls=%async_computation.2 | async-start | bytes 2097152 | tf_op jit(solution)/shard_map/all_to_all | solution.py:738
  111.3 1.9 %collective-permute-start = (f32[40,128]{1,0:T(8,128)}, f32[40,128]{1,0:T(8,128)S(1)}, u32[]{:S(2)}, u32[]{:S(2)}) collective-permute-start(f32[40,128]{1,0:T(8,128)} %shard_map.197), channel_id=1, source_target_pairs={{0,1},{1,0},{2,3},{3,2},{4,5},{5,4},{6,7},{7,6},{8,9},{9,8},{10,11... | collective-permute-start | bytes 61448 | tf_op jit(solution)/shard_map/ppermute | solution.py:744
  111.4 4.0 %collective-permute-start.1 = (f32[40,128]{1,0:T(8,128)}, f32[40,128]{1,0:T(8,128)S(1)}, u32[]{:S(2)}, u32[]{:S(2)}) collective-permute-start(f32[40,128]{1,0:T(8,128)} %shard_map.197), channel_id=1, source_target_pairs={{0,2},{1,3},{2,0},{3,1},{4,6},{5,7},{6,4},{7,5},{8,10},{9,11},{10,... | collective-permute-start | bytes 61448 | tf_op jit(solution)/shard_map/ppermute | solution.py:744
  113.1 3.4 %collective-permute-start.2 = (f32[40,128]{1,0:T(8,128)}, f32[40,128]{1,0:T(8,128)S(1)}, u32[]{:S(2)}, u32[]{:S(2)}) collective-permute-start(f32[40,128]{1,0:T(8,128)} %shard_map.197), channel_id=1, source_target_pairs={{0,3},{1,2},{2,1},{3,0},{4,7},{5,6},{6,5},{7,4},{8,11},{9,10},{10,... | collective-permute-start | bytes 61448 | tf_op jit(solution)/shard_map/ppermute | solution.py:744
  117.2 4.0 %collective-permute-start.3 = (f32[40,128]{1,0:T(8,128)S(1)}, f32[40,128]{1,0:T(8,128)S(1)}, u32[]{:S(2)}, u32[]{:S(2)}) collective-permute-start(f32[40,128]{1,0:T(8,128)S(1)} %add_add_fusion.1), channel_id=1, source_target_pairs={{0,4},{1,5},{2,6},{3,7},{4,0},{5,1},{6,2},{7,3},{8,12},{9,13},{10,... | collective-permute-start | bytes 61448 | tf_op jit(solution)/shard_map/ppermute | solution.py:744
  126.0 1.6 copy-start.3
  131.9 31.4 %all-to-all-start.3 = ((f32[32,2,32,128]{3,2,1,0:T(8,128)}), f32[32,2,32,128]{3,2,1,0:T(8,128)S(1)}, u32[]{:S(2)}, u32[]{:S(2)}) async-start(f32[32,2,32,128]{3,2,1,0:T(8,128)} %get-tuple-element.33), calls=%async_computation.3 | async-start | bytes 2097152 | tf_op jit(solution)/shard_map/all_to_all | solution.py:738
  135.5 18.4 %collective-permute-start.4 = (f32[40,128]{1,0:T(8,128)S(1)}, f32[40,128]{1,0:T(8,128)S(1)}, u32[]{:S(2)}, u32[]{:S(2)}) collective-permute-start(f32[40,128]{1,0:T(8,128)S(1)} %add.24), channel_id=1, source_target_pairs={{0,8},{1,9},{2,10},{3,11},{4,12},{5,13},{6,14},{7,15},{8,0},{9,1},... | collective-permute-start | bytes 61448 | tf_op jit(solution)/shard_map/ppermute | solution.py:744
  137.4 25.9 %collective-permute-start.5 = (f32[40,128]{1,0:T(8,128)S(1)}, f32[40,128]{1,0:T(8,128)S(1)}, u32[]{:S(2)}, u32[]{:S(2)}) collective-permute-start(f32[40,128]{1,0:T(8,128)S(1)} %add.24), channel_id=1, source_target_pairs={{0,16},{1,17},{2,18},{3,19},{4,20},{5,21},{6,22},{7,23},{8,24},{9,... | collective-permute-start | bytes 61448 | tf_op jit(solution)/shard_map/ppermute | solution.py:744
  139.8 23.5 %collective-permute-start.6 = (f32[40,128]{1,0:T(8,128)S(1)}, f32[40,128]{1,0:T(8,128)S(1)}, u32[]{:S(2)}, u32[]{:S(2)}) collective-permute-start(f32[40,128]{1,0:T(8,128)S(1)} %add.24), channel_id=1, source_target_pairs={{0,24},{1,25},{2,26},{3,27},{4,28},{5,29},{6,30},{7,31},{8,16},{9,... | collective-permute-start | bytes 61448 | tf_op jit(solution)/shard_map/ppermute | solution.py:744

commit v5 on v4

--- a/solution.py
+++ b/solution.py
@@ -16,7 +16,8 @@
 Q = KZ * KT
 CELLS = NZ * NT
 YB = 16
-PIECE = 8
+PIECE = 16
+AHEAD = 4
 F32, BF16 = jnp.float32, jnp.bfloat16
 HIGHEST = lax.Precision.HIGHEST
 MIB = 1 << 20
@@ -140,8 +141,18 @@
     )
 
 
-def each_piece(planes):
-    return [(plane, part) for plane in range(planes) for part in range(C // PIECE)]
+def plane_copies(source, target, signals, plane):
+    return [pieces(source, target, signals, plane, part) for part in range(C // PIECE)]
+
+
+def start_plane(source, target, signals, plane):
+    for copy in plane_copies(source, target, signals, plane):
+        copy.start()
+
+
+def wait_plane(source, target, signals, plane):
+    for copy in plane_copies(source, target, signals, plane):
+        copy.wait()
 
 
 def in_hbm():
@@ -154,13 +165,17 @@
 
 def forward_kernel(field, zt, y_table, out, buffer, gathered, arrived, *, lanes, group):
     planes = field.shape[0]
-    for plane, part in each_piece(planes):
-        pieces(field, buffer, arrived, plane, part).start()
+    for plane in range(min(AHEAD, planes)):
+        start_plane(field, buffer, arrived, plane)
 
     def one_plane(plane, _):
+        wait_plane(field, buffer, arrived, plane)
+
+        @pl.when(plane + AHEAD < planes)
+        def _():
+            start_plane(field, buffer, arrived, plane + AHEAD)
+
         for c in range(0, C, group):
-            for part in range(c // PIECE, (c + group) // PIECE):
-                pieces(field, buffer, arrived, plane, part).wait()
             values = buffer[plane, c : c + group].reshape(group * NY, CELLS)
             y_forward(dot(values, zt[...]), y_table[...], gathered, plane * C + c, lanes)
         return 0
@@ -567,75 +582,78 @@
     slope_out,
     spectra,
     bias_grad,
+    left,
+    right,
     gathered,
     collected,
+    left_in,
+    right_in,
+    left_out,
+    right_out,
     *,
     lanes,
-    block,
     group,
 ):
-    plane, part = pl.program_id(0), pl.program_id(1)
-    first_step = (plane == 0) & (part == 0)
-    last_step = (plane == pl.num_programs(0) - 1) & (part == pl.num_programs(1) - 1)
-
-    @pl.when(first_step)
-    def _():
-        planes_layout(back, gathered, lanes)
-        bias_grad[...] = jnp.zeros_like(bias_grad)
-
+    planes = cotangent.shape[0]
+    for plane in range(min(AHEAD, planes)):
+        start_plane(early, left, left_in, plane)
+        start_plane(cotangent, right, right_in, plane)
+    planes_layout(back, gathered, lanes)
+    bias_grad[...] = jnp.zeros_like(bias_grad)
     half_root = 1.0 / math.sqrt(2.0)
-    for g in range(0, block, group):
-        first_row = plane * C + part * block + g
-        own = y_inverse(gathered, y_back[...], first_row, group, lanes)
-        pre = dot(own, zt_turned[...])
-        low = []
-        for c in range(group):
-            v = pre[c * NY : (c + 1) * NY] + early[0, g + c].astype(F32)
-            grade = cotangent[0, g + c].astype(F32)
-            normal = 0.5 + 0.5 * lax.erf(v * half_root)
-            out[0, g + c] = (v * normal).astype(BF16)
-            bell = jnp.exp(-0.5 * v * v) * (1.0 / math.sqrt(2.0 * math.pi))
-            slope = grade * (normal + v * bell)
-            low.append(slope.astype(BF16))
-            slope_out[0, g + c] = low[-1]
-            folded = slope[:, :128]
-            for column in range(128, CELLS, 128):
-                folded = folded + slope[:, column : column + 128]
-            total = folded[:8]
-            for row in range(8, NY, 8):
-                total = total + folded[row : row + 8]
-            r = pl.ds(pl.multiple_of((part * block + g + c) * 8, 8), 8)
-            bias_grad[r, :] += total
-        sums = dot(jnp.concatenate(low, axis=0), zt[...])
-        y_forward(sums, y_table[...], collected, first_row, lanes)
-
-    @pl.when(last_step)
-    def _():
-        send_layout(collected, spectra, lanes)
-
-
-def middle(back, early, cotangent, zt, zt_turned, y_back, y_table, block=C, group=C):
+
+    def one_plane(plane, _):
+        wait_plane(early, left, left_in, plane)
+        wait_plane(cotangent, right, right_in, plane)
+
+        @pl.when(plane + AHEAD < planes)
+        def _():
+            start_plane(early, left, left_in, plane + AHEAD)
+            start_plane(cotangent, right, right_in, plane + AHEAD)
+
+        for g in range(0, C, group):
+            own = y_inverse(gathered, y_back[...], plane * C + g, group, lanes)
+            pre = dot(own, zt_turned[...])
+            parts = range(g // PIECE, (g + group) // PIECE)
+            low = []
+            for c in range(group):
+                v = pre[c * NY : (c + 1) * NY] + left[plane, g + c].astype(F32)
+                grade = right[plane, g + c].astype(F32)
+                normal = 0.5 + 0.5 * lax.erf(v * half_root)
+                left[plane, g + c] = (v * normal).astype(BF16)
+                bell = jnp.exp(-0.5 * v * v) * (1.0 / math.sqrt(2.0 * math.pi))
+                slope = grade * (normal + v * bell)
+                low.append(slope.astype(BF16))
+                right[plane, g + c] = low[-1]
+                folded = slope[:, :128]
+                for column in range(128, CELLS, 128):
+                    folded = folded + slope[:, column : column + 128]
+                total = folded[:8]
+                for row in range(8, NY, 8):
+                    total = total + folded[row : row + 8]
+                bias_grad[(g + c) * 8 : (g + c + 1) * 8, :] += total
+            for part in parts:
+                pieces(left, out, left_out, plane, part).start()
+                pieces(right, slope_out, right_out, plane, part).start()
+            sums = dot(jnp.concatenate(low, axis=0), zt[...])
+            y_forward(sums, y_table[...], collected, plane * C + g, lanes)
+        return 0
+
+    lax.fori_loop(0, planes, one_plane, 0)
+    send_layout(collected, spectra, lanes)
+    for plane in range(planes):
+        wait_plane(left, out, left_out, plane)
+        wait_plane(right, slope_out, right_out, plane)
+
+
+def middle(back, early, cotangent, zt, zt_turned, y_back, y_table, group=C):
     planes = cotangent.shape[0]
     lanes = planes * C
-    spec = pl.BlockSpec((1, block, NY, CELLS), lambda x, c: (x, c, 0, 0))
-    return pl.pallas_call(
-        functools.partial(middle_kernel, lanes=lanes, block=block, group=group),
-        grid=(planes, C // block),
-        in_specs=[
-            whole(back),
-            spec,
-            spec,
-            in_vmem(),
-            in_vmem(),
-            in_vmem(),
-            in_vmem(),
-        ],
-        out_specs=[
-            spec,
-            spec,
-            pl.BlockSpec((KY * 2 * Q, lanes), lambda x, c: (0, 0)),
-            pl.BlockSpec((C * 8, 128), lambda x, c: (0, 0)),
-        ],
+    signals = pltpu.SemaphoreType.DMA((planes * (C // PIECE),))
+    return pl.pallas_call(
+        functools.partial(middle_kernel, lanes=lanes, group=group),
+        in_specs=[in_vmem(), in_hbm(), in_hbm()] + [in_vmem()] * 4,
+        out_specs=[in_hbm(), in_hbm(), in_vmem(), in_vmem()],
         out_shape=[
             jax.ShapeDtypeStruct(cotangent.shape, BF16),
             jax.ShapeDtypeStruct(cotangent.shape, BF16),
@@ -643,12 +661,18 @@
             jax.ShapeDtypeStruct((C * 8, 128), F32),
         ],
         scratch_shapes=[
+            pltpu.VMEM(cotangent.shape, BF16),
+            pltpu.VMEM(cotangent.shape, BF16),
             pltpu.VMEM((KY * lanes, 2 * Q), F32),
             pltpu.VMEM((KY * lanes, 2 * Q), F32),
+            signals,
+            signals,
+            signals,
+            signals,
         ],
-        compiler_params=pltpu.CompilerParams(vmem_limit_bytes=50 * MIB),
+        compiler_params=pltpu.CompilerParams(vmem_limit_bytes=48 * MIB),
         cost_estimate=pl.CostEstimate(
-            flops=5 * 10**9, bytes_accessed=42 * MIB, transcendentals=8 * 10**6
+            flops=5 * 10**9, bytes_accessed=34 * MIB, transcendentals=8 * 10**6
         ),
     )(back, early, cotangent, zt, zt_turned, y_back, y_table)
 
@@ -671,28 +695,31 @@
     group,
 ):
     planes = early.shape[0]
-    for plane, part in each_piece(planes):
-        pieces(early, buffer, arrived, plane, part).start()
+    for plane in range(min(AHEAD, planes)):
+        start_plane(early, buffer, arrived, plane)
     planes_layout(back, gathered, lanes)
     local_grad[...] = sums[:C, :C]
     bias_grad[...] = sums[C : C + 1, :C]
 
     def one_plane(plane, _):
+        wait_plane(early, buffer, arrived, plane)
+
+        @pl.when(plane + AHEAD < planes)
+        def _():
+            start_plane(early, buffer, arrived, plane + AHEAD)
+
         for g in range(0, C, group):
             own = y_inverse(gathered, y_back[...], plane * C + g, group, lanes)
             total = dot(own, zt_turned[...]).reshape(group, NY, CELLS)
-            parts = range(g // PIECE, (g + group) // PIECE)
-            for part in parts:
-                pieces(early, buffer, arrived, plane, part).wait()
             here = slice(g, g + group)
             buffer[plane, here] = (total + buffer[plane, here].astype(F32)).astype(BF16)
-            for part in parts:
+            for part in range(g // PIECE, (g + group) // PIECE):
                 pieces(buffer, out, left, plane, part).start()
         return 0
 
     lax.fori_loop(0, planes, one_plane, 0)
-    for plane, part in each_piece(planes):
-        pieces(buffer, out, left, plane, part).wait()
+    for plane in range(planes):
+        wait_plane(buffer, out, left, plane)
 
 
 def last(back, early, zt_turned, y_back, sums, group=C):

time: 172 us -> 171 us (level)
  no operation moved by 1% of the time
where the time goes in v5:
time: 171 us; the launch traced here: 170 us
  Pallas kernels  77.4 us (45%)
  waiting for transfers between devices  35 us (20%)
  blocking collectives  33.6 us (20%)
  starting transfers between devices  18.8 us (11%)
  local copies, waits for them, and re-layouts  3.91 us (2%)
    all_to_all x1, blocking collectives, exchange(): return lax.all_to_all(value, 'gx', split_axis=0, concat_axis=0, tiled=True)  33.6 us
    pallas_call x1, Pallas kernels, middle(): pl.pallas_call(functools.partial(middle_kernel, lanes=lanes, group=group)...  19 us
    all_to_all x3, waiting for transfers between devices, exchange(): return lax.all_to_all(value, 'gx', split_axis=0, concat_axis=0, tiled=True)  18.4 us
    ppermute x7, waiting for transfers between devices, summed(): lax.ppermute(value, 'gx', [(d, d ^ k * span) for d in range(devices)])  16.7 us
    pallas_call x1, Pallas kernels, pointwise_gradient(): pl.pallas_call(pointwise_kernel, grid=(field.shape[0], parts), in_specs=[...  11.3 us
    all_to_all x3, starting transfers between devices, exchange(): return lax.all_to_all(value, 'gx', split_axis=0, concat_axis=0, tiled=True)  11 us
    pallas_call x1, Pallas kernels, local_term(): pl.pallas_call(local_kernel, grid=(field.shape[0], parts), in_specs=[bloc...  9.97 us
    pallas_call x1, Pallas kernels, late_term(): pl.pallas_call(late_kernel, grid=(slope.shape[0], parts), in_specs=[block...  9.86 us
  transfers between devices with their start and end apart: 10, of which 7 were waited for; matrix products, arithmetic and copies ran while one was open for 1% of the time, Pallas kernels for 20%

profile of v5, /device:TPU:0, one launch (start us, length us, event | category | flops | bytes accessed | tf_op | source)
XLA Modules:
  0.0 170.5 jit_solution(2735327214352119162)
XLA Ops:
  0.7 8.1 %shard_map.191 = f32[2048,128]{1,0:T(8,128)} custom-call(bf16[4,32,64,512]{3,2,1,0:T(8,128)(2,1)} %field.5, bf16[512,256]{1,0:T(8,128)(2,1)} %constant.22.clone.zt.refs_0_, bf16[32,128]{1,0:T(8,128)(2,1)} %constant.24.clone.y_table.refs_2_), custom_call_target="tpu_custom_call" | custom-call | flops 2000000000 | bytes 9437184 | tf_op jit(solution)/shard_map/pallas_call | solution.py:190
  8.8 33.6 %all_to_all.20.received = f32[32,2,32,128]{3,2,1,0:T(8,128)S(1)} all-to-all(f32[32,2,32,128]{3,2,1,0:T(8,128)} %bitcast.8), channel_id=1, replica_groups=mesh['groups'=1,'gx'=32] {'gx'}, dimensions={0} | all-to-all | bytes 2097152 | tf_op jit(solution)/shard_map/all_to_all | solution.py:765
  42.4 3.7 %shard_map.192 = (f32[32,2,32,128]{3,2,1,0:T(8,128)}, f32[32,32,128]{2,1,0:T(8,128)S(1)}) custom-call(f32[32,2,32,128]{3,2,1,0:T(8,128)S(1)} %all_to_all.20.received, bf16[32,2,32,512]{3,2,1,0:T(8,128)(2,1)S(1)} %copy-done.2, bf16[32,192]{1,0:T(8,128)(2,1)S(1)} %copy-done.4, bf16[64,96]{1,0:T(8,128)(2,1)S(1)} %copy-done.5, f32[16,128]{1,0:T(8,128)S(1)} %copy-done.6, ...), custom_call_target="tpu_custom_call" | custom-call | flops 1000000000 | bytes 5242880 | tf_op jit(solution)/shard_map/pallas_call | solution.py:326
  46.1 3.6 %all-to-all-start.1 = ((f32[32,2,32,128]{3,2,1,0:T(8,128)}), f32[32,2,32,128]{3,2,1,0:T(8,128)S(1)}, u32[]{:S(2)}, u32[]{:S(2)}) async-start(f32[32,2,32,128]{3,2,1,0:T(8,128)} %get-tuple-element.23), calls=%async_computation.1 | async-start | bytes 2097152 | tf_op jit(solution)/shard_map/all_to_all | solution.py:765
  52.4 10.0 %shard_map.193.early = bf16[4,32,64,512]{3,2,1,0:T(8,128)(2,1)} custom-call(bf16[4,32,64,512]{3,2,1,0:T(8,128)(2,1)} %field.5, bf16[32,32]{1,0:T(8,128)(2,1)} %bitcast.9, f32[512,1]{1,0:T(8,128)} %broadcast_in_dim_reshape.4.bias, bf16[512,32]{1,0:T(8,128)(2,1)} %constant.31.clone.pick, bf16[512,512]{1,0:T(8,128)(2,1)} %constant.32.clone.same), custom_call_target="tpu_custom_call" | custom-call | flops 4000000000 | bytes 17825792 | tf_op jit(solution)/shard_map/pallas_call | solution.py:479
  62.4 13.6 %all-to-all-done.1 = f32[32,2,32,128]{3,2,1,0:T(8,128)S(1)} async-done(((f32[32,2,32,128]{3,2,1,0:T(8,128)}), f32[32,2,32,128]{3,2,1,0:T(8,128)S(1)}, u32[]{:S(2)}, u32[]{:S(2)}) %all-to-all-start.1) | async-done | bytes 1048608 | tf_op jit(solution)/shard_map/all_to_all | solution.py:765
  75.9 19.0 %shard_map.195 = (bf16[4,32,64,512]{3,2,1,0:T(8,128)(2,1)}, bf16[4,32,64,512]{3,2,1,0:T(8,128)(2,1)}, f32[2048,128]{1,0:T(8,128)}, f32[256,128]{1,0:T(8,128)S(1)}) custom-call(f32[2048,128]{1,0:T(8,128)S(1)} %bitcast.7, bf16[4,32,64,512]{3,2,1,0:T(8,128)(2,1)} %shard_map.193.early, bf16[4,32,64,512]{3,2,1,0:T(8,128)(2,1)} %cotangent.1, ...), custom_call_target="tpu_custom_call" | custom-call | flops 5000000000 | bytes 35651584 | tf_op jit(solution)/shard_map/pallas_call | solution.py:653
  95.6 3.8 %all-to-all-start.2 = ((f32[32,2,32,128]{3,2,1,0:T(8,128)}), f32[32,2,32,128]{3,2,1,0:T(8,128)S(1)}, u32[]{:S(2)}, u32[]{:S(2)}) async-start(f32[32,2,32,128]{3,2,1,0:T(8,128)} %bitcast.3), calls=%async_computation.2 | async-start | bytes 2097152 | tf_op jit(solution)/shard_map/all_to_all | solution.py:765
  99.4 11.3 %shard_map.197 = f32[40,128]{1,0:T(8,128)} custom-call(bf16[4,32,64,512]{3,2,1,0:T(8,128)(2,1)} %field.5, bf16[4,32,64,512]{3,2,1,0:T(8,128)(2,1)} %get-tuple-element.34.slope, f32[256,128]{1,0:T(8,128)} %copy-done, bf16[512,32]{1,0:T(8,128)(2,1)} %constant.31.clone.pick, bf16[512,512]{1,0:T(8,128)(2,1)} %constant.32.clone.same), custom_call_target="tpu_custom_call" | custom-call | flops 4000000000 | bytes 17825792 | tf_op jit(solution)/shard_map/pallas_call | solution.py:561
  110.8 1.7 collective-permute-start.1
  112.6 2.2 %collective-permute-done.1 = f32[40,128]{1,0:T(8,128)S(1)} collective-permute-done((f32[40,128]{1,0:T(8,128)}, f32[40,128]{1,0:T(8,128)S(1)}, u32[]{:S(2)}, u32[]{:S(2)}) %collective-permute-start.1) | collective-permute-done | bytes 20512 | tf_op jit(solution)/shard_map/ppermute | solution.py:771
  116.6 1.5 collective-permute-start.3
  118.1 2.5 %collective-permute-done.3 = f32[40,128]{1,0:T(8,128)S(1)} collective-permute-done((f32[40,128]{1,0:T(8,128)S(1)}, f32[40,128]{1,0:T(8,128)S(1)}, u32[]{:S(2)}, u32[]{:S(2)}) %collective-permute-start.3) | collective-permute-done | bytes 20512 | tf_op jit(solution)/shard_map/ppermute | solution.py:771
  120.7 4.8 %all-to-all-done.2.received = f32[32,2,32,128]{3,2,1,0:T(8,128)S(1)} async-done(((f32[32,2,32,128]{3,2,1,0:T(8,128)}), f32[32,2,32,128]{3,2,1,0:T(8,128)S(1)}, u32[]{:S(2)}, u32[]{:S(2)}) %all-to-all-start.2) | async-done | bytes 1048608 | tf_op jit(solution)/shard_map/all_to_all | solution.py:765
  125.5 1.6 copy-done.3
  127.0 4.3 %shard_map.196 = (f32[32,2,32,128]{3,2,1,0:T(8,128)}, f32[32,32,128]{2,1,0:T(8,128)S(1)}) custom-call(f32[32,2,32,128]{3,2,1,0:T(8,128)S(1)} %all-to-all-done.2.received, bf16[32,2,32,512]{3,2,1,0:T(8,128)(2,1)S(1)} %copy-done.3, bf16[32,192]{1,0:T(8,128)(2,1)S(1)} %copy-done.4, bf16[64,96]{1,0:T(8,128)(2,1)S(1)} %copy-done.5, f32[16,128]{1,0:T(8,128)S(1)} %copy-done.6, ...), custom_call_target="tpu_custom_call" | custom-call | flops 1000000000 | bytes 5242880 | tf_op jit(solution)/shard_map/pallas_call | solution.py:382
  131.3 3.6 %all-to-all-start.3 = ((f32[32,2,32,128]{3,2,1,0:T(8,128)}), f32[32,2,32,128]{3,2,1,0:T(8,128)S(1)}, u32[]{:S(2)}, u32[]{:S(2)}) async-start(f32[32,2,32,128]{3,2,1,0:T(8,128)} %get-tuple-element.33), calls=%async_computation.3 | async-start | bytes 2097152 | tf_op jit(solution)/shard_map/all_to_all | solution.py:765
  134.9 1.8 %collective-permute-start.4 = (f32[40,128]{1,0:T(8,128)S(1)}, f32[40,128]{1,0:T(8,128)S(1)}, u32[]{:S(2)}, u32[]{:S(2)}) collective-permute-start(f32[40,128]{1,0:T(8,128)S(1)} %add.24), channel_id=1, source_target_pairs={{0,8},{1,9},{2,10},{3,11},{4,12},{5,13},{6,14},{7,15},{8,0},{9,1},... | collective-permute-start | bytes 61448 | tf_op jit(solution)/shard_map/ppermute | solution.py:771
  136.8 2.4 %collective-permute-start.5 = (f32[40,128]{1,0:T(8,128)S(1)}, f32[40,128]{1,0:T(8,128)S(1)}, u32[]{:S(2)}, u32[]{:S(2)}) collective-permute-start(f32[40,128]{1,0:T(8,128)S(1)} %add.24), channel_id=1, source_target_pairs={{0,16},{1,17},{2,18},{3,19},{4,20},{5,21},{6,22},{7,23},{8,24},{9,... | collective-permute-start | bytes 61448 | tf_op jit(solution)/shard_map/ppermute | solution.py:771
  139.4 9.9 %shard_map.198.early = bf16[4,32,64,512]{3,2,1,0:T(8,128)(2,1)} custom-call(bf16[4,32,64,512]{3,2,1,0:T(8,128)(2,1)} %get-tuple-element.34.slope, bf16[32,32]{1,0:T(8,128)(2,1)} %weight.5, bf16[512,32]{1,0:T(8,128)(2,1)} %constant.31.clone.pick, bf16[512,512]{1,0:T(8,128)(2,1)} %constant.32.clone.same), custom_call_target="tpu_custom_call" | custom-call | flops 4000000000 | bytes 17825792 | tf_op jit(solution)/shard_map/pallas_call | solution.py:507
  149.3 2.6 %shard_map.200 = f32[32,2,32,512]{3,2,1,0:T(8,128)} custom-call(f32[32,32,128]{2,1,0:T(8,128)S(1)} %get-tuple-element.37.modes, f32[32,32,128]{2,1,0:T(8,128)S(1)} %get-tuple-element.38.dmodes, f32[16,512]{1,0:T(8,128)S(1)} %copy-done.1), custom_call_target="tpu_custom_call" | custom-call | flops 100000000 | bytes 5242880 | tf_op jit(solution)/shard_map/pallas_call | solution.py:414
  151.9 1.5 collective-permute-done.4
  153.3 9.4 %collective-permute-done.5 = f32[40,128]{1,0:T(8,128)S(1)} collective-permute-done((f32[40,128]{1,0:T(8,128)S(1)}, f32[40,128]{1,0:T(8,128)S(1)}, u32[]{:S(2)}, u32[]{:S(2)}) %collective-permute-start.5) | collective-permute-done | bytes 20512 | tf_op jit(solution)/shard_map/ppermute | solution.py:771
  162.7 7.6 %shard_map.199 = (bf16[4,32,64,512]{3,2,1,0:T(8,128)(2,1)}, f32[32,32]{1,0:T(8,128)}, f32[1,32]{1,0:T(1,128)}) custom-call(f32[2048,128]{1,0:T(8,128)S(1)} %bitcast.6, bf16[4,32,64,512]{3,2,1,0:T(8,128)(2,1)} %shard_map.198.early, bf16[256,512]{1,0:T(8,128)(2,1)S(1)} %get-tuple-element.25.zt_turned, bf16[128,48]{1,0:T(8,128)(2,1)S(1)} %get-tuple-element.26.y_back, ...), custom_call_target="tpu_custom_call" | custom-call | flops 2000000000 | bytes 17825792 | tf_op jit(solution)/shard_map/pallas_call | solution.py:729
  (33 shorter events, 5.6 us)
Async XLA Ops:
  0.6 41.7 %copy-start.1 = (f32[16,512]{1,0:T(8,128)S(1)}, f32[16,512]{1,0:T(8,128)}, u32[]{:S(2)}) copy-start(f32[16,512]{1,0:T(8,128)} %constant.26.clone.mask) | copy-start | bytes 98308
  0.6 41.7 %copy-start.4 = (bf16[32,192]{1,0:T(8,128)(2,1)S(1)}, bf16[32,192]{1,0:T(8,128)(2,1)}, u32[]{:S(2)}) copy-start(bf16[32,192]{1,0:T(8,128)(2,1)} %constant.27.clone.forward) | copy-start | bytes 36868
  0.7 41.7 %copy-start.5 = (bf16[64,96]{1,0:T(8,128)(2,1)S(1)}, bf16[64,96]{1,0:T(8,128)(2,1)}, u32[]{:S(2)}) copy-start(bf16[64,96]{1,0:T(8,128)(2,1)} %constant.28.clone.inverse) | copy-start | bytes 36868
  0.7 41.7 %copy-start.6 = (f32[16,128]{1,0:T(8,128)S(1)}, f32[16,128]{1,0:T(8,128)}, u32[]{:S(2)}) copy-start(f32[16,128]{1,0:T(8,128)} %constant.29.clone.cosine) | copy-start | bytes 24580
  0.7 41.7 %copy-start.7 = (f32[16,128]{1,0:T(8,128)S(1)}, f32[16,128]{1,0:T(8,128)}, u32[]{:S(2)}) copy-start(f32[16,128]{1,0:T(8,128)} %constant.30.clone.sine) | copy-start | bytes 24580
  0.7 41.7 %copy-start.2 = (bf16[32,2,32,512]{3,2,1,0:T(8,128)(2,1)S(1)}, bf16[32,2,32,512]{3,2,1,0:T(8,128)(2,1)}, u32[]{:S(2)}) copy-start(bf16[32,2,32,512]{3,2,1,0:T(8,128)(2,1)} %weight.4) | copy-start | bytes 6291460
  0.7 49.0 %copy-start.9 = (f32[32]{0:T(128)S(1)}, f32[32]{0:T(128)}, u32[]{:S(2)}) copy-start(f32[32]{0:T(128)} %param.20) | copy-start | bytes 388
  0.7 49.9 %copy-start.8 = (bf16[32,32]{1,0:T(8,128)(2,1)S(1)}, bf16[32,32]{1,0:T(8,128)(2,1)}, u32[]{:S(2)}) copy-start(bf16[32,32]{1,0:T(8,128)(2,1)} %weight.5) | copy-start | bytes 6148
  46.1 29.9 %all-to-all-start.1 = ((f32[32,2,32,128]{3,2,1,0:T(8,128)}), f32[32,2,32,128]{3,2,1,0:T(8,128)S(1)}, u32[]{:S(2)}, u32[]{:S(2)}) async-start(f32[32,2,32,128]{3,2,1,0:T(8,128)} %get-tuple-element.23), calls=%async_computation.1 | async-start | bytes 2097152 | tf_op jit(solution)/shard_map/all_to_all | solution.py:765
  94.9 0.7 copy-start
  95.6 29.9 %all-to-all-start.2 = ((f32[32,2,32,128]{3,2,1,0:T(8,128)}), f32[32,2,32,128]{3,2,1,0:T(8,128)S(1)}, u32[]{:S(2)}, u32[]{:S(2)}) async-start(f32[32,2,32,128]{3,2,1,0:T(8,128)} %bitcast.3), calls=%async_computation.2 | async-start | bytes 2097152 | tf_op jit(solution)/shard_map/all_to_all | solution.py:765
  110.7 1.9 %collective-permute-start = (f32[40,128]{1,0:T(8,128)}, f32[40,128]{1,0:T(8,128)S(1)}, u32[]{:S(2)}, u32[]{:S(2)}) collective-permute-start(f32[40,128]{1,0:T(8,128)} %shard_map.197), channel_id=1, source_target_pairs={{0,1},{1,0},{2,3},{3,2},{4,5},{5,4},{6,7},{7,6},{8,9},{9,8},{10,11... | collective-permute-start | bytes 61448 | tf_op jit(solution)/shard_map/ppermute | solution.py:771
  110.8 4.0 %collective-permute-start.1 = (f32[40,128]{1,0:T(8,128)}, f32[40,128]{1,0:T(8,128)S(1)}, u32[]{:S(2)}, u32[]{:S(2)}) collective-permute-start(f32[40,128]{1,0:T(8,128)} %shard_map.197), channel_id=1, source_target_pairs={{0,2},{1,3},{2,0},{3,1},{4,6},{5,7},{6,4},{7,5},{8,10},{9,11},{10,... | collective-permute-start | bytes 61448 | tf_op jit(solution)/shard_map/ppermute | solution.py:771
  112.5 3.4 %collective-permute-start.2 = (f32[40,128]{1,0:T(8,128)}, f32[40,128]{1,0:T(8,128)S(1)}, u32[]{:S(2)}, u32[]{:S(2)}) collective-permute-start(f32[40,128]{1,0:T(8,128)} %shard_map.197), channel_id=1, source_target_pairs={{0,3},{1,2},{2,1},{3,0},{4,7},{5,6},{6,5},{7,4},{8,11},{9,10},{10,... | collective-permute-start | bytes 61448 | tf_op jit(solution)/shard_map/ppermute | solution.py:771
  116.6 4.0 %collective-permute-start.3 = (f32[40,128]{1,0:T(8,128)S(1)}, f32[40,128]{1,0:T(8,128)S(1)}, u32[]{:S(2)}, u32[]{:S(2)}) collective-permute-start(f32[40,128]{1,0:T(8,128)S(1)} %add_add_fusion.1), channel_id=1, source_target_pairs={{0,4},{1,5},{2,6},{3,7},{4,0},{5,1},{6,2},{7,3},{8,12},{9,13},{10,... | collective-permute-start | bytes 61448 | tf_op jit(solution)/shard_map/ppermute | solution.py:771
  125.5 1.6 copy-start.3
  131.3 31.4 %all-to-all-start.3 = ((f32[32,2,32,128]{3,2,1,0:T(8,128)}), f32[32,2,32,128]{3,2,1,0:T(8,128)S(1)}, u32[]{:S(2)}, u32[]{:S(2)}) async-start(f32[32,2,32,128]{3,2,1,0:T(8,128)} %get-tuple-element.33), calls=%async_computation.3 | async-start | bytes 2097152 | tf_op jit(solution)/shard_map/all_to_all | solution.py:765
  134.9 18.4 %collective-permute-start.4 = (f32[40,128]{1,0:T(8,128)S(1)}, f32[40,128]{1,0:T(8,128)S(1)}, u32[]{:S(2)}, u32[]{:S(2)}) collective-permute-start(f32[40,128]{1,0:T(8,128)S(1)} %add.24), channel_id=1, source_target_pairs={{0,8},{1,9},{2,10},{3,11},{4,12},{5,13},{6,14},{7,15},{8,0},{9,1},... | collective-permute-start | bytes 61448 | tf_op jit(solution)/shard_map/ppermute | solution.py:771
  136.8 25.9 %collective-permute-start.5 = (f32[40,128]{1,0:T(8,128)S(1)}, f32[40,128]{1,0:T(8,128)S(1)}, u32[]{:S(2)}, u32[]{:S(2)}) collective-permute-start(f32[40,128]{1,0:T(8,128)S(1)} %add.24), channel_id=1, source_target_pairs={{0,16},{1,17},{2,18},{3,19},{4,20},{5,21},{6,22},{7,23},{8,24},{9,... | collective-permute-start | bytes 61448 | tf_op jit(solution)/shard_map/ppermute | solution.py:771
  139.2 23.5 %collective-permute-start.6 = (f32[40,128]{1,0:T(8,128)S(1)}, f32[40,128]{1,0:T(8,128)S(1)}, u32[]{:S(2)}, u32[]{:S(2)}) collective-permute-start(f32[40,128]{1,0:T(8,128)S(1)} %add.24), channel_id=1, source_target_pairs={{0,24},{1,25},{2,26},{3,27},{4,28},{5,29},{6,30},{7,31},{8,16},{9,... | collective-permute-start | bytes 61448 | tf_op jit(solution)/shard_map/ppermute | solution.py:771

commit v6 on v5

--- a/solution.py
+++ b/solution.py
@@ -790,7 +790,7 @@
     )
     total = pointwise_gradient(hidden_field, slope, bias_part, pick, same)
     dback, dmodes = adjoint_modes(to_owner(dspectra), spectral_weight, tables)
-    near = min(devices, 8)
+    near = min(devices, 16)
     total = summed(total, 1, near)
     dback, slope, total = lax.optimization_barrier((dback, slope, total))
     late = late_term(slope, local_weight, pick, same)

time: 171 us -> 170 us (level)
    all_to_all x3, waiting for transfers between devices: 18.4 us -> 14.4 us  [exchange(): return lax.all_to_all(value, 'gx', split_axis=0, concat_axis=0, tiled=True)]
    ppermute x7, waiting for transfers between devices: 16.7 us -> 19.6 us  [summed(): lax.ppermute(value, 'gx', [(d, d ^ k * span) for d in range(devices)])]
  transfers between devices with their start and end apart: 10 -> 10, of which waited for: 7 -> 8; matrix products, arithmetic and copies ran while one was open for 1% -> 1% of each run, Pallas kernels for 20% -> 21%
where the time goes in v6:
time: 170 us
  Pallas kernels  77.4 us (46%)
  waiting for transfers between devices  34.1 us (20%)
  blocking collectives  33.6 us (20%)
  starting transfers between devices  19.2 us (11%)
  local copies, waits for them, and re-layouts  3.91 us (2%)
    all_to_all x1, blocking collectives, exchange(): return lax.all_to_all(value, 'gx', split_axis=0, concat_axis=0, tiled=True)  33.6 us
    ppermute x7, waiting for transfers between devices, summed(): lax.ppermute(value, 'gx', [(d, d ^ k * span) for d in range(devices)])  19.6 us
    pallas_call x1, Pallas kernels, middle(): pl.pallas_call(functools.partial(middle_kernel, lanes=lanes, group=group)...  19 us
    all_to_all x3, waiting for transfers between devices, exchange(): return lax.all_to_all(value, 'gx', split_axis=0, concat_axis=0, tiled=True)  14.4 us
    pallas_call x1, Pallas kernels, pointwise_gradient(): pl.pallas_call(pointwise_kernel, grid=(field.shape[0], parts), in_specs=[...  11.3 us
    all_to_all x3, starting transfers between devices, exchange(): return lax.all_to_all(value, 'gx', split_axis=0, concat_axis=0, tiled=True)  11 us
    pallas_call x1, Pallas kernels, local_term(): pl.pallas_call(local_kernel, grid=(field.shape[0], parts), in_specs=[bloc...  9.97 us
    pallas_call x1, Pallas kernels, late_term(): pl.pallas_call(late_kernel, grid=(slope.shape[0], parts), in_specs=[block...  9.86 us
  transfers between devices with their start and end apart: 10, of which 8 were waited for; matrix products, arithmetic and copies ran while one was open for 1% of the time, Pallas kernels for 21%

profile of v6, /device:TPU:0, one launch (start us, length us, event | category | flops | bytes accessed | tf_op | source)
XLA Modules:
  0.0 169.8 jit_solution(8364785398841864168)
XLA Ops:
  0.7 8.1 %shard_map.191 = f32[2048,128]{1,0:T(8,128)} custom-call(bf16[4,32,64,512]{3,2,1,0:T(8,128)(2,1)} %field.5, bf16[512,256]{1,0:T(8,128)(2,1)} %constant.22.clone.zt.refs_0_, bf16[32,128]{1,0:T(8,128)(2,1)} %constant.24.clone.y_table.refs_2_), custom_call_target="tpu_custom_call" | custom-call | flops 2000000000 | bytes 9437184 | tf_op jit(solution)/shard_map/pallas_call | solution.py:190
  8.8 33.6 %all_to_all.20.received = f32[32,2,32,128]{3,2,1,0:T(8,128)S(1)} all-to-all(f32[32,2,32,128]{3,2,1,0:T(8,128)} %bitcast.8), channel_id=1, replica_groups=mesh['groups'=1,'gx'=32] {'gx'}, dimensions={0} | all-to-all | bytes 2097152 | tf_op jit(solution)/shard_map/all_to_all | solution.py:765
  42.4 3.7 %shard_map.192 = (f32[32,2,32,128]{3,2,1,0:T(8,128)}, f32[32,32,128]{2,1,0:T(8,128)S(1)}) custom-call(f32[32,2,32,128]{3,2,1,0:T(8,128)S(1)} %all_to_all.20.received, bf16[32,2,32,512]{3,2,1,0:T(8,128)(2,1)S(1)} %copy-done.2, bf16[32,192]{1,0:T(8,128)(2,1)S(1)} %copy-done.4, bf16[64,96]{1,0:T(8,128)(2,1)S(1)} %copy-done.5, f32[16,128]{1,0:T(8,128)S(1)} %copy-done.6, ...), custom_call_target="tpu_custom_call" | custom-call | flops 1000000000 | bytes 5242880 | tf_op jit(solution)/shard_map/pallas_call | solution.py:326
  46.1 3.6 %all-to-all-start.1 = ((f32[32,2,32,128]{3,2,1,0:T(8,128)}), f32[32,2,32,128]{3,2,1,0:T(8,128)S(1)}, u32[]{:S(2)}, u32[]{:S(2)}) async-start(f32[32,2,32,128]{3,2,1,0:T(8,128)} %get-tuple-element.23), calls=%async_computation.1 | async-start | bytes 2097152 | tf_op jit(solution)/shard_map/all_to_all | solution.py:765
  52.4 10.0 %shard_map.193.early = bf16[4,32,64,512]{3,2,1,0:T(8,128)(2,1)} custom-call(bf16[4,32,64,512]{3,2,1,0:T(8,128)(2,1)} %field.5, bf16[32,32]{1,0:T(8,128)(2,1)} %bitcast.9, f32[512,1]{1,0:T(8,128)} %broadcast_in_dim_reshape.4.bias, bf16[512,32]{1,0:T(8,128)(2,1)} %constant.31.clone.pick, bf16[512,512]{1,0:T(8,128)(2,1)} %constant.32.clone.same), custom_call_target="tpu_custom_call" | custom-call | flops 4000000000 | bytes 17825792 | tf_op jit(solution)/shard_map/pallas_call | solution.py:479
  62.4 13.6 %all-to-all-done.1 = f32[32,2,32,128]{3,2,1,0:T(8,128)S(1)} async-done(((f32[32,2,32,128]{3,2,1,0:T(8,128)}), f32[32,2,32,128]{3,2,1,0:T(8,128)S(1)}, u32[]{:S(2)}, u32[]{:S(2)}) %all-to-all-start.1) | async-done | bytes 1048608 | tf_op jit(solution)/shard_map/all_to_all | solution.py:765
  75.9 19.0 %shard_map.195 = (bf16[4,32,64,512]{3,2,1,0:T(8,128)(2,1)}, bf16[4,32,64,512]{3,2,1,0:T(8,128)(2,1)}, f32[2048,128]{1,0:T(8,128)}, f32[256,128]{1,0:T(8,128)S(1)}) custom-call(f32[2048,128]{1,0:T(8,128)S(1)} %bitcast.7, bf16[4,32,64,512]{3,2,1,0:T(8,128)(2,1)} %shard_map.193.early, bf16[4,32,64,512]{3,2,1,0:T(8,128)(2,1)} %cotangent.1, ...), custom_call_target="tpu_custom_call" | custom-call | flops 5000000000 | bytes 35651584 | tf_op jit(solution)/shard_map/pallas_call | solution.py:653
  95.6 3.8 %all-to-all-start.2 = ((f32[32,2,32,128]{3,2,1,0:T(8,128)}), f32[32,2,32,128]{3,2,1,0:T(8,128)S(1)}, u32[]{:S(2)}, u32[]{:S(2)}) async-start(f32[32,2,32,128]{3,2,1,0:T(8,128)} %bitcast.3), calls=%async_computation.2 | async-start | bytes 2097152 | tf_op jit(solution)/shard_map/all_to_all | solution.py:765
  99.4 11.3 %shard_map.197 = f32[40,128]{1,0:T(8,128)} custom-call(bf16[4,32,64,512]{3,2,1,0:T(8,128)(2,1)} %field.5, bf16[4,32,64,512]{3,2,1,0:T(8,128)(2,1)} %get-tuple-element.34.slope, f32[256,128]{1,0:T(8,128)} %copy-done, bf16[512,32]{1,0:T(8,128)(2,1)} %constant.31.clone.pick, bf16[512,512]{1,0:T(8,128)(2,1)} %constant.32.clone.same), custom_call_target="tpu_custom_call" | custom-call | flops 4000000000 | bytes 17825792 | tf_op jit(solution)/shard_map/pallas_call | solution.py:561
  110.8 1.7 collective-permute-start.1
  112.6 2.2 %collective-permute-done.1 = f32[40,128]{1,0:T(8,128)S(1)} collective-permute-done((f32[40,128]{1,0:T(8,128)}, f32[40,128]{1,0:T(8,128)S(1)}, u32[]{:S(2)}, u32[]{:S(2)}) %collective-permute-start.1) | collective-permute-done | bytes 20512 | tf_op jit(solution)/shard_map/ppermute | solution.py:771
  114.8 1.1 collective-permute-done.2
  116.6 1.5 collective-permute-start.3
  118.1 1.5 collective-permute-start.4
  120.7 1.5 collective-permute-done.4
  122.2 2.4 %collective-permute-done.5 = f32[40,128]{1,0:T(8,128)S(1)} collective-permute-done((f32[40,128]{1,0:T(8,128)S(1)}, f32[40,128]{1,0:T(8,128)S(1)}, u32[]{:S(2)}, u32[]{:S(2)}) %collective-permute-start.5) | collective-permute-done | bytes 20512 | tf_op jit(solution)/shard_map/ppermute | solution.py:771
  125.5 1.6 copy-done.3
  127.0 4.3 %shard_map.196 = (f32[32,2,32,128]{3,2,1,0:T(8,128)}, f32[32,32,128]{2,1,0:T(8,128)S(1)}) custom-call(f32[32,2,32,128]{3,2,1,0:T(8,128)S(1)} %all-to-all-done.2.received, bf16[32,2,32,512]{3,2,1,0:T(8,128)(2,1)S(1)} %copy-done.3, bf16[32,192]{1,0:T(8,128)(2,1)S(1)} %copy-done.4, bf16[64,96]{1,0:T(8,128)(2,1)S(1)} %copy-done.5, f32[16,128]{1,0:T(8,128)S(1)} %copy-done.6, ...), custom_call_target="tpu_custom_call" | custom-call | flops 1000000000 | bytes 5242880 | tf_op jit(solution)/shard_map/pallas_call | solution.py:382
  131.3 3.6 %all-to-all-start.3 = ((f32[32,2,32,128]{3,2,1,0:T(8,128)}), f32[32,2,32,128]{3,2,1,0:T(8,128)S(1)}, u32[]{:S(2)}, u32[]{:S(2)}) async-start(f32[32,2,32,128]{3,2,1,0:T(8,128)} %get-tuple-element.33), calls=%async_computation.3 | async-start | bytes 2097152 | tf_op jit(solution)/shard_map/all_to_all | solution.py:765
  134.9 2.7 %collective-permute-start.6 = (f32[40,128]{1,0:T(8,128)S(1)}, f32[40,128]{1,0:T(8,128)S(1)}, u32[]{:S(2)}, u32[]{:S(2)}) collective-permute-start(f32[40,128]{1,0:T(8,128)S(1)} %add_add_fusion), channel_id=1, source_target_pairs={{0,16},{1,17},{2,18},{3,19},{4,20},{5,21},{6,22},{7,23},{8,24},{9,... | collective-permute-start | bytes 61448 | tf_op jit(solution)/shard_map/ppermute | solution.py:771
  137.7 9.9 %shard_map.198.early = bf16[4,32,64,512]{3,2,1,0:T(8,128)(2,1)} custom-call(bf16[4,32,64,512]{3,2,1,0:T(8,128)(2,1)} %get-tuple-element.34.slope, bf16[32,32]{1,0:T(8,128)(2,1)} %weight.5, bf16[512,32]{1,0:T(8,128)(2,1)} %constant.31.clone.pick, bf16[512,512]{1,0:T(8,128)(2,1)} %constant.32.clone.same), custom_call_target="tpu_custom_call" | custom-call | flops 4000000000 | bytes 17825792 | tf_op jit(solution)/shard_map/pallas_call | solution.py:507
  147.5 2.6 %shard_map.200 = f32[32,2,32,512]{3,2,1,0:T(8,128)} custom-call(f32[32,32,128]{2,1,0:T(8,128)S(1)} %get-tuple-element.37.modes, f32[32,32,128]{2,1,0:T(8,128)S(1)} %get-tuple-element.38.dmodes, f32[16,512]{1,0:T(8,128)S(1)} %copy-done.1), custom_call_target="tpu_custom_call" | custom-call | flops 100000000 | bytes 5242880 | tf_op jit(solution)/shard_map/pallas_call | solution.py:414
  150.2 11.9 %collective-permute-done.6 = f32[40,128]{1,0:T(8,128)S(1)} collective-permute-done((f32[40,128]{1,0:T(8,128)S(1)}, f32[40,128]{1,0:T(8,128)S(1)}, u32[]{:S(2)}, u32[]{:S(2)}) %collective-permute-start.6) | collective-permute-done | bytes 20512 | tf_op jit(solution)/shard_map/ppermute | solution.py:771
  162.1 7.6 %shard_map.199 = (bf16[4,32,64,512]{3,2,1,0:T(8,128)(2,1)}, f32[32,32]{1,0:T(8,128)}, f32[1,32]{1,0:T(1,128)}) custom-call(f32[2048,128]{1,0:T(8,128)S(1)} %bitcast.6, bf16[4,32,64,512]{3,2,1,0:T(8,128)(2,1)} %shard_map.198.early, bf16[256,512]{1,0:T(8,128)(2,1)S(1)} %get-tuple-element.25.zt_turned, bf16[128,48]{1,0:T(8,128)(2,1)S(1)} %get-tuple-element.26.y_back, ...), custom_call_target="tpu_custom_call" | custom-call | flops 2000000000 | bytes 17825792 | tf_op jit(solution)/shard_map/pallas_call | solution.py:729
  (33 shorter events, 6.3 us)
Async XLA Ops:
  0.6 41.7 %copy-start.1 = (f32[16,512]{1,0:T(8,128)S(1)}, f32[16,512]{1,0:T(8,128)}, u32[]{:S(2)}) copy-start(f32[16,512]{1,0:T(8,128)} %constant.26.clone.mask) | copy-start | bytes 98308
  0.6 41.7 %copy-start.4 = (bf16[32,192]{1,0:T(8,128)(2,1)S(1)}, bf16[32,192]{1,0:T(8,128)(2,1)}, u32[]{:S(2)}) copy-start(bf16[32,192]{1,0:T(8,128)(2,1)} %constant.27.clone.forward) | copy-start | bytes 36868
  0.7 41.7 %copy-start.5 = (bf16[64,96]{1,0:T(8,128)(2,1)S(1)}, bf16[64,96]{1,0:T(8,128)(2,1)}, u32[]{:S(2)}) copy-start(bf16[64,96]{1,0:T(8,128)(2,1)} %constant.28.clone.inverse) | copy-start | bytes 36868
  0.7 41.7 %copy-start.6 = (f32[16,128]{1,0:T(8,128)S(1)}, f32[16,128]{1,0:T(8,128)}, u32[]{:S(2)}) copy-start(f32[16,128]{1,0:T(8,128)} %constant.29.clone.cosine) | copy-start | bytes 24580
  0.7 41.7 %copy-start.7 = (f32[16,128]{1,0:T(8,128)S(1)}, f32[16,128]{1,0:T(8,128)}, u32[]{:S(2)}) copy-start(f32[16,128]{1,0:T(8,128)} %constant.30.clone.sine) | copy-start | bytes 24580
  0.7 41.7 %copy-start.2 = (bf16[32,2,32,512]{3,2,1,0:T(8,128)(2,1)S(1)}, bf16[32,2,32,512]{3,2,1,0:T(8,128)(2,1)}, u32[]{:S(2)}) copy-start(bf16[32,2,32,512]{3,2,1,0:T(8,128)(2,1)} %weight.4) | copy-start | bytes 6291460
  0.7 49.0 %copy-start.9 = (f32[32]{0:T(128)S(1)}, f32[32]{0:T(128)}, u32[]{:S(2)}) copy-start(f32[32]{0:T(128)} %param.20) | copy-start | bytes 388
  0.7 49.9 %copy-start.8 = (bf16[32,32]{1,0:T(8,128)(2,1)S(1)}, bf16[32,32]{1,0:T(8,128)(2,1)}, u32[]{:S(2)}) copy-start(bf16[32,32]{1,0:T(8,128)(2,1)} %weight.5) | copy-start | bytes 6148
  46.1 29.9 %all-to-all-start.1 = ((f32[32,2,32,128]{3,2,1,0:T(8,128)}), f32[32,2,32,128]{3,2,1,0:T(8,128)S(1)}, u32[]{:S(2)}, u32[]{:S(2)}) async-start(f32[32,2,32,128]{3,2,1,0:T(8,128)} %get-tuple-element.23), calls=%async_computation.1 | async-start | bytes 2097152 | tf_op jit(solution)/shard_map/all_to_all | solution.py:765
  94.9 0.7 copy-start
  95.6 29.9 %all-to-all-start.2 = ((f32[32,2,32,128]{3,2,1,0:T(8,128)}), f32[32,2,32,128]{3,2,1,0:T(8,128)S(1)}, u32[]{:S(2)}, u32[]{:S(2)}) async-start(f32[32,2,32,128]{3,2,1,0:T(8,128)} %bitcast.3), calls=%async_computation.2 | async-start | bytes 2097152 | tf_op jit(solution)/shard_map/all_to_all | solution.py:765
  110.7 1.9 %collective-permute-start = (f32[40,128]{1,0:T(8,128)}, f32[40,128]{1,0:T(8,128)S(1)}, u32[]{:S(2)}, u32[]{:S(2)}) collective-permute-start(f32[40,128]{1,0:T(8,128)} %shard_map.197), channel_id=1, source_target_pairs={{0,1},{1,0},{2,3},{3,2},{4,5},{5,4},{6,7},{7,6},{8,9},{9,8},{10,11... | collective-permute-start | bytes 61448 | tf_op jit(solution)/shard_map/ppermute | solution.py:771
  110.8 4.0 %collective-permute-start.1 = (f32[40,128]{1,0:T(8,128)}, f32[40,128]{1,0:T(8,128)S(1)}, u32[]{:S(2)}, u32[]{:S(2)}) collective-permute-start(f32[40,128]{1,0:T(8,128)} %shard_map.197), channel_id=1, source_target_pairs={{0,2},{1,3},{2,0},{3,1},{4,6},{5,7},{6,4},{7,5},{8,10},{9,11},{10,... | collective-permute-start | bytes 61448 | tf_op jit(solution)/shard_map/ppermute | solution.py:771
  112.5 3.4 %collective-permute-start.2 = (f32[40,128]{1,0:T(8,128)}, f32[40,128]{1,0:T(8,128)S(1)}, u32[]{:S(2)}, u32[]{:S(2)}) collective-permute-start(f32[40,128]{1,0:T(8,128)} %shard_map.197), channel_id=1, source_target_pairs={{0,3},{1,2},{2,1},{3,0},{4,7},{5,6},{6,5},{7,4},{8,11},{9,10},{10,... | collective-permute-start | bytes 61448 | tf_op jit(solution)/shard_map/ppermute | solution.py:771
  116.6 4.0 %collective-permute-start.3 = (f32[40,128]{1,0:T(8,128)S(1)}, f32[40,128]{1,0:T(8,128)S(1)}, u32[]{:S(2)}, u32[]{:S(2)}) collective-permute-start(f32[40,128]{1,0:T(8,128)S(1)} %add_add_fusion.1), channel_id=1, source_target_pairs={{0,4},{1,5},{2,6},{3,7},{4,0},{5,1},{6,2},{7,3},{8,12},{9,13},{10,... | collective-permute-start | bytes 61448 | tf_op jit(solution)/shard_map/ppermute | solution.py:771
  118.1 4.1 %collective-permute-start.4 = (f32[40,128]{1,0:T(8,128)S(1)}, f32[40,128]{1,0:T(8,128)S(1)}, u32[]{:S(2)}, u32[]{:S(2)}) collective-permute-start(f32[40,128]{1,0:T(8,128)S(1)} %add_add_fusion.1), channel_id=1, source_target_pairs={{0,8},{1,9},{2,10},{3,11},{4,12},{5,13},{6,14},{7,15},{8,0},{9,1},... | collective-permute-start | bytes 61448 | tf_op jit(solution)/shard_map/ppermute | solution.py:771
  119.6 5.0 %collective-permute-start.5 = (f32[40,128]{1,0:T(8,128)S(1)}, f32[40,128]{1,0:T(8,128)S(1)}, u32[]{:S(2)}, u32[]{:S(2)}) collective-permute-start(f32[40,128]{1,0:T(8,128)S(1)} %add_add_fusion.1), channel_id=1, source_target_pairs={{0,12},{1,13},{2,14},{3,15},{4,8},{5,9},{6,10},{7,11},{8,4},{9,5},... | collective-permute-start | bytes 61448 | tf_op jit(solution)/shard_map/ppermute | solution.py:771
  125.5 1.6 copy-start.3
  131.3 30.7 %all-to-all-start.3 = ((f32[32,2,32,128]{3,2,1,0:T(8,128)}), f32[32,2,32,128]{3,2,1,0:T(8,128)S(1)}, u32[]{:S(2)}, u32[]{:S(2)}) async-start(f32[32,2,32,128]{3,2,1,0:T(8,128)} %get-tuple-element.33), calls=%async_computation.3 | async-start | bytes 2097152 | tf_op jit(solution)/shard_map/all_to_all | solution.py:765
  134.9 27.1 %collective-permute-start.6 = (f32[40,128]{1,0:T(8,128)S(1)}, f32[40,128]{1,0:T(8,128)S(1)}, u32[]{:S(2)}, u32[]{:S(2)}) collective-permute-start(f32[40,128]{1,0:T(8,128)S(1)} %add_add_fusion), channel_id=1, source_target_pairs={{0,16},{1,17},{2,18},{3,19},{4,20},{5,21},{6,22},{7,23},{8,24},{9,... | collective-permute-start | bytes 61448 | tf_op jit(solution)/shard_map/ppermute | solution.py:771
